TPU v7x, 32 devices: a whole 2x2x4 slice. The times are simulated.
32 devices in a mesh: seq: 2 (over x), fsdp: 16 (over z, y, core).
Axes of the slice: x: 2, y: 2, z: 4, core: 2. Of those that a mesh axis runs over, the one named last changes fastest.
Arguments:
- tokens: bfloat16 [16, 384, 2048], P('fsdp', 'seq'), may hold values from -6 to 6
- cotangent: bfloat16 [16, 384, 2048], P('fsdp', 'seq'), may hold values from -6 to 6
- mixer_gain: bfloat16 [2048], P('fsdp'), may hold values from 0.099609375 to 1.8984375
- query_weight: bfloat16 [2048, 1024], P('fsdp'), may hold values from -0.125 to 0.125
- key_weight: bfloat16 [2048, 256], P('fsdp'), may hold values from -0.125 to 0.125
- value_weight: bfloat16 [2048, 256], P('fsdp'), may hold values from -0.125 to 0.125
- attn_out_weight: bfloat16 [1024, 2048], P('fsdp'), may hold values from -0.75 to 0.75
- mamba_in_weight: bfloat16 [2048, 6704], P('fsdp'), may hold values from -0.125 to 0.125
- conv_weight: bfloat16 [4, 3584], P(None, 'fsdp'), may hold values from -3 to 3
- conv_bias: bfloat16 [3584], P('fsdp'), may hold values from -3 to 3
- decay_log: bfloat16 [48], replicated, may hold values from -4.59375 to -0.69921875
- step_bias: bfloat16 [48], replicated, may hold values from -4 to -1
- skip_gain: bfloat16 [48], replicated, may hold values from 0.5 to 1.5
- mamba_gain: bfloat16 [3072], P('fsdp'), may hold values from 0.099609375 to 1.8984375
- mamba_out_weight: bfloat16 [3072, 2048], P('fsdp'), may hold values from -0.109375 to 0.109375
- ffn_gain: bfloat16 [2048], P('fsdp'), may hold values from 0.099609375 to 1.8984375
- gate_weight: bfloat16 [2048, 4096], P('fsdp'), may hold values from -0.125 to 0.125
- up_weight: bfloat16 [2048, 4096], P('fsdp'), may hold values from -0.125 to 0.125
- down_weight: bfloat16 [4096, 2048], P('fsdp'), may hold values from -0.09375 to 0.09375
Outputs:
- output: bfloat16 [16, 384, 2048], P('fsdp', 'seq')
- tokens_grad: float32 [16, 384, 2048], P('fsdp', 'seq')
- mixer_gain_grad: float32 [2048], P('fsdp')
- query_grad: float32 [2048, 1024], P('fsdp')
- key_grad: float32 [2048, 256], P('fsdp')
- value_grad: float32 [2048, 256], P('fsdp')
- attn_out_grad: float32 [1024, 2048], P('fsdp')
- mamba_in_grad: float32 [2048, 6704], P('fsdp')
- conv_weight_grad: float32 [4, 3584], P(None, 'fsdp')
- conv_bias_grad: float32 [3584], P('fsdp')
- decay_log_grad: float32 [48], replicated
- step_bias_grad: float32 [48], replicated
- skip_gain_grad: float32 [48], replicated
- mamba_gain_grad: float32 [3072], P('fsdp')
- mamba_out_grad: float32 [3072, 2048], P('fsdp')
- ffn_gain_grad: float32 [2048], P('fsdp')
- gate_grad: float32 [2048, 4096], P('fsdp')
- up_grad: float32 [2048, 4096], P('fsdp')
- down_grad: float32 [4096, 2048], P('fsdp')
All inputs are finite; a program needn't handle non-finite values.
Results may differ from a plain program's by a relative error of at most 0.018.
Values may be sent and summed in bfloat16 or wider, within the bound.
A program may use at most 448 MiB of HBM per device.

v0:
```python
import math

import jax
import jax.numpy as jnp
from jax import lax
from jax.sharding import PartitionSpec as P

HQ = 8
KVH = 2
HD = 128
MH = 48
MP = 64
NST = 256
SPAN = 128


EPSILON = 1e-05
ROPE_BASE = 100000000000.0
MASKED = -1e30
PRECISE = lax.Precision.HIGHEST


def rms_norm(values, scaling):
    factor = lax.rsqrt(jnp.mean(values * values, axis=-1, keepdims=True) + EPSILON)
    return values * factor * scaling


def norm_back(values, scaling, incoming):
    factor = lax.rsqrt(jnp.mean(values * values, axis=-1, keepdims=True) + EPSILON)
    normal = values * factor
    scaled = incoming * scaling
    grad_values = factor * (scaled - normal * jnp.mean(scaled * normal, axis=-1, keepdims=True))
    return (grad_values, jnp.sum(incoming * normal, axis=0))


def outer_product(left, right):
    return lax.dot_general(
        left, right, (((0,), (0,)), ((), ())), preferred_element_type=jnp.float32
    )


def across(left, weight):
    return lax.dot_general(
        left, weight, (((1,), (1,)), ((), ())), preferred_element_type=jnp.float32
    )


def causal_conv(signal, kernel):
    length = signal.shape[0]
    tap_count = kernel.shape[0]
    padded = jnp.pad(signal, ((tap_count - 1, 0), (0, 0)))
    summed = padded[0:length] * kernel[0]
    for offset in range(1, tap_count):
        summed = summed + padded[offset : offset + length] * kernel[offset]
    return summed


def rope_tables(length, head_size):
    half_size = head_size // 2
    frequency = jnp.exp(
        jnp.arange(half_size, dtype=jnp.float32) * (-2.0 * math.log(ROPE_BASE) / head_size)
    )
    angles = jnp.arange(length, dtype=jnp.float32)[:, None] * frequency[None, :]
    return (jnp.cos(angles)[:, None, :], jnp.sin(angles)[:, None, :])


def rotate(values, cosine, sine_table):
    half_size = values.shape[-1] // 2
    front_half = values[..., :half_size]
    back_half = values[..., half_size:]
    return jnp.concatenate(
        [
            front_half * cosine - back_half * sine_table,
            back_half * cosine + front_half * sine_table,
        ],
        axis=-1,
    )


def scan_states(inputs, step_sizes, decay_rates, input_map, output_map):
    length, head_count, head_width = inputs.shape
    state_size = input_map.shape[1]
    number = length // SPAN
    blocks = (
        inputs.reshape(number, SPAN, head_count, head_width),
        step_sizes.reshape(number, SPAN, head_count),
        input_map.reshape(number, SPAN, state_size),
        output_map.reshape(number, SPAN, state_size),
    )
    causal = jnp.arange(SPAN)[:, None] >= jnp.arange(SPAN)[None, :]

    def advance(state_now, pieces):
        block_x, block_dt, block_b, block_c = pieces
        cumulated = jnp.cumsum(block_dt * decay_rates, axis=0)
        log_gaps = jnp.where(
            causal[:, :, None], cumulated[:, None, :] - cumulated[None, :, :], MASKED
        )
        coupling = jnp.dot(block_c, block_b.T, precision=PRECISE)
        weights = coupling[:, :, None] * jnp.exp(log_gaps) * block_dt[None, :, :]
        within = jnp.einsum("tsh,shp->thp", weights, block_x, precision=PRECISE)
        carried = (
            jnp.einsum("tn,hpn->thp", block_c, state_now, precision=PRECISE)
            * jnp.exp(cumulated)[:, :, None]
        )
        ending = cumulated[-1]
        fading = jnp.exp(ending[None, :] - cumulated) * block_dt
        state_now = state_now * jnp.exp(ending)[:, None, None] + jnp.einsum(
            "sh,shp,sn->hpn", fading, block_x, block_b, precision=PRECISE
        )
        return (state_now, within + carried)

    initial = jnp.zeros((head_count, head_width, state_size), jnp.float32)
    ignored, outputs = lax.scan(jax.checkpoint(advance), initial, blocks)
    return outputs.reshape(length, head_count, head_width)


def mamba_core(
    seq_inputs,
    step_raw,
    map_inputs,
    x_kernel,
    x_bias,
    map_kernel,
    map_bias,
    decay_log,
    step_bias,
    skip_gain,
):
    length = seq_inputs.shape[0]
    head_count = step_raw.shape[1]
    head_width = seq_inputs.shape[1] // head_count
    state_size = map_inputs.shape[1] // 2
    convolved = jax.nn.silu(causal_conv(seq_inputs, x_kernel) + x_bias).reshape(
        length, head_count, head_width
    )
    map_values = jax.nn.silu(causal_conv(map_inputs, map_kernel) + map_bias)
    step_sizes = jax.nn.softplus(step_raw + step_bias)
    decay_rates = -jnp.exp(decay_log)
    outputs = scan_states(
        convolved, step_sizes, decay_rates, map_values[:, :state_size], map_values[:, state_size:]
    )
    outputs = outputs + skip_gain[:, None] * convolved
    return outputs.reshape(length, head_count * head_width)


def score_rows(rotated_query, rotated_keys):
    length, query_heads, head_size = rotated_query.shape
    key_heads = rotated_keys.shape[1]
    grouped = rotated_query.reshape(length, key_heads, query_heads // key_heads, head_size)
    causal = jnp.arange(length)[:, None] >= jnp.arange(length)[None, :]
    scores = jnp.einsum(
        "qcgd,kcd->cgqk", grouped, rotated_keys, preferred_element_type=jnp.float32
    ) * head_size ** (-0.5)
    return (grouped, jnp.where(causal, scores, MASKED))


def attend(rotated_query, rotated_keys, value_heads):
    length, query_heads, head_size = rotated_query.shape
    grouped, scores = score_rows(rotated_query, rotated_keys)
    highest = jnp.max(scores, axis=-1, keepdims=True)
    weights = jnp.exp(scores - highest)
    row_total = jnp.sum(weights, axis=-1, keepdims=True)
    normalized = (weights / row_total).astype(jnp.bfloat16)
    attended = jnp.einsum(
        "cgqk,kcd->qcgd", normalized, value_heads, preferred_element_type=jnp.float32
    )
    return (attended.reshape(length, query_heads * head_size), highest + jnp.log(row_total))


def attend_back(rotated_query, rotated_keys, value_heads, log_total, incoming):
    length, query_heads, head_size = rotated_query.shape
    key_heads = rotated_keys.shape[1]
    grouped, scores = score_rows(rotated_query, rotated_keys)
    softmax_w = jnp.exp(scores - log_total)
    rounded_w = softmax_w.astype(jnp.bfloat16)
    grad_heads = incoming.reshape(length, key_heads, query_heads // key_heads, head_size)
    grad_value = jnp.einsum(
        "cgqk,qcgd->kcd", rounded_w, grad_heads, preferred_element_type=jnp.float32
    )
    grad_prob = jnp.einsum(
        "qcgd,kcd->cgqk", grad_heads, value_heads, preferred_element_type=jnp.float32
    )
    grad_scores = softmax_w * (grad_prob - jnp.sum(softmax_w * grad_prob, axis=-1, keepdims=True))
    grad_scores = grad_scores.astype(jnp.bfloat16)
    scaling = head_size ** (-0.5)
    grad_grouped = (
        jnp.einsum("cgqk,kcd->qcgd", grad_scores, rotated_keys, preferred_element_type=jnp.float32)
        * scaling
    )
    grad_keys = (
        jnp.einsum("cgqk,qcgd->kcd", grad_scores, grouped, preferred_element_type=jnp.float32)
        * scaling
    )
    return (grad_grouped.reshape(length, query_heads, head_size), grad_keys, grad_value)


def shards(
    tokens,
    cotangent,
    mixer_gain,
    query_weight,
    key_weight,
    value_weight,
    attn_out_weight,
    mamba_in_weight,
    conv_weight,
    conv_bias,
    decay_log,
    step_bias,
    skip_gain,
    mamba_gain,
    mamba_out_weight,
    ffn_gain,
    gate_weight,
    up_weight,
    down_weight,
):
    token_count = tokens.shape[1]
    model_dim = tokens.shape[2]
    groups = lax.axis_size("seq")
    seq_rank = lax.axis_index("seq")
    inner_width = MH * MP
    state_size = NST
    query_local = HQ // groups
    key_heads = KVH // groups
    mamba_local = MH // groups
    mamba_cols = mamba_local * MP
    (
        gain_in,
        w_query,
        w_key,
        w_value,
        w_attn_out,
        w_mamba_in,
        w_conv,
        b_conv,
        gain_mamba,
        w_mamba_out,
    ) = (
        lax.all_gather(mixer_gain, "fsdp", axis=0, tiled=True),
        lax.all_gather(query_weight, "fsdp", axis=0, tiled=True),
        lax.all_gather(key_weight, "fsdp", axis=0, tiled=True),
        lax.all_gather(value_weight, "fsdp", axis=0, tiled=True),
        lax.all_gather(attn_out_weight, "fsdp", axis=0, tiled=True),
        lax.all_gather(mamba_in_weight, "fsdp", axis=0, tiled=True),
        lax.all_gather(conv_weight, "fsdp", axis=1, tiled=True),
        lax.all_gather(conv_bias, "fsdp", axis=0, tiled=True),
        lax.all_gather(mamba_gain, "fsdp", axis=0, tiled=True),
        lax.all_gather(mamba_out_weight, "fsdp", axis=0, tiled=True),
    )
    gain_ffn, w_gate, w_up, w_down = (
        lax.all_gather(ffn_gain, "fsdp", axis=0, tiled=True),
        lax.all_gather(gate_weight, "fsdp", axis=0, tiled=True),
        lax.all_gather(up_weight, "fsdp", axis=0, tiled=True),
        lax.all_gather(down_weight, "fsdp", axis=0, tiled=True),
    )
    token_rows = tokens.reshape(token_count, model_dim).astype(jnp.float32)
    hidden = rms_norm(token_rows, gain_in.astype(jnp.float32)).astype(jnp.bfloat16)
    query_proj = jnp.dot(hidden, w_query, preferred_element_type=jnp.float32).astype(jnp.bfloat16)
    key_proj = jnp.dot(hidden, w_key, preferred_element_type=jnp.float32).astype(jnp.bfloat16)
    value_proj = jnp.dot(hidden, w_value, preferred_element_type=jnp.float32).astype(jnp.bfloat16)
    projected = jnp.dot(hidden, w_mamba_in, preferred_element_type=jnp.float32)
    gate_branch = projected[:, :inner_width]
    seq_inputs = projected[:, inner_width : 2 * inner_width].astype(jnp.bfloat16)
    map_inputs = projected[:, 2 * inner_width : 2 * inner_width + 2 * state_size].astype(
        jnp.bfloat16
    )
    step_raw = projected[:, 2 * inner_width + 2 * state_size :].astype(jnp.bfloat16)
    heads_query, heads_key, heads_value, heads_input, heads_step = (
        lax.all_to_all(query_proj, "seq", split_axis=1, concat_axis=0, tiled=True),
        lax.all_to_all(key_proj, "seq", split_axis=1, concat_axis=0, tiled=True),
        lax.all_to_all(value_proj, "seq", split_axis=1, concat_axis=0, tiled=True),
        lax.all_to_all(seq_inputs, "seq", split_axis=1, concat_axis=0, tiled=True),
        lax.all_to_all(step_raw, "seq", split_axis=1, concat_axis=0, tiled=True),
    )
    whole_maps = lax.all_gather(map_inputs, "seq", axis=0, tiled=True)
    length = heads_query.shape[0]
    cosine, sine_table = rope_tables(length, HD)
    rotated_query = rotate(
        heads_query.reshape(length, query_local, HD).astype(jnp.float32), cosine, sine_table
    ).astype(jnp.bfloat16)
    rotated_keys = rotate(
        heads_key.reshape(length, key_heads, HD).astype(jnp.float32), cosine, sine_table
    ).astype(jnp.bfloat16)
    value_heads = heads_value.reshape(length, key_heads, HD)
    attended, log_total = attend(rotated_query, rotated_keys, value_heads)
    conv_full = w_conv.astype(jnp.float32)
    bias_full = b_conv.astype(jnp.float32)
    core_inputs = (
        heads_input.astype(jnp.float32),
        heads_step.astype(jnp.float32),
        whole_maps.astype(jnp.float32),
        lax.dynamic_slice_in_dim(conv_full, seq_rank * mamba_cols, mamba_cols, 1),
        lax.dynamic_slice_in_dim(bias_full, seq_rank * mamba_cols, mamba_cols, 0),
        conv_full[:, inner_width:],
        bias_full[inner_width:],
        lax.dynamic_slice_in_dim(
            decay_log.astype(jnp.float32), seq_rank * mamba_local, mamba_local, 0
        ),
        lax.dynamic_slice_in_dim(
            step_bias.astype(jnp.float32), seq_rank * mamba_local, mamba_local, 0
        ),
        lax.dynamic_slice_in_dim(
            skip_gain.astype(jnp.float32), seq_rank * mamba_local, mamba_local, 0
        ),
    )
    scanned, core_pull = jax.vjp(mamba_core, *core_inputs)
    back_attended, back_scanned = (
        lax.all_to_all(
            attended.astype(jnp.bfloat16), "seq", split_axis=0, concat_axis=1, tiled=True
        ),
        lax.all_to_all(
            scanned.astype(jnp.bfloat16), "seq", split_axis=0, concat_axis=1, tiled=True
        ),
    )
    scanned_rows = back_scanned.astype(jnp.float32)
    sigmoid_z = jax.nn.sigmoid(gate_branch)
    silu_z = gate_branch * sigmoid_z
    gated_values = scanned_rows * silu_z
    normed = rms_norm(gated_values, gain_mamba.astype(jnp.float32)).astype(jnp.bfloat16)
    mixer_sum = jnp.dot(back_attended, w_attn_out, preferred_element_type=jnp.float32) + jnp.dot(
        normed, w_mamba_out, preferred_element_type=jnp.float32
    )
    middle = token_rows + mixer_sum
    second = rms_norm(middle, gain_ffn.astype(jnp.float32)).astype(jnp.bfloat16)
    gate_act = jnp.dot(second, w_gate, preferred_element_type=jnp.float32)
    up_act = jnp.dot(second, w_up, preferred_element_type=jnp.float32)
    sigmoid_g = jax.nn.sigmoid(gate_act)
    active = (gate_act * sigmoid_g * up_act).astype(jnp.bfloat16)
    result = middle + jnp.dot(active, w_down, preferred_element_type=jnp.float32)
    output = result.astype(jnp.bfloat16).reshape(1, token_count, model_dim)
    gain_ffn, w_gate, w_up, w_down = (
        lax.all_gather(ffn_gain, "fsdp", axis=0, tiled=True),
        lax.all_gather(gate_weight, "fsdp", axis=0, tiled=True),
        lax.all_gather(up_weight, "fsdp", axis=0, tiled=True),
        lax.all_gather(down_weight, "fsdp", axis=0, tiled=True),
    )
    incoming = cotangent.reshape(token_count, model_dim)
    grad_down = outer_product(active, incoming)
    grad_active = across(incoming, w_down)
    grad_gate = (grad_active * up_act * sigmoid_g * (1.0 + gate_act * (1.0 - sigmoid_g))).astype(
        jnp.bfloat16
    )
    grad_up = (grad_active * gate_act * sigmoid_g).astype(jnp.bfloat16)
    grad_wgate = outer_product(second, grad_gate)
    grad_wup = outer_product(second, grad_up)
    grad_second = across(grad_gate, w_gate) + across(grad_up, w_up)
    grad_middle_norm, grad_gain_ffn = norm_back(middle, gain_ffn.astype(jnp.float32), grad_second)
    grad_middle = incoming.astype(jnp.float32) + grad_middle_norm
    ffn_shards = (
        lax.psum_scatter(grad_gain_ffn, "fsdp", scatter_dimension=0, tiled=True),
        lax.psum_scatter(grad_wgate, "fsdp", scatter_dimension=0, tiled=True),
        lax.psum_scatter(grad_wup, "fsdp", scatter_dimension=0, tiled=True),
        lax.psum_scatter(grad_down, "fsdp", scatter_dimension=0, tiled=True),
    )
    gain_in, w_query, w_key, w_value, w_attn_out, w_mamba_in, gain_mamba, w_mamba_out = (
        lax.all_gather(mixer_gain, "fsdp", axis=0, tiled=True),
        lax.all_gather(query_weight, "fsdp", axis=0, tiled=True),
        lax.all_gather(key_weight, "fsdp", axis=0, tiled=True),
        lax.all_gather(value_weight, "fsdp", axis=0, tiled=True),
        lax.all_gather(attn_out_weight, "fsdp", axis=0, tiled=True),
        lax.all_gather(mamba_in_weight, "fsdp", axis=0, tiled=True),
        lax.all_gather(mamba_gain, "fsdp", axis=0, tiled=True),
        lax.all_gather(mamba_out_weight, "fsdp", axis=0, tiled=True),
    )
    grad_mixer = grad_middle.astype(jnp.bfloat16)
    grad_attn_out = outer_product(back_attended, grad_mixer)
    grad_mamba_out = outer_product(normed, grad_mixer)
    grad_attended = across(grad_mixer, w_attn_out).astype(jnp.bfloat16)
    grad_normed = across(grad_mixer, w_mamba_out)
    grad_gated, grad_gain_mamba = norm_back(
        gated_values, gain_mamba.astype(jnp.float32), grad_normed
    )
    grad_scanned = (grad_gated * silu_z).astype(jnp.bfloat16)
    grad_gate_branch = (
        grad_gated * scanned_rows * sigmoid_z * (1.0 + gate_branch * (1.0 - sigmoid_z))
    )
    heads_grad_att, heads_grad_scan = (
        lax.all_to_all(grad_attended, "seq", split_axis=1, concat_axis=0, tiled=True),
        lax.all_to_all(grad_scanned, "seq", split_axis=1, concat_axis=0, tiled=True),
    )
    grad_rot_query, grad_rot_keys, grad_value_heads = attend_back(
        rotated_query, rotated_keys, value_heads, log_total, heads_grad_att
    )
    grad_query_heads = (
        rotate(grad_rot_query, cosine, -sine_table)
        .reshape(length, query_local * HD)
        .astype(jnp.bfloat16)
    )
    grad_key_heads = (
        rotate(grad_rot_keys, cosine, -sine_table)
        .reshape(length, key_heads * HD)
        .astype(jnp.bfloat16)
    )
    grad_value_rows = grad_value_heads.reshape(length, key_heads * HD).astype(jnp.bfloat16)
    (
        grad_input,
        grad_step,
        grad_maps,
        grad_xkernel,
        grad_xbias,
        grad_mkernel,
        grad_mbias,
        grad_decay,
        grad_sbias,
        grad_skip,
    ) = core_pull(heads_grad_scan.astype(jnp.float32))
    tok_grad_query, tok_grad_key, tok_grad_value, tok_grad_input, tok_grad_step = (
        lax.all_to_all(grad_query_heads, "seq", split_axis=0, concat_axis=1, tiled=True),
        lax.all_to_all(grad_key_heads, "seq", split_axis=0, concat_axis=1, tiled=True),
        lax.all_to_all(grad_value_rows, "seq", split_axis=0, concat_axis=1, tiled=True),
        lax.all_to_all(
            grad_input.astype(jnp.bfloat16), "seq", split_axis=0, concat_axis=1, tiled=True
        ),
        lax.all_to_all(
            grad_step.astype(jnp.bfloat16), "seq", split_axis=0, concat_axis=1, tiled=True
        ),
    )
    tok_grad_maps = lax.psum_scatter(
        grad_maps.astype(jnp.bfloat16), "seq", scatter_dimension=0, tiled=True
    )
    grad_projected = jnp.concatenate(
        [grad_gate_branch.astype(jnp.bfloat16), tok_grad_input, tok_grad_maps, tok_grad_step],
        axis=1,
    )
    grad_wquery = outer_product(hidden, tok_grad_query)
    grad_wkey = outer_product(hidden, tok_grad_key)
    grad_wvalue = outer_product(hidden, tok_grad_value)
    grad_wmamba_in = outer_product(hidden, grad_projected)
    grad_hidden = (
        across(tok_grad_query, w_query)
        + across(tok_grad_key, w_key)
        + across(tok_grad_value, w_value)
        + across(grad_projected, w_mamba_in)
    )
    grad_rows_norm, grad_gain_in = norm_back(token_rows, gain_in.astype(jnp.float32), grad_hidden)
    tokens_grad = (grad_middle + grad_rows_norm).reshape(1, token_count, model_dim)
    conv_channels = inner_width + 2 * state_size
    conv_grad = jnp.zeros((conv_weight.shape[0], conv_channels), jnp.float32)
    conv_grad = lax.dynamic_update_slice_in_dim(conv_grad, grad_xkernel, seq_rank * mamba_cols, 1)
    conv_grad = conv_grad.at[:, inner_width:].set(grad_mkernel)
    conv_bias_grad = jnp.zeros((conv_channels,), jnp.float32)
    conv_bias_grad = lax.dynamic_update_slice_in_dim(
        conv_bias_grad, grad_xbias, seq_rank * mamba_cols, 0
    )
    conv_bias_grad = conv_bias_grad.at[inner_width:].set(grad_mbias)
    head_params = jnp.zeros((3, MH), jnp.float32)
    head_params = lax.dynamic_update_slice_in_dim(
        head_params, jnp.stack([grad_decay, grad_sbias, grad_skip]), seq_rank * mamba_local, 1
    )
    head_total = lax.psum(head_params, ("seq", "fsdp"))
    mixer_shards = (
        lax.psum_scatter(grad_gain_in, "fsdp", scatter_dimension=0, tiled=True),
        lax.psum_scatter(grad_wquery, "fsdp", scatter_dimension=0, tiled=True),
        lax.psum_scatter(grad_wkey, "fsdp", scatter_dimension=0, tiled=True),
        lax.psum_scatter(grad_wvalue, "fsdp", scatter_dimension=0, tiled=True),
        lax.psum_scatter(grad_attn_out, "fsdp", scatter_dimension=0, tiled=True),
        lax.psum_scatter(grad_wmamba_in, "fsdp", scatter_dimension=0, tiled=True),
        lax.psum_scatter(conv_grad, "fsdp", scatter_dimension=1, tiled=True),
        lax.psum_scatter(conv_bias_grad, "fsdp", scatter_dimension=0, tiled=True),
        lax.psum_scatter(grad_gain_mamba, "fsdp", scatter_dimension=0, tiled=True),
        lax.psum_scatter(grad_mamba_out, "fsdp", scatter_dimension=0, tiled=True),
    )
    summed = (
        lax.psum(mixer_shards[0].astype(jnp.bfloat16), "seq").astype(jnp.float32),
        lax.psum(mixer_shards[1].astype(jnp.bfloat16), "seq").astype(jnp.float32),
        lax.psum(mixer_shards[2].astype(jnp.bfloat16), "seq").astype(jnp.float32),
        lax.psum(mixer_shards[3].astype(jnp.bfloat16), "seq").astype(jnp.float32),
        lax.psum(mixer_shards[4].astype(jnp.bfloat16), "seq").astype(jnp.float32),
        lax.psum(mixer_shards[5].astype(jnp.bfloat16), "seq").astype(jnp.float32),
        lax.psum(mixer_shards[6].astype(jnp.bfloat16), "seq").astype(jnp.float32),
        lax.psum(mixer_shards[7].astype(jnp.bfloat16), "seq").astype(jnp.float32),
        lax.psum(mixer_shards[8].astype(jnp.bfloat16), "seq").astype(jnp.float32),
        lax.psum(mixer_shards[9].astype(jnp.bfloat16), "seq").astype(jnp.float32),
        lax.psum(ffn_shards[0].astype(jnp.bfloat16), "seq").astype(jnp.float32),
        lax.psum(ffn_shards[1].astype(jnp.bfloat16), "seq").astype(jnp.float32),
        lax.psum(ffn_shards[2].astype(jnp.bfloat16), "seq").astype(jnp.float32),
        lax.psum(ffn_shards[3].astype(jnp.bfloat16), "seq").astype(jnp.float32),
    )
    return (
        output,
        tokens_grad,
        summed[0],
        summed[1],
        summed[2],
        summed[3],
        summed[4],
        summed[5],
        summed[6],
        summed[7],
        head_total[0],
        head_total[1],
        head_total[2],
        summed[8],
        summed[9],
        summed[10],
        summed[11],
        summed[12],
        summed[13],
    )


def solution(mesh):
    return jax.shard_map(
        shards,
        mesh=mesh,
        in_specs=(
            P("fsdp", "seq", None),
            P("fsdp", "seq", None),
            P("fsdp"),
            P("fsdp", None),
            P("fsdp", None),
            P("fsdp", None),
            P("fsdp", None),
            P("fsdp", None),
            P(None, "fsdp"),
            P("fsdp"),
            P(),
            P(),
            P(),
            P("fsdp"),
            P("fsdp", None),
            P("fsdp"),
            P("fsdp", None),
            P("fsdp", None),
            P("fsdp", None),
        ),
        out_specs=(
            P("fsdp", "seq", None),
            P("fsdp", "seq", None),
            P("fsdp"),
            P("fsdp", None),
            P("fsdp", None),
            P("fsdp", None),
            P("fsdp", None),
            P("fsdp", None),
            P(None, "fsdp"),
            P("fsdp"),
            P(),
            P(),
            P(),
            P("fsdp"),
            P("fsdp", None),
            P("fsdp"),
            P("fsdp", None),
            P("fsdp", None),
            P("fsdp", None),
        ),
        check_vma=False,
    )
```

profile of v0, /device:TPU:0, one launch (start us, length us, event | category | flops | bytes accessed | tf_op | source)
XLA Modules:
  0.0 3459.6 jit_solution(1774276215356756820)
XLA Ops:
  13.5 23.0 all-gather
  39.0 57.9 %all-reduce.28 = (bf16[3584]{0:T(1024)(128)(2,1)S(1)}, bf16[3072]{0:T(1024)(128)(2,1)}) all-reduce(bf16[3584]{0:T(1024)(128)(2,1)S(1)} %dynamic-update-slice.5, bf16[3072]{0:T(1024)(128)(2,1)S(1)} %dynamic-update-slice.6), channel_id=1, replica_groups=mesh['seq'=2,'fsdp'=16] {'fsdp'}, use_global_device_ids=true, to_apply=%add.21 | all-reduce | flops 6656 | bytes 26624
  98.2 17.3 all-gather.1
  170.9 118.7 %all-gather.21.cloned.1.call-done = bf16[2048,6704]{0,1:T(8,128)(2,1)} async-done(((bf16[128,6704]{0,1:T(8,128)(2,1)}), bf16[2048,6704]{0,1:T(8,128)(2,1)}) %all-gather.21.cloned.1.call-update) | async-done | bytes 27459600 | tf_op jit(solution)/shard_map/all_gather | solution.py:245
  289.6 16.6 fusion.229
  364.0 44.3 %while.43 = (s32[]{:T(128)}, f32[24,64,256]{2,1,0:T(8,128)S(1)}, f32[3,128,24,64]{1,3,2,0:T(8,128)}, f32[3,24,64,256]{3,2,1,0:T(8,128)}, f32[3,128,24]{2,1,0:T(8...) while((s32[]{:T(128)}, f32[24,64,256]{2,1,0:T(8,128)S(1)}, ...), condition=%wide.region_5.6_spmd.clone, body=%wide.region_3.5_spmd.clone.sunk | while | flops 1564809216 | bytes 12743473 | solution.py:113
  425.4 19.3 all-gather.2
  464.0 105.8 %all-gather.25.cloned.1.call-done = bf16[2048,4096]{1,0:T(8,128)(2,1)} async-done(((bf16[128,4096]{1,0:T(8,128)(2,1)}), bf16[2048,4096]{1,0:T(8,128)(2,1)}) %all-gather.25.cloned.1.call-update) | async-done | bytes 16777232 | tf_op jit(solution)/shard_map/all_gather | solution.py:253
  580.7 116.4 %all-gather.27.cloned.1.call-done = bf16[2048,4096]{1,0:T(8,128)(2,1)} async-done(((bf16[128,4096]{1,0:T(8,128)(2,1)}), bf16[2048,4096]{1,0:T(8,128)(2,1)}) %all-gather.27.cloned.1.call-update) | async-done | bytes 16777232 | tf_op jit(solution)/shard_map/all_gather | solution.py:254
  707.9 116.4 %all-gather.29.cloned.1.call-done = bf16[4096,2048]{1,0:T(8,128)(2,1)} async-done(((bf16[256,2048]{1,0:T(8,128)(2,1)}), bf16[4096,2048]{1,0:T(8,128)(2,1)}) %all-gather.29.cloned.1.call-update) | async-done | bytes 16777232 | tf_op jit(solution)/shard_map/all_gather | solution.py:255
  850.1 14.2 multiply_reduce_fusion.11
  916.4 152.8 %while.44 = (s32[]{:T(128)}, f32[24]{0:T(128)}, f32[24,64,256]{2,1,0:T(8,128)}, f32[3,128,24,64]{1,3,2,0:T(8,128)}, f32[3,128,24]{2,1,0:T(8,128)}, /*index=5*/f3...) while((s32[]{:T(128)}, f32[24]{0:T(128)}, ...), condition=%wide.region_22.23_spmd.clone, body=%wide.region_11.22_spmd.clone.sunk | while | flops 3786185728 | bytes 44187520 | solution.py:113
  1156.5 13.8 fusion.238
  1225.9 24.5 fusion.164
  1256.4 70.4 %reduce-scatter.22.cloned.1.call-done = f32[64,2048]{1,0:T(8,128)} async-done(((f32[1024,2048]{1,0:T(8,128)}), f32[64,2048]{1,0:T(8,128)}) %reduce-scatter.22.cloned.1.call-update) | async-done | bytes 524304 | tf_op jit(solution)/shard_map/reduce_scatter | solution.py:457
  1328.5 107.1 %reduce-scatter.16.cloned.1.call-done = f32[128,1024]{1,0:T(8,128)} async-done(((f32[2048,1024]{1,0:T(8,128)}), f32[128,1024]{1,0:T(8,128)}) %reduce-scatter.16.cloned.1.call-update) | async-done | bytes 524304 | tf_op jit(solution)/shard_map/reduce_scatter | solution.py:454
  1437.4 246.4 %reduce-scatter.26.cloned.1.call-done = f32[192,2048]{1,0:T(8,128)} async-done(((f32[3072,2048]{1,0:T(8,128)}), f32[192,2048]{1,0:T(8,128)}) %reduce-scatter.26.cloned.1.call-update) | async-done | bytes 1572880 | tf_op jit(solution)/shard_map/reduce_scatter | solution.py:462
  1686.3 334.0 %reduce-scatter.28.cloned.1.call-done = f32[128,4096]{1,0:T(8,128)} async-done(((f32[2048,4096]{1,0:T(8,128)}), f32[128,4096]{1,0:T(8,128)}) %reduce-scatter.28.cloned.1.call-update) | async-done | bytes 2097168 | tf_op jit(solution)/shard_map/reduce_scatter | solution.py:352
  2023.0 333.7 %reduce-scatter.30.cloned.1.call-done = f32[128,4096]{1,0:T(8,128)} async-done(((f32[2048,4096]{1,0:T(8,128)}), f32[128,4096]{1,0:T(8,128)}) %reduce-scatter.30.cloned.1.call-update) | async-done | bytes 2097168 | tf_op jit(solution)/shard_map/reduce_scatter | solution.py:353
  2359.4 333.8 %reduce-scatter.32.cloned.1.call-done = f32[256,2048]{1,0:T(8,128)} async-done(((f32[4096,2048]{1,0:T(8,128)}), f32[256,2048]{1,0:T(8,128)}) %reduce-scatter.32.cloned.1.call-update) | async-done | bytes 2097168 | tf_op jit(solution)/shard_map/reduce_scatter | solution.py:354
  2695.8 519.1 %reduce-scatter.24.cloned.1.call-done = f32[128,6704]{0,1:T(8,128)} async-done(((f32[2048,6704]{0,1:T(8,128)}), f32[128,6704]{0,1:T(8,128)}) %reduce-scatter.24.cloned.1.call-update) | async-done | bytes 3432464 | tf_op jit(solution)/shard_map/reduce_scatter | solution.py:458
  3245.6 39.8 %psum.113 = f32[3,48]{1,0:T(4,128)S(1)} all-reduce(f32[3,48]{1,0:T(4,128)} %dynamic_update_slice.61), channel_id=1, replica_groups=mesh['seq'=2,'fsdp'=16] {'seq','fsdp'}, use_global_device_ids=true, to_apply=%region_55.56 | all-reduce | flops 144 | bytes 1152 | tf_op jit(solution)/shard_map/psum | solution.py:451
  3303.5 59.3 %all-reduce.27 = (bf16[2048]{0:T(1024)(128)(2,1)S(1)}, bf16[3584]{0:T(1024)(128)(2,1)S(1)}, bf16[3072]{0:T(1024)(128)(2,1)S(1)}, bf16[2048]{0:T(1024)(128)(2,1)S(1)}) all-reduce(f32[2048]{0:T(1024)S(1)} %get-tuple-element.667, f32[3584]{0:T(1024)S(1)} %copy-done.96, ...), channel_id=3, replica_groups=mesh['seq'=2,'fsdp'=16] {'fsdp'}, use_global_device_ids=true, to_apply=%region_26.27.clone | all-reduce | flops 10752 | bytes 64512
  3375.0 65.1 %all-reduce.33.cloned.1.call-done = (bf16[128,1024]{1,0:T(8,128)(2,1)}, bf16[128,256]{1,0:T(8,128)(2,1)}, bf16[128,256]{1,0:T(8,128)(2,1)}, bf16[64,2048]{1,0:T(...) async-done(((bf16[128,1024]{1,0:T(8,128)(2,1)}, ...) | async-done | bytes 6303760 | tf_op jit(solution)/shard_map/psum | solution.py:466
  (751 shorter events, 686.3 us)
Async XLA Ops:
  7.2 114.8 %all-gather.15.cloned.1.call-start = ((), (), s32[]{:S(2)}) async-start(), calls=%async_computation.26 | async-start | bytes 1114112 | tf_op jit(solution)/shard_map/all_gather | solution.py:242
  7.9 119.8 %all-gather.13.cloned.1.call-start = ((), (), s32[]{:S(2)}) async-start(), calls=%async_computation.25 | async-start | bytes 1114112 | tf_op jit(solution)/shard_map/all_gather | solution.py:243
  8.7 133.2 %all-gather.17.cloned.1.call-start = ((), (), s32[]{:S(2)}) async-start(), calls=%async_computation.27 | async-start | bytes 4456448 | tf_op jit(solution)/shard_map/all_gather | solution.py:241
  9.4 280.2 %all-gather.21.cloned.1.call-start = ((), (), s32[]{:S(2)}) async-start(), calls=%async_computation.29 | async-start | bytes 29175808 | tf_op jit(solution)/shard_map/all_gather | solution.py:245
  10.1 440.1 %all-gather.23.cloned.1.call-start = ((), (), s32[]{:S(2)}) async-start(), calls=%async_computation.30 | async-start | bytes 13369344 | tf_op jit(solution)/shard_map/all_gather | solution.py:249
  10.7 449.2 %all-gather.19.cloned.1.call-start = ((), (), s32[]{:S(2)}) async-start(), calls=%async_computation.28 | async-start | bytes 4456448 | tf_op jit(solution)/shard_map/all_gather | solution.py:244
  11.2 558.6 %all-gather.25.cloned.1.call-start = ((), (), s32[]{:S(2)}) async-start(), calls=%async_computation.31 | async-start | bytes 17825792 | tf_op jit(solution)/shard_map/all_gather | solution.py:253
  12.0 685.1 %all-gather.27.cloned.1.call-start = ((), (), s32[]{:S(2)}) async-start(), calls=%async_computation.32 | async-start | bytes 17825792 | tf_op jit(solution)/shard_map/all_gather | solution.py:254
  12.7 811.6 %all-gather.29.cloned.1.call-start = ((), (), s32[]{:S(2)}) async-start(), calls=%async_computation.33 | async-start | bytes 17825792 | tf_op jit(solution)/shard_map/all_gather | solution.py:255
  343.9 77.8 %all-to-all-start.3 = ((bf16[2,192,512]{2,1,0:T(8,128)(2,1)}), bf16[2,192,512]{2,1,0:T(8,128)(2,1)}, u32[]{:S(2)}, u32[]{:S(2)}) async-start(bf16[2,192,512]{2,1,0:T(8,128)(2,1)} %convert_element_type.342), calls=%async_computation.3 | async-start | bytes 786432 | tf_op jit(solution)/shard_map/all_to_all | solution.py:309
  421.6 24.7 all-to-all-start.6
  899.7 175.5 %all-to-all-start.7 = ((bf16[192,2,512]{2,0,1:T(8,128)(2,1)}), bf16[192,2,512]{2,0,1:T(8,128)(2,1)}, u32[]{:S(2)}, u32[]{:S(2)}) async-start(bf16[192,2,512]{2,0,1:T(8,128)(2,1)} %bitcast.488), calls=%async_computation.7 | async-start | bytes 786432 | tf_op jit(solution)/shard_map/all_to_all | solution.py:379
  903.9 322.0 %reduce-scatter.14.cloned.1.call-start = ((), (), s32[]{:S(2)}) async-start(), calls=%async_computation.34 | async-start | bytes 589824 | tf_op jit(solution)/shard_map/reduce_scatter | solution.py:419
  1074.5 178.7 %reduce-scatter.20.cloned.1.call-start = ((), (), s32[]{:S(2)}) async-start(), calls=%async_computation.37 | async-start | bytes 2228224 | tf_op jit(solution)/shard_map/reduce_scatter | solution.py:456
  1092.1 162.8 %reduce-scatter.18.cloned.1.call-start = ((), (), s32[]{:S(2)}) async-start(), calls=%async_computation.36 | async-start | bytes 2228224 | tf_op jit(solution)/shard_map/reduce_scatter | solution.py:455
  1105.2 221.5 %reduce-scatter.22.cloned.1.call-start = ((), (), s32[]{:S(2)}) async-start(), calls=%async_computation.38 | async-start | bytes 8912896 | tf_op jit(solution)/shard_map/reduce_scatter | solution.py:457
  1109.9 325.7 %reduce-scatter.16.cloned.1.call-start = ((), (), s32[]{:S(2)}) async-start(), calls=%async_computation.35 | async-start | bytes 8912896 | tf_op jit(solution)/shard_map/reduce_scatter | solution.py:454
  1126.8 557.1 %reduce-scatter.26.cloned.1.call-start = ((), (), s32[]{:S(2)}) async-start(), calls=%async_computation.40 | async-start | bytes 26738688 | tf_op jit(solution)/shard_map/reduce_scatter | solution.py:462
  1140.0 880.2 %reduce-scatter.28.cloned.1.call-start = ((), (), s32[]{:S(2)}) async-start(), calls=%async_computation.41 | async-start | bytes 35651584 | tf_op jit(solution)/shard_map/reduce_scatter | solution.py:352
  1155.1 1201.5 %reduce-scatter.30.cloned.1.call-start = ((), (), s32[]{:S(2)}) async-start(), calls=%async_computation.42 | async-start | bytes 35651584 | tf_op jit(solution)/shard_map/reduce_scatter | solution.py:353
  1170.3 1522.8 %reduce-scatter.32.cloned.1.call-start = ((), (), s32[]{:S(2)}) async-start(), calls=%async_computation.43 | async-start | bytes 35651584 | tf_op jit(solution)/shard_map/reduce_scatter | solution.py:354
  1214.6 2000.4 %reduce-scatter.24.cloned.1.call-start = ((), (), s32[]{:S(2)}) async-start(), calls=%async_computation.39 | async-start | bytes 58351616 | tf_op jit(solution)/shard_map/reduce_scatter | solution.py:458
  1250.5 2036.6 %reduce-scatter.34.cloned.1.call-start = ((), (), s32[]{:S(2)}) async-start(), calls=%async_computation.44 | async-start | bytes 1949696
  1253.2 2186.9 %all-reduce.33.cloned.1.call-start = ((), (), s32[]{:S(2)}) async-start(), calls=%async_computation.45 | async-start | bytes 12607488 | tf_op jit(solution)/shard_map/psum | solution.py:466
  (174 other events, 4517.0 us)
Sparse Core Ops, SparseCore 0:
  10.2 40.6 all-gather.14
  53.1 36.8 all-gather.12
  92.1 49.6 all-gather.16
  143.2 146.3 all-gather.20
  291.8 99.6 all-gather.22
  393.5 48.7 all-gather.18
  444.4 125.3 all-gather.24
  572.0 125.0 all-gather.26
  699.3 125.0 all-gather.28
  1074.6 11.7 reduce-scatter.13
  1092.2 61.4 reduce-scatter.19
  1157.9 60.5 reduce-scatter.17
  1223.1 103.6 reduce-scatter.21
  1331.2 104.3 reduce-scatter.15
  1440.1 243.6 reduce-scatter.25
  1688.5 331.7 reduce-scatter.27
  2025.0 331.6 reduce-scatter.29
  2361.4 331.6 reduce-scatter.31
  2697.8 517.0 reduce-scatter.23
  3219.5 60.2 reduce-scatter.33
  3284.7 155.2 all-reduce.32
where the time goes:
time: 3470 us; the launch traced here: 3460 us
  waiting for transfers between devices  2520 us (73%)
  matrix products  348 us (10%)
  blocking collectives  252 us (7%)
  local copies, waits for them, and re-layouts  147 us (4%)
  other arithmetic  131 us (4%)
  starting transfers between devices  41.2 us (1%)
    reduce_scatter x1, waiting for transfers between devices, shards(): lax.psum_scatter(grad_wmamba_in, 'fsdp', scatter_dimension=0, tiled=True)  519 us
    reduce_scatter x1, waiting for transfers between devices, shards(): lax.psum_scatter(grad_wgate, 'fsdp', scatter_dimension=0, tiled=True)  334 us
    reduce_scatter x1, waiting for transfers between devices, shards(): lax.psum_scatter(grad_down, 'fsdp', scatter_dimension=0, tiled=True)  334 us
    reduce_scatter x1, waiting for transfers between devices, shards(): lax.psum_scatter(grad_wup, 'fsdp', scatter_dimension=0, tiled=True)  334 us
    reduce_scatter x1, waiting for transfers between devices, shards(): lax.psum_scatter(grad_mamba_out, 'fsdp', scatter_dimension=0, tiled=True)  246 us
    all_gather x1, waiting for transfers between devices, shards(): lax.all_gather(mamba_in_weight, 'fsdp', axis=0, tiled=True)  119 us
    unnamed x2, blocking collectives  117 us
    all_gather x1, waiting for transfers between devices, shards(): lax.all_gather(down_weight, 'fsdp', axis=0, tiled=True)  116 us
  transfers between devices with their start and end apart: 32, of which 18 were waited for; matrix products, arithmetic and copies ran while one was open for 16% of the time, Pallas kernels for 0%

commit v1 on v0

v1 whole, which is shorter than its diff:
```python
import math

import jax
import jax.numpy as jnp
from jax import lax
from jax.sharding import Mesh
from jax.sharding import PartitionSpec as P

HQ = 8
KVH = 2
HD = 128
MH = 48
MP = 64
NST = 256
EPSILON = 1e-05
ROPE_BASE = 100000000000.0
MASKED = -1e30
BF = jnp.bfloat16
F32 = jnp.float32
MESH_AXES = ("x", "z", "y", "c")
FSDP = ("z", "y", "c")
PARTS = 8


def mm(left, right):
    return jnp.dot(left, right, preferred_element_type=F32)


def outer_product(left, right):
    return lax.dot_general(left, right, (((0,), (0,)), ((), ())), preferred_element_type=F32)


def across(left, right):
    return lax.dot_general(left, right, (((1,), (1,)), ((), ())), preferred_element_type=F32)


def norm_factor(values, width=None):
    return lax.rsqrt(jnp.mean(values * values, axis=-1, keepdims=True) + EPSILON)


def norm_back(values, scaling, incoming):
    factor = norm_factor(values)
    normal = values * factor
    scaled = incoming * scaling
    grad_values = factor * (scaled - normal * jnp.mean(scaled * normal, axis=-1, keepdims=True))
    return (grad_values, jnp.sum(incoming * normal, axis=0))


def rope_tables(length, head_size):
    half_size = head_size // 2
    frequency = jnp.exp(
        jnp.arange(half_size, dtype=F32) * (-2.0 * math.log(ROPE_BASE) / head_size)
    )
    angles = jnp.arange(length, dtype=F32)[:, None] * frequency[None, :]
    return (jnp.cos(angles), jnp.sin(angles))


def rotate(values, cosine, sine):
    half = values.shape[-1] // 2
    front, back = values[..., :half], values[..., half:]
    return jnp.concatenate([front * cosine - back * sine, back * cosine + front * sine], axis=-1)


def conv(signal, kernel):
    taps, length = kernel.shape[0], signal.shape[1]
    padded = jnp.pad(signal, ((0, 0), (taps - 1, 0), (0, 0)))
    return sum(padded[:, j : j + length] * kernel[j] for j in range(taps))


def conv_back(signal, kernel, grad):
    taps, length = kernel.shape[0], signal.shape[1]
    padded = jnp.pad(signal, ((0, 0), (taps - 1, 0), (0, 0)))
    later = jnp.pad(grad, ((0, 0), (0, taps - 1), (0, 0)))
    grad_signal = sum(
        later[:, taps - 1 - j : taps - 1 - j + length] * kernel[j] for j in range(taps)
    )
    grad_kernel = jnp.stack(
        [jnp.sum(padded[:, j : j + length] * grad, axis=(0, 1)) for j in range(taps)]
    )
    return grad_signal, grad_kernel, jnp.sum(grad, axis=(0, 1))


def silu_back(values, grad):
    sig = jax.nn.sigmoid(values)
    return grad * sig * (1.0 + values * (1.0 - sig))


def core_parts(xin, step, maps, params):
    xk, xb, mk, mb, decay_log, step_bias, skip = params
    seqs, length, width = xin.shape
    heads = step.shape[-1]
    ux = conv(xin.astype(F32), xk) + xb
    um = conv(maps.astype(F32), mk) + mb
    xs = (ux * jax.nn.sigmoid(ux)).reshape(seqs, length, heads, MP)
    mv = (um * jax.nn.sigmoid(um)).astype(BF)
    bees, cees = mv[..., :NST], mv[..., NST:]
    dt = jax.nn.softplus(step.astype(F32) + step_bias)
    rate = -jnp.exp(decay_log)
    cum = jnp.cumsum(dt * rate, axis=1)
    causal = jnp.arange(length)[:, None] >= jnp.arange(length)[None, :]
    cumt = jnp.swapaxes(cum, 1, 2)
    decay = jnp.exp(jnp.where(causal, cumt[..., :, None] - cumt[..., None, :], MASKED))
    coupling = jnp.einsum("btn,bsn->bts", cees, bees, preferred_element_type=F32)
    mixing = (coupling[:, None] * decay).astype(BF)
    xr = (dt[..., None] * xs).astype(BF)
    y = jnp.einsum("bhts,bshp->bthp", mixing, xr, preferred_element_type=F32)
    return ux, um, xs, bees, cees, dt, rate, decay, mixing, xr, y


def core_forward(xin, step, maps, params):
    parts = core_parts(xin, step, maps, params)
    return (parts[-1] + params[-1][:, None] * parts[2]).reshape(xin.shape)


def core_backward(xin, step, maps, params, grad):
    xk, xb, mk, mb, decay_log, step_bias, skip = params
    ux, um, xs, bees, cees, dt, rate, decay, mixing, xr, y = core_parts(xin, step, maps, params)
    gy = grad.reshape(xs.shape)
    gyf = gy.astype(F32)
    gxr = jnp.einsum("bhts,bthp->bshp", mixing, gy, preferred_element_type=F32)
    gm = jnp.einsum("bthp,bshp->bhts", gy, xr, preferred_element_type=F32)
    gcoup = jnp.sum(gm * decay, axis=1).astype(BF)
    gc = jnp.einsum("bts,bsn->btn", gcoup, bees, preferred_element_type=F32)
    gb = jnp.einsum("bts,btn->bsn", gcoup, cees, preferred_element_type=F32)
    gcum = jnp.sum(gyf * y, axis=-1) - jnp.sum(xr.astype(F32) * gxr, axis=-1)
    ga = jnp.flip(jnp.cumsum(jnp.flip(gcum, 1), axis=1), 1)
    gdt = ga * rate + jnp.sum(gxr * xs, axis=-1)
    gdecay = jnp.sum(ga * dt, axis=(0, 1)) * rate
    gxs = gxr * dt[..., None] + skip[:, None] * gyf
    gskip = jnp.sum(gyf * xs, axis=(0, 1, 3))
    gstep = gdt * jax.nn.sigmoid(step.astype(F32) + step_bias)
    gsb = jnp.sum(gstep, axis=(0, 1))
    gux = silu_back(ux, gxs.reshape(ux.shape))
    gum = silu_back(um, jnp.concatenate([gb, gc], axis=-1))
    gxin, gxk, gxb = conv_back(xin.astype(F32), xk, gux)
    gmaps, gmk, gmb = conv_back(maps.astype(F32), mk, gum)
    return gxin, gstep, gmaps, gxk, gxb, gmk, gmb, gdecay, gsb, gskip


def score_rows(rq, rk):
    length = rq.shape[1]
    causal = jnp.arange(length)[:, None] >= jnp.arange(length)[None, :]
    scores = jnp.einsum("bqd,bkd->bqk", rq, rk, preferred_element_type=F32) * HD ** (-0.5)
    return jnp.where(causal, scores, MASKED)


def attend(rq, rk, v):
    scores = score_rows(rq, rk)
    highest = jnp.max(scores, axis=-1, keepdims=True)
    weights = jnp.exp(scores - highest)
    total = jnp.sum(weights, axis=-1, keepdims=True)
    probs = (weights / total).astype(BF)
    att = jnp.einsum("bqk,bkd->bqd", probs, v, preferred_element_type=F32).astype(BF)
    return att, highest + jnp.log(total)


def attend_back(rq, rk, v, lse, grad):
    p = jnp.exp(score_rows(rq, rk) - lse)
    gv = jnp.einsum("bqk,bqd->bkd", p.astype(BF), grad, preferred_element_type=F32)
    gp = jnp.einsum("bqd,bkd->bqk", grad, v, preferred_element_type=F32)
    gs = (p * (gp - jnp.sum(p * gp, axis=-1, keepdims=True))).astype(BF)
    scale = HD ** (-0.5)
    gq = jnp.einsum("bqk,bkd->bqd", gs, rk, preferred_element_type=F32) * scale
    gk = jnp.einsum("bqk,bqd->bkd", gs, rq, preferred_element_type=F32) * scale
    return gq, gk, gv


def flip(value, *axes):
    count = 2 ** len(axes)
    pairs = [(i, count - 1 - i) for i in range(count)]
    axes = tuple(sorted(axes, key=MESH_AXES.index))
    return lax.ppermute(value, axes, pairs)


def ordered(own, other, axis):
    second = lax.axis_index(axis) == 1
    return jnp.where(second, other, own), jnp.where(second, own, other)


def plane_gather(block):
    half = block.shape[0] // 2
    by_x, by_y = flip(block, "x"), flip(block, "y")
    diagonal = jnp.concatenate([flip(by_x[:half], "y"), flip(by_y[half:], "x")])
    here = [block, by_x, by_y, diagonal]
    there = [flip(v, "c") for v in here]
    out = []
    for own, other in ((0, 1), (2, 3)):
        out += ordered(here[own], here[other], "x")
    for own, other in ((0, 1), (2, 3)):
        out += ordered(there[own], there[other], "x")
    return jnp.concatenate(out)


def plane_scatter(partial):
    rows = partial(1).shape[0]
    far = partial(1).astype(BF)
    near = partial(0)
    width = near.shape[1]
    count = rows // 4
    x = lax.axis_index("x")
    outs = []
    for at, first in ((0, "y"), (1, "x")):
        cols = slice(at * (width // 2), (at + 1) * (width // 2))
        chip = near[:, cols] + flip(far[:, cols], "c").astype(F32)
        chip = chip.reshape(2, 2, count, width // 2)
        if first == "y":
            got = flip(chip[1].astype(BF), "y")
            line = chip[0] + got.astype(F32)
            away = lax.dynamic_index_in_dim(line, 1 - x, 0, keepdims=False)
            kept = lax.dynamic_index_in_dim(line, x, 0, keepdims=False)
            got = flip(away.astype(BF), "x")
        else:
            away = lax.dynamic_index_in_dim(chip, 1 - x, 1, keepdims=False)
            kept = lax.dynamic_index_in_dim(chip, x, 1, keepdims=False)
            line = kept + flip(away.astype(BF), "x").astype(F32)
            kept, got = line[0], flip(line[1].astype(BF), "y")
        outs.append(kept + got.astype(F32))
    return jnp.concatenate(outs, axis=1)


def flip_rows(value, axis):
    got = flip(value, axis)
    if axis == "x":
        return got
    parts = got.reshape((2, 2, -1) + value.shape[1:])
    return jnp.flip(parts, 0 if axis == "c" else 1).reshape(value.shape)


def plane_sum(value):
    for axis in ("c", "y", "x"):
        value = value + flip_rows(value, axis)
    return value


def column_sum(value, axes):
    for axis in axes:
        half = value.shape[1] // 2
        at = lax.axis_index(axis)
        away = lax.dynamic_slice_in_dim(value, (1 - at) * half, half, 1)
        kept = lax.dynamic_slice_in_dim(value, at * half, half, 1)
        value = kept.astype(F32) + flip_rows(away.astype(BF), axis).astype(F32)
    return value


def row_half(value, index):
    half = value.shape[0] // 2
    return value[index * half : (index + 1) * half]


def part_index():
    return 4 * lax.axis_index("x") + 2 * lax.axis_index("c") + lax.axis_index("y")


def half_columns(weight):
    half = weight.shape[1] // 2
    return lax.dynamic_slice_in_dim(weight, lax.axis_index("x") * half, half, 1)


def exchange(blocks, high, low):
    h, l = lax.axis_index(high), lax.axis_index(low)

    def block(dh, dl):
        return lax.dynamic_index_in_dim(blocks, 2 * (h ^ dh) + (l ^ dl), 0, keepdims=False)

    own, by_low = block(0, 0), flip(block(0, 1), low)
    by_high, by_both = flip(block(1, 0), high), flip(block(1, 1), high, low)
    near, far = ordered(own, by_low, low), ordered(by_high, by_both, low)
    first, second = ordered(near[0], far[0], high), ordered(near[1], far[1], high)
    return [[first[0], second[0]], [first[1], second[1]]]


def gather_inner(block):
    by_c = flip(block, "c")
    by_y, by_both = flip(block, "y"), flip(by_c, "y")
    near, far = ordered(block, by_c, "c"), ordered(by_y, by_both, "c")
    first, second = ordered(near[0], far[0], "y"), ordered(near[1], far[1], "y")
    whole = jnp.stack([first[0], second[0], first[1], second[1]], axis=1)
    return whole.reshape(-1, block.shape[-1])


def fetch_columns(weights):
    rows = weights[0].shape[0]
    block = jnp.concatenate(
        [half_columns(w).reshape(rows, 4, w.shape[1] // PARTS) for w in weights], axis=2
    )
    got = exchange(block.transpose(1, 0, 2), "c", "y")
    moved = jnp.concatenate([got[0][0], got[1][0], got[0][1], got[1][1]])
    return lax.all_gather(moved, "z", axis=0, tiled=True)


def return_columns(grad, widths):
    part = lax.psum_scatter(grad.astype(BF), "z", scatter_dimension=0, tiled=True)
    rows, width = part.shape[0] // 4, part.shape[1]
    part = part.reshape(2, 2, rows, width).transpose(1, 0, 2, 3).reshape(4, rows, width)
    got = exchange(part, "c", "y")
    moved = jnp.stack([got[0][0], got[0][1], got[1][0], got[1][1]], axis=1)
    whole = jnp.stack(ordered(moved, flip(moved, "x"), "x"), axis=1)
    outs, at = [], 0
    for w in widths:
        outs.append(whole[..., at : at + w].astype(F32))
        at += w
    return outs


def fetch_rows(weight):
    if lax.axis_size("z") != 4:
        whole = lax.all_gather(weight, FSDP, axis=0, tiled=True)
        rows = whole.shape[0] // PARTS
        return lax.dynamic_slice_in_dim(whole, part_index() * rows, rows, 0)
    block = lax.all_gather(half_columns(weight), "z", axis=0, tiled=False)
    got = exchange(block, "x", "c")
    return jnp.concatenate(
        [jnp.concatenate([got[0][c], got[1][c]], axis=1) for c in (0, 1)], axis=0
    )


def return_rows(grad):
    rows, cols = grad.shape
    if lax.axis_size("z") != 4:
        whole = jnp.zeros((rows * PARTS, cols), BF)
        whole = lax.dynamic_update_slice_in_dim(whole, grad.astype(BF), part_index() * rows, 0)
        whole = lax.psum_scatter(whole, FSDP, scatter_dimension=0, tiled=True)
        return lax.psum(whole, "x").astype(F32)
    block = grad.astype(BF).reshape(2, rows // 2, 2, cols // 2).transpose(2, 0, 1, 3)
    got = exchange(block.reshape(4, rows // 2, cols // 2), "x", "c")
    moved = jnp.stack([got[0][0], got[0][1], got[1][0], got[1][1]])
    part = lax.psum_scatter(moved, "z", scatter_dimension=0, tiled=False)
    return jnp.concatenate(ordered(part, flip(part, "x"), "x"), axis=1).astype(F32)


def pack(arrays, multiple):
    flat = jnp.concatenate([a.reshape(-1) for a in arrays])
    return jnp.pad(flat, (0, -flat.shape[0] % multiple))


def shards(
    tokens,
    cotangent,
    mixer_gain,
    query_weight,
    key_weight,
    value_weight,
    attn_out_weight,
    mamba_in_weight,
    conv_weight,
    conv_bias,
    decay_log,
    step_bias,
    skip_gain,
    mamba_gain,
    mamba_out_weight,
    ffn_gain,
    gate_weight,
    up_weight,
    down_weight,
):
    token_count, model_dim = tokens.shape[1], tokens.shape[2]
    length = 2 * token_count
    inner = MH * MP
    channels = inner + 2 * NST
    part = part_index()
    wide, heads = inner // PARTS, MH // PARTS
    rows = token_count * PARTS
    seqs = rows // length
    fsdp = lax.axis_size("z") * 4

    smalls = [mixer_gain, ffn_gain, mamba_gain, conv_bias, conv_weight]
    gathered = lax.all_gather(pack(smalls, 128), FSDP, axis=0, tiled=False)
    got, at = [], 0
    for s in smalls:
        got.append(gathered[:, at : at + s.size].reshape((fsdp,) + s.shape))
        at += s.size
    gain_in = got[0].reshape(-1).astype(F32)
    gain_ffn = got[1].reshape(-1).astype(F32)
    gain_mamba = got[2].reshape(-1).astype(F32)
    bias_full = got[3].reshape(-1).astype(F32)
    conv_full = got[4].transpose(1, 0, 2).reshape(4, channels).astype(F32)
    gain_mamba = lax.dynamic_slice_in_dim(gain_mamba, part * wide, wide, 0)

    def own_heads(v):
        return lax.dynamic_slice_in_dim(v.astype(F32), part * heads, heads, 0)

    core_params = (
        lax.dynamic_slice_in_dim(conv_full, part * wide, wide, 1),
        lax.dynamic_slice_in_dim(bias_full, part * wide, wide, 0),
        conv_full[:, inner:],
        bias_full[inner:],
        own_heads(decay_log),
        own_heads(step_bias),
        own_heads(skip_gain),
    )

    kvh = HD * lax.axis_index("x")
    shared = jnp.concatenate(
        [
            lax.dynamic_slice_in_dim(key_weight, kvh, HD, 1),
            lax.dynamic_slice_in_dim(value_weight, kvh, HD, 1),
            mamba_in_weight[:, 2 * inner :],
        ],
        axis=1,
    )
    shared = gather_inner(lax.all_gather(shared, "z", axis=0, tiled=False))
    w_in = fetch_columns(
        [query_weight, mamba_in_weight[:, :inner], mamba_in_weight[:, inner : 2 * inner]]
    )
    w_attn_out = fetch_rows(attn_out_weight)
    w_mamba_out = fetch_rows(mamba_out_weight)
    w_gateup = fetch_columns([gate_weight, up_weight])
    w_down = fetch_rows(down_weight)
    ff = w_down.shape[0]

    token_rows = tokens.reshape(token_count, model_dim).astype(F32)
    hidden = (token_rows * norm_factor(token_rows) * gain_in).astype(BF)
    hidden = plane_gather(hidden)
    incoming = plane_gather(cotangent.reshape(token_count, model_dim))

    projected = mm(hidden, w_in)
    query = projected[:, :HD].astype(BF)
    gate_branch = projected[:, HD : HD + wide]
    xin = projected[:, HD + wide :].astype(BF).reshape(seqs, length, wide)
    common = mm(hidden, shared).astype(BF)
    key, value = common[:, :HD], common[:, HD : 2 * HD]
    maps = common[:, 2 * HD : 2 * HD + 2 * NST].reshape(seqs, length, 2 * NST)
    step = lax.dynamic_slice_in_dim(common, 2 * HD + 2 * NST + part * heads, heads, 1)
    step = step.reshape(seqs, length, heads)

    cosine, sine = rope_tables(length, HD)
    rq = rotate(query.reshape(seqs, length, HD).astype(F32), cosine, sine).astype(BF)
    rk = rotate(key.reshape(seqs, length, HD).astype(F32), cosine, sine).astype(BF)
    value = value.reshape(seqs, length, HD)
    attended, lse = attend(rq, rk, value)
    attended = attended.reshape(rows, HD)
    scanned = core_forward(xin, step, maps, core_params).reshape(rows, wide)
    scanned = scanned.astype(BF).astype(F32)

    sig_z = jax.nn.sigmoid(gate_branch)
    silu_z = gate_branch * sig_z
    gated = scanned * silu_z
    squares = plane_sum(jnp.sum(gated * gated, axis=-1))
    factor = lax.rsqrt(squares / inner + EPSILON)[:, None]
    normal = gated * factor
    normed = (normal * gain_mamba).astype(BF)
    mixed = jnp.concatenate([attended, normed], axis=1)
    w_out = jnp.concatenate([w_attn_out, w_mamba_out], axis=0)
    mixer_sum = plane_scatter(lambda i: mm(row_half(mixed, i), w_out))
    middle = token_rows + mixer_sum
    second = (middle * norm_factor(middle) * gain_ffn).astype(BF)
    second = plane_gather(second)
    gate_up = mm(second, w_gateup)
    gate_act, up_act = gate_up[:, :ff], gate_up[:, ff:]
    sig_g = jax.nn.sigmoid(gate_act)
    active = (gate_act * sig_g * up_act).astype(BF)
    result = middle + plane_scatter(lambda i: mm(row_half(active, i), w_down))
    output = result.astype(BF).reshape(1, token_count, model_dim)

    grad_down = outer_product(active, incoming)
    grad_active = across(incoming, w_down)
    grad_gate = grad_active * up_act * sig_g * (1.0 + gate_act * (1.0 - sig_g))
    grad_up = grad_active * gate_act * sig_g
    grad_gateup = jnp.concatenate([grad_gate.astype(BF), grad_up.astype(BF)], axis=1)
    grad_wgateup = outer_product(second, grad_gateup)
    grad_second = plane_scatter(lambda i: across(row_half(grad_gateup, i), w_gateup))
    grad_norm, grad_gain_ffn = norm_back(middle, gain_ffn, grad_second)
    grad_middle = cotangent.reshape(token_count, model_dim).astype(F32) + grad_norm

    grad_mixer = plane_gather(grad_middle.astype(BF))
    grad_out = outer_product(mixed, grad_mixer)
    grad_att = across(grad_mixer, w_attn_out).astype(BF).reshape(seqs, length, HD)
    grad_normed = across(grad_mixer, w_mamba_out)
    grad_gain_mamba = jnp.sum(grad_normed * normal, axis=0)
    scaled = grad_normed * gain_mamba
    dots = plane_sum(jnp.sum(scaled * normal, axis=-1))[:, None] / inner
    grad_gated = factor * (scaled - normal * dots)
    grad_scanned = (grad_gated * silu_z).astype(BF).reshape(seqs, length, wide)
    grad_gate_branch = grad_gated * scanned * sig_z * (1.0 + gate_branch * (1.0 - sig_z))

    gq, gk, gv = attend_back(rq, rk, value, lse, grad_att)
    gq = rotate(gq, cosine, -sine).astype(BF).reshape(rows, HD)
    gk = rotate(gk, cosine, -sine).reshape(rows, HD)
    gv = gv.reshape(rows, HD)
    gxin, gstep, gmaps, gxk, gxb, gmk, gmb, gdecay, gsb, gskip = core_backward(
        xin, step, maps, core_params, grad_scanned
    )
    grad_in = jnp.concatenate(
        [gq, grad_gate_branch.astype(BF), gxin.reshape(rows, wide).astype(BF)], axis=1
    )
    grad_win = outer_product(hidden, grad_in)
    gstep_all = lax.dynamic_update_slice_in_dim(
        jnp.zeros((rows, MH), BF), gstep.reshape(rows, heads).astype(BF), part * heads, 1
    )
    grad_common = jnp.concatenate(
        [gk.astype(BF), gv.astype(BF), gmaps.reshape(rows, 2 * NST).astype(BF), gstep_all], axis=1
    )
    kv_part = column_sum(grad_common[:, : 2 * HD], ("c", "y"))
    maps_part = column_sum(grad_common[:, 2 * HD : 2 * HD + 2 * NST], ("c", "y", "x"))
    grad_slices = jnp.concatenate([kv_part, maps_part, gstep.reshape(rows, heads)], axis=1)
    grad_wslices = outer_product(hidden, grad_slices.astype(BF))
    grad_hidden = plane_scatter(
        lambda i: across(row_half(grad_in, i), w_in) + across(row_half(grad_common, i), shared)
    )
    grad_norm, grad_gain_in = norm_back(token_rows, gain_in, grad_hidden)
    tokens_grad = (grad_middle + grad_norm).reshape(1, token_count, model_dim)

    shard_down = return_rows(grad_down)
    shard_gate, shard_up = return_columns(grad_wgateup, [ff, ff])
    shard_attn_out = return_rows(grad_out[:HD])
    shard_mamba_out = return_rows(grad_out[HD:])
    grad_win = jnp.concatenate([grad_win, grad_wslices], axis=1)
    shard_query, shard_gate_br, shard_xin, kv, mapped, stepped = return_columns(
        grad_win, [HD, wide, wide, HD // 2, NST // 4, heads]
    )
    count = query_weight.shape[0]
    shard_key = kv[:, :, :2].reshape(count, 2 * HD)
    shard_value = kv[:, :, 2:].reshape(count, 2 * HD)
    shard_mamba_in = jnp.concatenate(
        [
            shard_gate_br.reshape(count, inner),
            shard_xin.reshape(count, inner),
            mapped.transpose(0, 2, 1, 3).reshape(count, 2 * NST),
            stepped.reshape(count, MH),
        ],
        axis=1,
    )
    shard_query = shard_query.reshape(count, HQ * HD)
    shard_gate = shard_gate.reshape(count, PARTS * ff)
    shard_up = shard_up.reshape(count, PARTS * ff)

    conv_grad = jnp.zeros((4, channels), F32)
    conv_grad = lax.dynamic_update_slice_in_dim(conv_grad, gxk, part * wide, 1)
    conv_grad = conv_grad.at[:, inner:].set(gmk)
    bias_grad = jnp.zeros((channels,), F32)
    bias_grad = lax.dynamic_update_slice_in_dim(bias_grad, gxb, part * wide, 0)
    bias_grad = bias_grad.at[inner:].set(gmb)
    gain_grad = lax.dynamic_update_slice_in_dim(
        jnp.zeros((inner,), F32), grad_gain_mamba, part * wide, 0
    )
    head_grad = lax.dynamic_update_slice_in_dim(
        jnp.zeros((3, MH), F32), jnp.stack([gdecay, gsb, gskip]), part * heads, 1
    )
    spread = [grad_gain_in, grad_gain_ffn, gain_grad, bias_grad]
    little = [v.reshape(fsdp, -1) for v in spread]
    little.append(conv_grad.reshape(4, fsdp, -1).transpose(1, 0, 2).reshape(fsdp, -1))
    little.append(jnp.broadcast_to(head_grad.reshape(1, -1), (fsdp, 3 * MH)))
    little = jnp.concatenate(little, axis=1)
    total = lax.all_to_all(little, FSDP, split_axis=0, concat_axis=0, tiled=True).sum(axis=0)
    total = total + flip(total, "x")
    got, at = [], 0
    for like in (mixer_gain, ffn_gain, mamba_gain, conv_bias, conv_weight, head_grad):
        got.append(total[at : at + like.size].reshape(like.shape))
        at += like.size

    return (
        output,
        tokens_grad,
        got[0],
        shard_query,
        shard_key,
        shard_value,
        shard_attn_out,
        shard_mamba_in,
        got[4],
        got[3],
        got[5][0],
        got[5][1],
        got[5][2],
        got[2],
        shard_mamba_out,
        got[1],
        shard_gate,
        shard_up,
        shard_down,
    )


def solution(mesh):
    fsdp = mesh.shape["fsdp"]
    grid = Mesh(mesh.devices.reshape(2, fsdp // 4, 2, 2), ("x", "z", "y", "c"))
    rows, flat, whole = P(FSDP, None), P(FSDP), P()
    stream = P(FSDP, "x", None)
    weights = (
        flat, rows, rows, rows, rows, rows, P(None, FSDP), flat, whole, whole, whole,
        flat, rows, flat, rows, rows, rows,
    )
    return jax.shard_map(
        shards,
        mesh=grid,
        in_specs=(stream, stream) + weights,
        out_specs=(stream, stream) + weights,
        check_vma=False,
    )
```

time: 3470 us -> 1020 us (0.29)
  waiting for transfers between devices: 2520 us -> 297 us
  matrix products: 348 us -> 162 us
  blocking collectives: 252 us -> 81.3 us
  starting transfers between devices: 41.2 us -> 96.4 us
  other arithmetic: 131 us -> 184 us
    reduce_scatter x10 -> x5, waiting for transfers between devices: 1940 us -> 0.03 us  [the longest x3 0.02 us: return_rows(): part = lax.psum_scatter(moved, 'z', scatter_dimension=0, tiled=False)]
    all_gather x9 -> x4, waiting for transfers between devices: 467 us -> 0.01 us  [the longest x2 0.01 us: fetch_rows(): block = lax.all_gather(half_columns(weight), 'z', axis=0, tiled=False)]
    ppermute x0 -> x106, waiting for transfers between devices: none -> 287 us  [flip(): return lax.ppermute(value, axes, pairs)]
    dot_general x66 -> x28, matrix products: 258 us -> 126 us  [the longest x7 47.4 us: mm(): return jnp.dot(left, right, preferred_element_type=F32)]
    unnamed x2 -> x0, blocking collectives: 117 us -> none
    ppermute x0 -> x106, starting transfers between devices: none -> 84.8 us  [flip(): return lax.ppermute(value, axes, pairs)]
    psum x1 -> x0, waiting for transfers between devices: 65.1 us -> none  [shards(): lax.psum(mixer_shards[1].astype(jnp.bfloat16), 'seq').astype(jnp.float32)]
    dot_general x9 -> x5, matrix products: 89.8 us -> 35.2 us  [outer_product(): lax.dot_general(left, right, (((0,), (0,)), ((), ())), preferred_element_...]
  transfers between devices with their start and end apart: 32 -> 116, of which waited for: 18 -> 48; matrix products, arithmetic and copies ran while one was open for 16% -> 45% of each run, Pallas kernels for 0% -> 0%
where the time goes in v1:
time: 1020 us; the launch traced here: 1000 us
  waiting for transfers between devices  297 us (29%)
  other arithmetic  184 us (18%)
  local copies, waits for them, and re-layouts  167 us (16%)
  matrix products  162 us (16%)
  starting transfers between devices  96.4 us (9%)
  blocking collectives  81.3 us (8%)
  between operations  17.8 us (2%)
    ppermute x106, waiting for transfers between devices, flip(): return lax.ppermute(value, axes, pairs)  287 us
    ppermute x106, starting transfers between devices, flip(): return lax.ppermute(value, axes, pairs)  84.8 us
    dot_general x7, matrix products, mm(): return jnp.dot(left, right, preferred_element_type=F32)  47.4 us
    dot_general x9, matrix products, across(): lax.dot_general(left, right, (((1,), (1,)), ((), ())), preferred_element_...  46.6 us
    all_gather x1, blocking collectives, shards(): shared = gather_inner(lax.all_gather(shared, 'z', axis=0, tiled=False))  39.4 us
    unnamed x404, local copies, waits for them, and re-layouts  36.6 us
    dot_general x5, matrix products, outer_product(): lax.dot_general(left, right, (((0,), (0,)), ((), ())), preferred_element_...  35.2 us
    unnamed x29, other arithmetic  26.4 us
  transfers between devices with their start and end apart: 116, of which 48 were waited for; matrix products, arithmetic and copies ran while one was open for 45% of the time, Pallas kernels for 0%

profile of v1, /device:TPU:0, one launch (start us, length us, event | category | flops | bytes accessed | tf_op | source)
XLA Modules:
  0.0 1004.8 jit_solution(7236463954632380060)
XLA Ops:
  26.2 22.5 %all-gather.5 = bf16[16,1,1664]{2,1,0:T(2,128)(2,1)S(1)} all-gather(bf16[1,1,1664]{2,1,0:T(2,128)(2,1)S(1)} %reshape.824), channel_id=2, replica_groups=mesh['x'=2,'z'=4,'y'=2,'c'=2] {'z','y','c'}, dimensions={0}, use_global_device_ids=true | all-gather | bytes 56576 | tf_op jit(solution)/shard_map/all_gather | solution.py:368
  54.4 19.4 %all-gather.2 = bf16[256,1024]{1,0:T(8,128)(2,1)S(1)} all-gather(bf16[64,1024]{1,0:T(8,128)(2,1)S(1)} %constant_dynamic-slice_fusion.6), channel_id=4, replica_groups=mesh['x'=2,'z'=4,'y'=2,'c'=2] {'z'}, dimensions={0}, use_global_device_ids=true | all-gather | bytes 655360 | tf_op jit(solution)/shard_map/all_gather | solution.py:310
  89.8 39.4 %all-gather.1 = bf16[512,816]{0,1:T(8,128)(2,1)} all-gather(bf16[128,816]{0,1:T(8,128)(2,1)S(1)} %pad_maximum_fusion.23), channel_id=3, replica_groups=mesh['x'=2,'z'=4,'y'=2,'c'=2] {'z'}, dimensions={0}, use_global_device_ids=true | all-gather | bytes 1044480 | tf_op jit(solution)/shard_map/all_gather | solution.py:402
  164.2 17.5 %collective-permute-done.49 = bf16[192,2048]{1,0:T(8,128)(2,1)} collective-permute-done((bf16[192,2048]{1,0:T(8,128)(2,1)S(1)}, bf16[192,2048]{1,0:T(8,128)(2,1)}, u32[]{:S(2)}, u32[]{:S(2)}) %collective-permute-start.49) | collective-permute-done | bytes 786464 | tf_op jit(solution)/shard_map/ppermute | solution.py:172
  207.7 13.2 %collective-permute-done.13 = bf16[4,128,816]{1,0,2:T(4,128)(2,1)S(1)} collective-permute-done((bf16[4,128,816]{1,0,2:T(4,128)(2,1)S(1)}, bf16[4,128,816]{1,0,2:T(4,128)(2,1)S(1)}, u32[]{:S(2)}, u32[]{:S(2)}) %collective-permute-start.13) | collective-permute-done | bytes 835616 | tf_op jit(solution)/shard_map/ppermute | solution.py:172
  220.9 17.5 %collective-permute-done.12 = bf16[4,128,816]{1,0,2:T(4,128)(2,1)S(1)} collective-permute-done((bf16[4,128,816]{1,0,2:T(4,128)(2,1)S(1)}, bf16[4,128,816]{1,0,2:T(4,128)(2,1)S(1)}, u32[]{:S(2)}, u32[]{:S(2)}) %collective-permute-start.12) | collective-permute-done | bytes 835616 | tf_op jit(solution)/shard_map/ppermute | solution.py:172
  316.7 11.4 %fusion.178 = (bf16[1536,896]{1,0:T(8,128)(2,1)S(1)}, f32[1536,896]{1,0:T(8,128)}) fusion(bf16[1536,2048]{1,0:T(8,128)(2,1)} %select_dynamic-update-slice_fusion.24, bf16[2048,896]{0,1:T(8,128)(2,1)} %all-gather.11.cloned.1.call-done), kind=kOutput, calls=%fused_computation.576 | convolution fusion | flops 5638520832 | bytes 18219008 | tf_op jit(solution)/shard_map/dot_general | solution.py:26
  391.2 13.2 %collective-permute-done.27 = bf16[2,192,1024]{2,1,0:T(8,128)(2,1)S(1)} collective-permute-done((bf16[2,192,1024]{2,1,0:T(8,128)(2,1)S(1)}, bf16[2,192,1024]{2,1,0:T(8,128)(2,1)S(1)}, u32[]{:S(2)}, u32[]{:S(2)}) %collective-permute-start.27) | collective-permute-done | bytes 786464 | tf_op jit(solution)/shard_map/ppermute | solution.py:172
  432.4 10.8 %collective-permute-done.40 = bf16[256,1024]{1,0:T(8,128)(2,1)S(1)} collective-permute-done((bf16[256,1024]{1,0:T(8,128)(2,1)S(1)}, bf16[256,1024]{1,0:T(8,128)(2,1)S(1)}, u32[]{:S(2)}, u32[]{:S(2)}) %collective-permute-start.40) | collective-permute-done | bytes 524320 | tf_op jit(solution)/shard_map/ppermute | solution.py:172
  448.1 12.4 %collective-permute-done.29 = bf16[192,2048]{1,0:T(8,128)(2,1)S(1)} collective-permute-done((bf16[192,2048]{1,0:T(8,128)(2,1)S(1)}, bf16[192,2048]{1,0:T(8,128)(2,1)S(1)}, u32[]{:S(2)}, u32[]{:S(2)}) %collective-permute-start.29) | collective-permute-done | bytes 786464 | tf_op jit(solution)/shard_map/ppermute | solution.py:172
  476.4 10.7 %fusion.180 = f32[1536,1024]{0,1:T(8,128)S(1)} fusion(bf16[1536,2048]{1,0:T(8,128)(2,1)} %select_dynamic-update-slice_fusion.16, bf16[2048,1024]{1,0:T(8,128)(2,1)} %all-gather.13.cloned.1.call-done), kind=kOutput, calls=%fused_computation.578 | convolution fusion | flops 6442450944 | bytes 16777216 | tf_op jit(solution)/shard_map/dot_general | solution.py:26
  533.5 10.0 collective-permute-done.61
  563.2 10.4 %collective-permute-done.102 = bf16[256,1024]{1,0:T(8,128)(2,1)S(1)} collective-permute-done((bf16[256,1024]{1,0:T(8,128)(2,1)S(1)}, bf16[256,1024]{1,0:T(8,128)(2,1)S(1)}, u32[]{:S(2)}, u32[]{:S(2)}) %collective-permute-start.102) | collective-permute-done | bytes 524320 | tf_op jit(solution)/shard_map/ppermute | solution.py:172
  578.0 13.3 %collective-permute-done.63 = bf16[192,2048]{1,0:T(8,128)(2,1)S(1)} collective-permute-done((bf16[192,2048]{1,0:T(8,128)(2,1)S(1)}, bf16[192,2048]{1,0:T(8,128)(2,1)S(1)}, u32[]{:S(2)}, u32[]{:S(2)}) %collective-permute-start.63) | collective-permute-done | bytes 786464 | tf_op jit(solution)/shard_map/ppermute | solution.py:172
  658.5 10.5 %collective-permute-done.47 = bf16[2,192,1024]{2,1,0:T(8,128)(2,1)} collective-permute-done((bf16[2,192,1024]{2,1,0:T(8,128)(2,1)S(1)}, bf16[2,192,1024]{2,1,0:T(8,128)(2,1)}, u32[]{:S(2)}, u32[]{:S(2)}) %collective-permute-start.47) | collective-permute-done | bytes 786464 | tf_op jit(solution)/shard_map/ppermute | solution.py:172
  673.1 12.1 %convolution_convert_fusion = bf16[2048,1024]{1,0:T(8,128)(2,1)} fusion(bf16[1536,2048]{1,0:T(8,128)(2,1)} %select_dynamic-update-slice_fusion.16, bf16[1536,512]{0,1:T(8,128)(2,1)S(1)} %copy-done.188, bf16[1536,512]{0,1:T(8,128)(2,1)S(1)} %copy-done.190), kind=kOutput, calls=%fused_computation.22 | convolution fusion | flops 6450839552 | bytes 13631488 | tf_op jit(solution)/shard_map/dot_general | solution.py:30
  750.4 8.2 multiply_reduce_fusion.4
  771.5 10.4 %convolution_convert_fusion.1 = bf16[2048,896]{0,1:T(8,128)(2,1)} fusion(bf16[1536,2048]{1,0:T(8,128)(2,1)} %select_dynamic-update-slice_fusion.24, bf16[1536,896]{1,0:T(8,128)(2,1)S(1)} %pad_maximum_fusion.4), kind=kOutput, calls=%fused_computation.23 | convolution fusion | flops 5638979584 | bytes 12713984 | tf_op jit(solution)/shard_map/dot_general | solution.py:30
  800.2 11.9 %collective-permute-done.82 = bf16[1536,64]{1,0:T(8,128)(2,1)} collective-permute-done((bf16[1536,64]{1,0:T(8,128)(2,1)}, bf16[1536,64]{1,0:T(8,128)(2,1)}, u32[]{:S(2)}, u32[]{:S(2)}) %collective-permute-start.82) | collective-permute-done | bytes 196640 | tf_op jit(solution)/shard_map/ppermute | solution.py:172
  818.5 9.2 collective-permute-done.85
  870.0 9.5 collective-permute-done.75
  896.8 11.1 %all-to-all-start = ((f32[16,1,1712]{2,1,0:T(1,128)}), f32[16,1,1712]{2,1,0:T(1,128)S(1)}, u32[]{:S(2)}, u32[]{:S(2)}) async-start(f32[16,1,1712]{2,1,0:T(1,128)} %copy.510), calls=%async_computation | async-start | bytes 229376 | tf_op jit(solution)/shard_map/all_to_all | solution.py:545
  907.9 10.4 %all-to-all-done = f32[16,1,1712]{2,1,0:T(1,128)S(1)} async-done(((f32[16,1,1712]{2,1,0:T(1,128)}), f32[16,1,1712]{2,1,0:T(1,128)S(1)}, u32[]{:S(2)}, u32[]{:S(2)}) %all-to-all-start) | async-done | bytes 109600 | tf_op jit(solution)/shard_map/all_to_all | solution.py:545
  982.7 8.8 collective-permute-done.89
  (993 shorter events, 663.1 us)
Async XLA Ops:
  7.2 283.9 %all-gather.15.cloned.1.call-start = ((), (), s32[]{:S(2)}) async-start(), calls=%async_computation.13 | async-start | bytes 1966080 | tf_op jit(solution)/shard_map/all_gather | solution.py:310
  9.2 307.4 %all-gather.11.cloned.1.call-start = ((), (), s32[]{:S(2)}) async-start(), calls=%async_computation.6 | async-start | bytes 4587520 | tf_op jit(solution)/shard_map/all_gather | solution.py:288
  25.9 385.1 %all-gather.17.cloned.1.call-start = ((), (), s32[]{:S(2)}) async-start(), calls=%async_computation.14 | async-start | bytes 2621440 | tf_op jit(solution)/shard_map/all_gather | solution.py:310
  51.0 110.0 %collective-permute-start.2 = (bf16[192,2048]{1,0:T(8,128)(2,1)}, bf16[192,2048]{1,0:T(8,128)(2,1)S(1)}, u32[]{:S(2)}, u32[]{:S(2)}) collective-permute-start(bf16[192,2048]{1,0:T(8,128)(2,1)} %fusion.31), channel_id=1, source_target_pairs={{0,2},{2,0},{1,3},{3,1},{4,6},{6,4},{5,7},{7,5},{8,10},{10,8},{9,1... | collective-permute-start | bytes 2359304 | tf_op jit(solution)/shard_map/ppermute | solution.py:172
  51.0 110.1 %collective-permute-start = (bf16[192,2048]{1,0:T(8,128)(2,1)}, bf16[192,2048]{1,0:T(8,128)(2,1)S(1)}, u32[]{:S(2)}, u32[]{:S(2)}) collective-permute-start(bf16[192,2048]{1,0:T(8,128)(2,1)} %fusion.31), channel_id=1, source_target_pairs={{0,16},{16,0},{1,17},{17,1},{2,18},{18,2},{3,19},{19,3},{4,20},{20... | collective-permute-start | bytes 2359304 | tf_op jit(solution)/shard_map/ppermute | solution.py:172
  53.4 423.0 %all-gather.13.cloned.1.call-start = ((), (), s32[]{:S(2)}) async-start(), calls=%async_computation.7 | async-start | bytes 5242880 | tf_op jit(solution)/shard_map/all_gather | solution.py:288
  74.5 62.4 %collective-permute-start.19 = (bf16[64,1024]{1,0:T(8,128)(2,1)}, bf16[64,1024]{1,0:T(8,128)(2,1)}, u32[]{:S(2)}, u32[]{:S(2)}) collective-permute-start(bf16[64,1024]{1,0:T(8,128)(2,1)} %get-tuple-element.312), channel_id=1, source_target_pairs={{0,1},{1,0},{2,3},{3,2},{4,5},{5,4},{6,7},{7,6},{8,9},{9,8},{10,11... | collective-permute-start | bytes 393224 | tf_op jit(solution)/shard_map/ppermute | solution.py:172
  74.6 64.5 %collective-permute-start.18 = (bf16[64,1024]{1,0:T(8,128)(2,1)}, bf16[64,1024]{1,0:T(8,128)(2,1)}, u32[]{:S(2)}, u32[]{:S(2)}) collective-permute-start(bf16[64,1024]{1,0:T(8,128)(2,1)} %get-tuple-element.313), channel_id=1, source_target_pairs={{0,16},{16,0},{1,17},{17,1},{2,18},{18,2},{3,19},{19,3},{4,20},{20... | collective-permute-start | bytes 393224 | tf_op jit(solution)/shard_map/ppermute | solution.py:172
  74.7 64.3 %collective-permute-start.17 = (bf16[64,1024]{1,0:T(8,128)(2,1)}, bf16[64,1024]{1,0:T(8,128)(2,1)}, u32[]{:S(2)}, u32[]{:S(2)}) collective-permute-start(bf16[64,1024]{1,0:T(8,128)(2,1)} %get-tuple-element.314), channel_id=1, source_target_pairs={{0,17},{1,16},{16,1},{17,0},{2,19},{3,18},{18,3},{19,2},{4,21},{5,... | collective-permute-start | bytes 393224 | tf_op jit(solution)/shard_map/ppermute | solution.py:172
  156.2 46.6 %collective-permute-start.5 = (bf16[192,2048]{1,0:T(8,128)(2,1)}, bf16[192,2048]{1,0:T(8,128)(2,1)}, u32[]{:S(2)}, u32[]{:S(2)}) collective-permute-start(bf16[192,2048]{1,0:T(8,128)(2,1)} %fusion.31), channel_id=1, source_target_pairs={{0,1},{1,0},{2,3},{3,2},{4,5},{5,4},{6,7},{7,6},{8,9},{9,8},{10,11... | collective-permute-start | bytes 2359304 | tf_op jit(solution)/shard_map/ppermute | solution.py:172
  156.6 221.9 %collective-permute-start.54 = (bf16[192,2048]{1,0:T(8,128)(2,1)S(1)}, bf16[192,2048]{1,0:T(8,128)(2,1)}, u32[]{:S(2)}, u32[]{:S(2)}) collective-permute-start(bf16[192,2048]{1,0:T(8,128)(2,1)S(1)} %bitcast.555), channel_id=1, source_target_pairs={{0,1},{1,0},{2,3},{3,2},{4,5},{5,4},{6,7},{7,6},{8,9},{9,8},{10,11... | collective-permute-start | bytes 2359304 | tf_op jit(solution)/shard_map/ppermute | solution.py:172
  161.0 527.7 %reduce-scatter.14.cloned.1.call-start = ((), (), s32[]{:S(2)}) async-start(), calls=%async_computation.12 | async-start | bytes 2621440 | tf_op jit(solution)/shard_map/reduce_scatter | solution.py:327
  202.8 53.4 %collective-permute-start.7 = (bf16[192,2048]{1,0:T(8,128)(2,1)S(1)}, bf16[192,2048]{1,0:T(8,128)(2,1)}, u32[]{:S(2)}, u32[]{:S(2)}) collective-permute-start(bf16[192,2048]{1,0:T(8,128)(2,1)S(1)} %collective-permute-done.2), channel_id=1, source_target_pairs={{0,1},{1,0},{2,3},{3,2},{4,5},{5,4},{6,7},{7,6},{8,9},{9,8},{10,11... | collective-permute-start | bytes 2359304 | tf_op jit(solution)/shard_map/ppermute | solution.py:172
  203.1 185.4 %collective-permute-start.56 = (bf16[192,2048]{1,0:T(8,128)(2,1)}, bf16[192,2048]{1,0:T(8,128)(2,1)}, u32[]{:S(2)}, u32[]{:S(2)}) collective-permute-start(bf16[192,2048]{1,0:T(8,128)(2,1)} %collective-permute-done.51), channel_id=1, source_target_pairs={{0,1},{1,0},{2,3},{3,2},{4,5},{5,4},{6,7},{7,6},{8,9},{9,8},{10,11... | collective-permute-start | bytes 2359304 | tf_op jit(solution)/shard_map/ppermute | solution.py:172
  302.2 76.3 %collective-permute-start.53 = (bf16[192,2048]{1,0:T(8,128)(2,1)}, bf16[192,2048]{1,0:T(8,128)(2,1)S(1)}, u32[]{:S(2)}, u32[]{:S(2)}) collective-permute-start(bf16[192,2048]{1,0:T(8,128)(2,1)} %collective-permute-done.49), channel_id=1, source_target_pairs={{0,1},{1,0},{2,3},{3,2},{4,5},{5,4},{6,7},{7,6},{8,9},{9,8},{10,11... | collective-permute-start | bytes 2359304 | tf_op jit(solution)/shard_map/ppermute | solution.py:172
  560.5 67.7 %collective-permute-start.43 = (bf16[768,1024]{1,0:T(8,128)(2,1)}, bf16[768,1024]{1,0:T(8,128)(2,1)}, u32[]{:S(2)}, u32[]{:S(2)}) collective-permute-start(bf16[768,1024]{1,0:T(8,128)(2,1)} %get-tuple-element.218), channel_id=1, source_target_pairs={{0,1},{1,0},{2,3},{3,2},{4,5},{5,4},{6,7},{7,6},{8,9},{9,8},{10,11... | collective-permute-start | bytes 4718600 | tf_op jit(solution)/shard_map/ppermute | solution.py:172
  563.2 65.0 %collective-permute-start.46 = (bf16[768,1024]{1,0:T(8,128)(2,1)}, bf16[768,1024]{1,0:T(8,128)(2,1)}, u32[]{:S(2)}, u32[]{:S(2)}) collective-permute-start(bf16[768,1024]{1,0:T(8,128)(2,1)} %get-tuple-element.219), channel_id=1, source_target_pairs={{0,1},{1,0},{2,3},{3,2},{4,5},{5,4},{6,7},{7,6},{8,9},{9,8},{10,11... | collective-permute-start | bytes 4718600 | tf_op jit(solution)/shard_map/ppermute | solution.py:172
  575.5 287.8 %reduce-scatter.8.cloned.1.call-start = ((), (), s32[]{:S(2)}) async-start(), calls=%async_computation.9 | async-start | bytes 655360 | tf_op jit(solution)/shard_map/reduce_scatter | solution.py:327
  626.0 297.7 %reduce-scatter.10.cloned.1.call-start = ((), (), s32[]{:S(2)}) async-start(), calls=%async_computation.10 | async-start | bytes 1966080 | tf_op jit(solution)/shard_map/reduce_scatter | solution.py:327
  646.9 278.1 %reduce-scatter.12.cloned.1.call-start = ((), (), s32[]{:S(2)}) async-start(), calls=%async_computation.11 | async-start | bytes 5242880 | tf_op jit(solution)/shard_map/reduce_scatter | solution.py:292
  685.3 243.9 %reduce-scatter.6.cloned.1.call-start = ((), (), s32[]{:S(2)}) async-start(), calls=%async_computation.8 | async-start | bytes 5283840 | tf_op jit(solution)/shard_map/reduce_scatter | solution.py:292
  688.8 173.3 %collective-permute-start.105 = (bf16[256,1024]{1,0:T(8,128)(2,1)}, bf16[256,1024]{1,0:T(8,128)(2,1)}, u32[]{:S(2)}, u32[]{:S(2)}) collective-permute-start(bf16[256,1024]{1,0:T(8,128)(2,1)} %bitcast.628), channel_id=1, source_target_pairs={{0,16},{16,0},{1,17},{17,1},{2,18},{18,2},{3,19},{19,3},{4,20},{20... | collective-permute-start | bytes 1572872 | tf_op jit(solution)/shard_map/ppermute | solution.py:172
  715.3 68.5 %collective-permute-start.81 = (bf16[1536,128]{1,0:T(8,128)(2,1)}, bf16[1536,128]{1,0:T(8,128)(2,1)}, u32[]{:S(2)}, u32[]{:S(2)}) collective-permute-start(bf16[1536,128]{1,0:T(8,128)(2,1)} %fusion.120), channel_id=1, source_target_pairs={{0,1},{1,0},{2,3},{3,2},{4,5},{5,4},{6,7},{7,6},{8,9},{9,8},{10,11... | collective-permute-start | bytes 1179656 | tf_op jit(solution)/shard_map/ppermute | solution.py:172
  923.8 36.6 %collective-permute-start.97 = (bf16[192,1024]{1,0:T(8,128)(2,1)}, bf16[192,1024]{1,0:T(8,128)(2,1)}, u32[]{:S(2)}, u32[]{:S(2)}) collective-permute-start(bf16[192,1024]{1,0:T(8,128)(2,1)} %bitcast.633), channel_id=1, source_target_pairs={{0,16},{16,0},{1,17},{17,1},{2,18},{18,2},{3,19},{19,3},{4,20},{20... | collective-permute-start | bytes 1179656 | tf_op jit(solution)/shard_map/ppermute | solution.py:172
  (288 other events, 3214.2 us)
Sparse Core Ops, SparseCore 0:
  9.6 40.2 all-gather.14
  52.0 88.5 all-gather.10
  142.2 44.4 all-gather.16
  188.7 79.4 all-gather.12
  575.6 50.3 reduce-scatter.13
  628.8 25.2 reduce-scatter.7
  657.1 33.5 reduce-scatter.9
  693.0 75.7 reduce-scatter.11
  835.0 84.3 reduce-scatter.5

commit v2 on v1

v2 whole, which is shorter than its diff:
```python
import math

import jax
import jax.numpy as jnp
from jax import lax
from jax.experimental import pallas as pl
from jax.experimental.pallas import tpu as pltpu
from jax.sharding import Mesh
from jax.sharding import PartitionSpec as P

HQ = 8
KVH = 2
HD = 128
MH = 48
MP = 64
NST = 256
EPSILON = 1e-05
ROPE_BASE = 100000000000.0
MASKED = -1e30
BF = jnp.bfloat16
F32 = jnp.float32
MESH_AXES = ("x", "z", "y", "c")
FSDP = ("z", "y", "c")
PARTS = 8
VMEM = 48 * 1024 * 1024


def mm(left, right):
    return jnp.dot(left, right, preferred_element_type=F32)


def outer_product(left, right):
    return lax.dot_general(left, right, (((0,), (0,)), ((), ())), preferred_element_type=F32)


def across(left, right):
    return lax.dot_general(left, right, (((1,), (1,)), ((), ())), preferred_element_type=F32)


def rope_tables(length, head_size):
    half_size = head_size // 2
    frequency = jnp.exp(
        jnp.arange(half_size, dtype=F32) * (-2.0 * math.log(ROPE_BASE) / head_size)
    )
    angles = jnp.arange(length, dtype=F32)[:, None] * frequency[None, :]
    cosine, sine = jnp.cos(angles), jnp.sin(angles)
    return [jnp.concatenate(v, axis=1) for v in ([cosine, cosine], [-sine, sine])]


def silu_parts(values):
    sig = 1.0 / (1.0 + jnp.exp(-values))
    return values * sig, sig


def shifted(values, count):
    if count == 0:
        return values
    rows = values.shape[0]
    at = lax.broadcasted_iota(jnp.int32, values.shape, 0)
    kept = (at >= count) if count > 0 else (at < rows + count)
    return jnp.where(kept, pltpu.roll(values, count % rows, 0), 0.0)


def conv_silu(signal, kernel, bias):
    taps = kernel.shape[0]
    total = bias + signal * kernel[taps - 1 : taps]
    for back in range(1, taps):
        total = total + shifted(signal, back) * kernel[taps - 1 - back : taps - back]
    value, sig = silu_parts(total)
    return value, sig * (1.0 + total * (1.0 - sig))


def conv_grads(signal, kernel, grad):
    taps = kernel.shape[0]
    back = grad * kernel[taps - 1 : taps]
    rows = []
    for count in range(taps - 1, 0, -1):
        rows.append(jnp.sum(shifted(signal, count) * grad, axis=0, keepdims=True))
        back = back + shifted(grad, -count) * kernel[taps - 1 - count : taps - count]
    rows.append(jnp.sum(signal * grad, axis=0, keepdims=True))
    return back, jnp.concatenate(rows, axis=0), jnp.sum(grad, axis=0, keepdims=True)


def dot(left, right, dims=((1,), (0,)), precision=None):
    return lax.dot_general(
        left, right, (dims, ((), ())), preferred_element_type=F32, precision=precision
    )


ROWS = ((0,), (0,))
LANES = ((1,), (1,))
PRECISE = lax.Precision.HIGHEST


def step_place():
    return (MH // PARTS) * (2 * lax.axis_index("c") + lax.axis_index("y"))


def scan_parts(x_ref, m_ref, s_ref, xk_ref, xb_ref, mk_ref, mb_ref, h_ref):
    length = x_ref.shape[0]
    xin, maps = x_ref[...].astype(BF).astype(F32), m_ref[...].astype(F32)
    xs, xslope = conv_silu(xin, xk_ref[...], xb_ref[...])
    mv, mslope = conv_silu(maps, mk_ref[...], mb_ref[...])
    mv = mv.astype(BF)
    bees, cees = mv[:, :NST], mv[:, NST:]
    raw = pltpu.roll(s_ref[...].astype(F32), 2 * MP - step_place(), 1) + h_ref[1:2]
    dt = jnp.maximum(raw, 0.0) + jnp.log1p(jnp.exp(-jnp.abs(raw)))
    rate = -jnp.exp(h_ref[0:1])
    t = lax.broadcasted_iota(jnp.int32, (length, length), 0)
    s = lax.broadcasted_iota(jnp.int32, (length, length), 1)
    lower = (t >= s).astype(F32)
    cum = dot(lower, dt * rate, precision=PRECISE)
    coupling = dot(cees, bees, LANES)
    return xin, maps, xs, xslope, mslope, bees, cees, raw, dt, rate, lower, cum, coupling


def lane_pair(values, first):
    lane = lax.broadcasted_iota(jnp.int32, (values.shape[0], 2 * MP), 1)
    return jnp.where(lane < MP, values[:, first : first + 1], values[:, first + 1 : first + 2])


def decay_of(cum, cumt, lower, head):
    gap = cum[:, head : head + 1] - cumt[head : head + 1, :]
    return jnp.exp(jnp.where(lower > 0.0, gap, MASKED))


def rotated(ref, cos_ref, sin_ref):
    value = ref[...].astype(BF).astype(F32)
    return (value * cos_ref[...] + pltpu.roll(value, HD // 2, 1) * sin_ref[...]).astype(BF)


def causal_scores(rq, rk):
    length = rq.shape[0]
    t = lax.broadcasted_iota(jnp.int32, (length, length), 0)
    s = lax.broadcasted_iota(jnp.int32, (length, length), 1)
    scores = jnp.where(t >= s, dot(rq, rk, LANES) * HD ** (-0.5), MASKED)
    highest = jnp.max(scores, axis=1, keepdims=True)
    weights = jnp.exp(scores - highest)
    return weights, jnp.sum(weights, axis=1, keepdims=True)


def mixer_kernel(
    x_ref, m_ref, s_ref, z_ref, q_ref, k_ref, v_ref, xk_ref, xb_ref, mk_ref, mb_ref, h_ref,
    cos_ref, sin_ref, scan_ref, gated_ref, square_ref, att_ref,
):
    xin, maps, xs, xslope, mslope, bees, cees, raw, dt, rate, lower, cum, coupling = scan_parts(
        x_ref, m_ref, s_ref, xk_ref, xb_ref, mk_ref, mb_ref, h_ref
    )
    cumt = cum.T
    lane = lax.broadcasted_iota(jnp.int32, (xs.shape[0], 2 * MP), 1)
    squares = jnp.zeros((xs.shape[0], 1), F32)
    for pair in range(xs.shape[1] // (2 * MP)):
        cols = slice(2 * MP * pair, 2 * MP * (pair + 1))
        xp = xs[:, cols]
        xr = (xp * lane_pair(dt, 2 * pair)).astype(BF)
        ys = []
        for head in (2 * pair, 2 * pair + 1):
            mixing = (coupling * decay_of(cum, cumt, lower, head)).astype(BF)
            ys.append(dot(mixing, xr))
        y = jnp.where(lane < MP, ys[0], ys[1]) + lane_pair(h_ref[2:3], 2 * pair) * xp
        y = y.astype(BF)
        scan_ref[:, cols] = y
        gated = y.astype(F32) * silu_parts(z_ref[:, cols])[0]
        gated_ref[:, cols] = gated
        squares = squares + jnp.sum(gated * gated, axis=1, keepdims=True)
    square_ref[...] = squares
    weights, total = causal_scores(
        rotated(q_ref, cos_ref, sin_ref), rotated(k_ref, cos_ref, sin_ref)
    )
    att_ref[...] = dot((weights / total).astype(BF), v_ref[...]).astype(BF)


def mixer_back_kernel(
    x_ref, m_ref, s_ref, z_ref, q_ref, k_ref, v_ref, xk_ref, xb_ref, mk_ref, mb_ref, h_ref,
    cos_ref, sin_ref, scan_ref, gn_ref, gain_ref, factor_ref, dots_ref, ga_ref,
    gin_ref, gcom_ref,
    gxk_ref, gxb_ref, gmk_ref, gmb_ref, gh_ref,
):
    xin, maps, xs, xslope, mslope, bees, cees, raw, dt, rate, lower, cum, coupling = scan_parts(
        x_ref, m_ref, s_ref, xk_ref, xb_ref, mk_ref, mb_ref, h_ref
    )
    length, width = xs.shape
    cumt = cum.T
    lane = lax.broadcasted_iota(jnp.int32, (length, 2 * MP), 1)
    factor, dots = factor_ref[...], dots_ref[...]
    gcoup = jnp.zeros((length, length), F32)
    gcum = jnp.zeros((length, 2 * MP), F32)
    gdt = jnp.zeros((length, 2 * MP), F32)
    gskip = jnp.zeros((1, 2 * MP), F32)
    gus = []
    for pair in range(width // (2 * MP)):
        cols = slice(2 * MP * pair, 2 * MP * (pair + 1))
        gate, scanned = z_ref[:, cols], scan_ref[:, cols].astype(F32)
        silu_z, sig_z = silu_parts(gate)
        normal = scanned * silu_z * factor
        ggated = factor * (gn_ref[:, cols] * gain_ref[:, cols] - normal * dots)
        gin_ref[:, cols] = (ggated * scanned * sig_z * (1.0 + gate * (1.0 - sig_z))).astype(BF)
        gy = (ggated * silu_z).astype(BF)
        gyf = gy.astype(F32)
        xp, dtp = xs[:, cols], lane_pair(dt, 2 * pair)
        xr = (xp * dtp).astype(BF)
        ys, gxrs = [], []
        for own, head in enumerate((2 * pair, 2 * pair + 1)):
            mine = (lane < MP) if own == 0 else (lane >= MP)
            decay = decay_of(cum, cumt, lower, head)
            mixing = (coupling * decay).astype(BF)
            ys.append(dot(mixing, xr))
            gxrs.append(dot(mixing, gy, ROWS))
            gcoup = gcoup + dot(jnp.where(mine, gy, jnp.zeros_like(gy)), xr, LANES) * decay
        y = jnp.where(lane < MP, ys[0], ys[1])
        gxr = jnp.where(lane < MP, gxrs[0], gxrs[1])
        flow, drive, direct = gyf * y - xr.astype(F32) * gxr, gxr * xp, gyf * xp
        for own, head in enumerate((2 * pair, 2 * pair + 1)):
            mine = (lane < MP) if own == 0 else (lane >= MP)

            def share(v):
                return jnp.sum(jnp.where(mine, v, 0.0), axis=1, keepdims=True)

            gcum = jnp.where(lane == head, share(flow), gcum)
            gdt = jnp.where(lane == head, share(drive), gdt)
            gskip = jnp.where(
                lane[:1] == head, jnp.sum(share(direct), axis=0, keepdims=True), gskip
            )
        gus.append((gxr * dtp + lane_pair(h_ref[2:3], 2 * pair) * gyf) * xslope[:, cols])
    gu = jnp.concatenate(gus, axis=1)
    gx, gxk, gxb = conv_grads(xin, xk_ref[...], gu)
    gin_ref[:, width : 2 * width] = gx.astype(BF)
    gflow = dot(lower, gcum, ROWS, precision=PRECISE)
    gdt = gdt + gflow * rate
    graw = gdt / (1.0 + jnp.exp(-raw))
    graw = jnp.where(lane < width // MP, graw, 0.0)
    gcom_ref[:, 2 * NST + 2 * HD :] = pltpu.roll(graw, step_place(), 1).astype(BF)
    gdecay = jnp.sum(gflow * dt, axis=0, keepdims=True) * rate
    gcb = gcoup.astype(BF)
    gmaps = jnp.concatenate([dot(gcb, cees, ROWS), dot(gcb, bees)], axis=1) * mslope
    gm, gmk, gmb = conv_grads(maps, mk_ref[...], gmaps)
    gcom_ref[:, : 2 * NST] = gm.astype(BF)
    gh = jnp.concatenate([gdecay, jnp.sum(graw, axis=0, keepdims=True), gskip], axis=0)

    @pl.when(pl.program_id(0) == 0)
    def _():
        for ref in (gxk_ref, gxb_ref, gmk_ref, gmb_ref, gh_ref):
            ref[...] = jnp.zeros_like(ref)

    gxk_ref[...] += gxk
    gxb_ref[...] += gxb
    gmk_ref[...] += gmk
    gmb_ref[...] += gmb
    gh_ref[0:3] += gh

    rq, rk = rotated(q_ref, cos_ref, sin_ref), rotated(k_ref, cos_ref, sin_ref)
    weights, total = causal_scores(rq, rk)
    probs = weights / total
    gatt = ga_ref[...]
    gcom_ref[:, 2 * NST + HD : 2 * NST + 2 * HD] = dot(probs.astype(BF), gatt, ROWS).astype(BF)
    gp = dot(gatt, v_ref[...], LANES)
    gsc = (probs * (gp - jnp.sum(probs * gp, axis=1, keepdims=True))).astype(BF)
    places = ((gin_ref, 2 * width), (gcom_ref, 2 * NST))
    for (ref, at), grad in zip(places, (dot(gsc, rk), dot(gsc, rq, ROWS))):
        grad = grad * HD ** (-0.5)
        back = grad * cos_ref[...] - pltpu.roll(grad, HD // 2, 1) * sin_ref[...]
        ref[:, at : at + HD] = back.astype(BF)


def column_block(length, width, at):
    return pl.BlockSpec((length, width), lambda i: (i, at // width))


def mixer_specs(length, wide):
    return [
        column_block(length, wide, wide),
        column_block(length, 2 * NST, 0),
        column_block(length, 2 * MP, 2 * NST + 2 * HD),
        column_block(length, wide, 0),
        column_block(length, HD, 2 * wide),
        column_block(length, HD, 2 * NST),
        column_block(length, HD, 2 * NST + HD),
    ]


def whole_specs(arrays):
    return [pl.BlockSpec(a.shape, lambda i: (0, 0)) for a in arrays]


def mixer_forward(seqs, length, projected, common, params, tables):
    wide = params[0].shape[1]
    outs = [(wide, BF), (wide, F32), (1, F32), (HD, BF)]
    return pl.pallas_call(
        mixer_kernel,
        grid=(seqs,),
        in_specs=mixer_specs(length, wide) + whole_specs(params + tables),
        out_specs=[column_block(length, w, 0) for w, _ in outs],
        out_shape=[jax.ShapeDtypeStruct((seqs * length, w), d) for w, d in outs],
        compiler_params=pltpu.CompilerParams(vmem_limit_bytes=VMEM),
        name="mixer",
    )(projected, common, common, projected, projected, common, common, *params, *tables)


def mixer_backward(seqs, length, projected, common, params, tables, scanned, grad_normed, gain, factor, dots, grad_att):
    wide = params[0].shape[1]
    outs = [2 * wide + HD, 2 * NST + 2 * HD + 2 * MP]
    sums = [(4, wide), (1, wide), (4, 2 * NST), (1, 2 * NST), (8, 2 * MP)]
    rows = [scanned, grad_normed]
    tail = [factor, dots, grad_att]
    return pl.pallas_call(
        mixer_back_kernel,
        grid=(seqs,),
        in_specs=mixer_specs(length, wide) + whole_specs(params + tables)
        + [column_block(length, a.shape[1], 0) for a in rows] + whole_specs([gain])
        + [column_block(length, a.shape[1], 0) for a in tail],
        out_specs=[column_block(length, w, 0) for w in outs]
        + [pl.BlockSpec(s, lambda i: (0, 0)) for s in sums],
        out_shape=[jax.ShapeDtypeStruct((seqs * length, w), BF) for w in outs]
        + [jax.ShapeDtypeStruct(s, F32) for s in sums],
        compiler_params=pltpu.CompilerParams(vmem_limit_bytes=VMEM),
        name="mixer_back",
    )(
        projected, common, common, projected, projected, common, common,
        *params, *tables, *rows, gain, *tail,
    )


def remote(src, dst, send, recv, axis):
    other = 1 - lax.axis_index(axis)
    return pltpu.make_async_remote_copy(
        src_ref=src,
        dst_ref=dst,
        send_sem=send,
        recv_sem=recv,
        device_id={axis: other},
        device_id_type=pl.DeviceIdType.MESH,
    )


def greet(axes):
    barrier = pltpu.get_barrier_semaphore()
    for axis in axes:
        other = 1 - lax.axis_index(axis)
        pl.semaphore_signal(
            barrier, inc=1, device_id={axis: other}, device_id_type=pl.DeviceIdType.MESH
        )
    pl.semaphore_wait(barrier, len(axes))


def line_item(region, sems, sources=None):
    z, n = lax.axis_index("z"), lax.axis_size("z")

    def copy(way, k, at, src):
        return pltpu.make_async_remote_copy(
            src_ref=src,
            dst_ref=region(at),
            send_sem=sems.at[0, way, k],
            recv_sem=sems.at[1, way, k],
            device_id={"z": z + 1 - 2 * way},
            device_id_type=pl.DeviceIdType.MESH,
        )

    def send(k):
        src = sources if k == 0 and sources is not None else None

        @pl.when((z + 1 < n) & (z - k >= 0))
        def _():
            copy(0, k, z - k, region(z - k) if src is None else src).start()

        @pl.when((z >= 1) & (z + k < n))
        def _():
            copy(1, k, z + k, region(z + k) if src is None else src).start()

    def arrive(k):
        @pl.when(z - 1 - k >= 0)
        def _():
            copy(0, k, z - 1 - k, region(z - 1 - k)).wait_recv()

        @pl.when(z + 1 + k < n)
        def _():
            copy(1, k, z + 1 + k, region(z + 1 + k)).wait_recv()

    def finish():
        for k in range(n - 1):
            src = sources if k == 0 and sources is not None else None

            @pl.when((z + 1 < n) & (z - k >= 0))
            def _(k=k, src=src):
                copy(0, k, z - k, region(z - k) if src is None else src).wait_send()

            @pl.when((z >= 1) & (z + k < n))
            def _(k=k, src=src):
                copy(1, k, z + k, region(z + k) if src is None else src).wait_send()

    return send, arrive, finish


def gather_regions(region, half, sems, own_ready, own=None):
    x, y, c = (lax.axis_index(a) for a in ("x", "y", "c"))
    sent = []

    def send(i, ref, axis, src=None):
        src = ref if src is None else src
        copy = remote(src, ref, sems.at[0, i], sems.at[1, i], axis)
        copy.start()
        sent.append(copy)

    def got(i, ref, axis):
        remote(ref, ref, sems.at[0, i], sems.at[1, i], axis).wait_recv()

    def begin():
        if own is None:
            own_ready()
        for i, axis in enumerate(("x", "y", "c")):
            send(i, region(x, y, c), axis, own)

    def forward():
        got(0, region(1 - x, y, c), "x")
        send(3, half(region(1 - x, y, c), 0), "y")
        send(4, region(1 - x, y, c), "c")
        got(1, region(x, 1 - y, c), "y")
        send(5, half(region(x, 1 - y, c), 1), "x")
        send(6, region(x, 1 - y, c), "c")

    def end():
        got(3, half(region(1 - x, 1 - y, c), 0), "y")
        got(5, half(region(1 - x, 1 - y, c), 1), "x")
        send(7, region(1 - x, 1 - y, c), "c")
        got(2, region(x, y, 1 - c), "c")
        got(4, region(1 - x, y, 1 - c), "c")
        got(6, region(x, 1 - y, 1 - c), "c")
        got(7, region(1 - x, 1 - y, 1 - c), "c")
        for copy in sent:
            copy.wait_send()
        if own is not None:
            own_ready()

    return begin, forward, end


def greet_all():
    barrier = pltpu.get_barrier_semaphore()
    x, z, y, c = (lax.axis_index(a) for a in ("x", "z", "y", "c"))
    n = lax.axis_size("z")

    def tell(where):
        pl.semaphore_signal(
            barrier, inc=1, device_id=where, device_id_type=pl.DeviceIdType.MESH
        )

    for where in ({"x": 1 - x}, {"y": 1 - y}, {"c": 1 - c}, {"y": 1 - y, "c": 1 - c}):
        tell(where)

    @pl.when(z >= 1)
    def _():
        tell({"z": z - 1})

    @pl.when(z + 1 < n)
    def _():
        tell({"z": z + 1})

    pl.semaphore_wait(barrier, 4 + jnp.minimum(z, 1) + jnp.minimum(n - 1 - z, 1))


def sum_scratch(count, width):
    half = width // 2
    return [
        pltpu.VMEM((2, 2, 2, count, half), BF),
        pltpu.VMEM((2, 2, count, half), BF),
        pltpu.VMEM((2, 2, count, half), BF),
        pltpu.VMEM((2, count, half), BF),
        pltpu.VMEM((2, count, half), BF),
        pltpu.SemaphoreType.DMA((2, 6)),
    ]


def reduce_plane(part, scratch):
    core, wide_in, wide_out, thin_in, thin_out, sems = scratch
    half = part.shape[4] // 2
    x, y, c = (lax.axis_index(a) for a in ("x", "y", "c"))
    firsts, seconds = ("y", "x"), ("x", "y")
    cols = [slice(0, half), slice(half, 2 * half)]

    def chip(i, yy, xx):
        return part[yy, c, xx, :, cols[i]].astype(F32) + core[i, yy, xx].astype(F32)

    def kept(i, index):
        mine = chip(i, y, index) if i == 0 else chip(i, index, x)
        return mine + wide_in[i, index].astype(F32)

    copies = [
        remote(part.at[:, 1 - c, :, :, cols[i]], core.at[i], sems.at[0, i], sems.at[1, i], "c")
        for i in (0, 1)
    ]
    wides = [
        remote(wide_out.at[i], wide_in.at[i], sems.at[0, 2 + i], sems.at[1, 2 + i], firsts[i])
        for i in (0, 1)
    ]
    thins = [
        remote(thin_out.at[i], thin_in.at[i], sems.at[0, 4 + i], sems.at[1, 4 + i], seconds[i])
        for i in (0, 1)
    ]

    def begin():
        for copy in copies:
            copy.start()

    def wide():
        for i in (0, 1):
            copies[i].wait()
            for k in (0, 1):
                wide_out[i, k] = (chip(i, 1 - y, k) if i == 0 else chip(i, k, 1 - x)).astype(BF)
            wides[i].start()

    def thin():
        for i in (0, 1):
            wides[i].wait()
            thin_out[i] = kept(i, 1 - x if i == 0 else 1 - y).astype(BF)
            thins[i].start()

    def end():
        outs = []
        for i in (0, 1):
            thins[i].wait()
            outs.append(kept(i, x if i == 0 else y) + thin_in[i].astype(F32))
        return jnp.concatenate(outs, axis=1)

    return begin, wide, thin, end


def gathered(block, out, sems, local):
    x, y, c = (lax.axis_index(a) for a in ("x", "y", "c"))
    half = block.shape[0] // 2
    own = pltpu.make_async_copy(block, out.at[y, c, x], local)
    own.start()
    steps = gather_regions(
        lambda x, y, c: out.at[y, c, x],
        lambda ref, i: ref.at[pl.ds(i * half, half)],
        sems,
        own.wait,
        block,
    )
    return steps


def factor_of(values):
    return lax.rsqrt(jnp.mean(values * values, axis=1, keepdims=True) + EPSILON)


def norm_back_parts(values, scaling, grad):
    factor = factor_of(values)
    normal = values * factor
    scaled = grad * scaling
    inner = jnp.mean(scaled * normal, axis=1, keepdims=True)
    return factor * (scaled - normal * inner), jnp.sum(grad * normal, axis=0, keepdims=True)


def middle_kernel(
    part_ref, rows_ref, gain_ref, down_ref, out_ref, middle_ref, whole_ref,
    block, sems, local, down_sems, *scratch,
):
    z, n = lax.axis_index("z"), lax.axis_size("z")
    greet_all()
    begin, wide, thin, end = reduce_plane(part_ref, scratch)
    begin()
    own = pltpu.make_async_copy(down_ref, whole_ref.at[z], local.at[1])
    own.start()
    send, arrive, finish = line_item(lambda at: whole_ref.at[at], down_sems, down_ref)
    send(0)

    def more(k):
        if k < n:
            arrive(k - 1)
        if k < n - 1:
            send(k)

    wide()
    more(1)
    thin()
    middle = rows_ref[...].astype(F32) + end()
    middle_ref[...] = middle
    block[...] = (middle * factor_of(middle) * gain_ref[...]).astype(BF)
    first, *steps = gathered(block, out_ref, sems, local.at[0])
    first()
    more(2)
    for step in steps:
        step()
    for k in range(3, n):
        more(k)
    own.wait()
    finish()


def middle_back_kernel(
    part_ref, rows_ref, gain_ref, cot_ref, out_ref, grad_ref, gain_grad_ref,
    block, sems, local, *scratch,
):
    greet(("x", "y", "c"))
    begin, wide, thin, end = reduce_plane(part_ref, scratch)
    begin()
    wide()
    thin()
    grad, gain_grad_ref[...] = norm_back_parts(rows_ref[...], gain_ref[...], end())
    grad = grad + cot_ref[...].astype(F32)
    grad_ref[...] = grad
    block[...] = grad.astype(BF)
    for step in gathered(block, out_ref, sems, local.at[0]):
        step()


def middle_calls(part, rows, gain, down=None, cot=None):
    n = lax.axis_size("z")
    count, width = rows.shape
    vmem, hbm = pl.BlockSpec(memory_space=pltpu.VMEM), pl.BlockSpec(memory_space=pl.ANY)
    dma = pltpu.SemaphoreType.DMA
    out = [jax.ShapeDtypeStruct((2, 2, 2, count, width), BF), jax.ShapeDtypeStruct((count, width), F32)]
    scratch = [pltpu.VMEM((count, width), BF), dma((2, 8)), dma((2,))]
    if cot is None:
        inputs, specs = [part, rows, gain, down], [vmem] * 3 + [hbm]
        out += [jax.ShapeDtypeStruct((n,) + down.shape, BF)]
        out_specs = [hbm, vmem, hbm]
        scratch += [dma((2, 2, n))]
    else:
        inputs, specs = [part, rows, gain, cot], [vmem] * 4
        out += [jax.ShapeDtypeStruct((1, width), F32)]
        out_specs = [hbm, vmem, vmem]
    return pl.pallas_call(
        middle_kernel if cot is None else middle_back_kernel,
        in_specs=specs,
        out_specs=out_specs,
        out_shape=out,
        scratch_shapes=scratch + sum_scratch(count, width),
        compiler_params=pltpu.CompilerParams(
            collective_id=1 if cot is None else 2, has_side_effects=True, vmem_limit_bytes=VMEM
        ),
        name="middle" if cot is None else "middle_back",
    )(*inputs)


def total_kernel(value_ref, out_ref, got, sems):
    greet(("c", "y", "x"))
    out_ref[...] = value_ref[...]
    for i, axis in enumerate(("c", "y", "x")):
        hop = remote(out_ref, got.at[i], sems.at[0, i], sems.at[1, i], axis)
        hop.start()
        hop.wait()
        out_ref[...] = out_ref[...] + got[i]


def plane_total(value, identity):
    vmem = pl.BlockSpec(memory_space=pltpu.VMEM)
    return pl.pallas_call(
        total_kernel,
        in_specs=[vmem],
        out_specs=vmem,
        out_shape=jax.ShapeDtypeStruct(value.shape, F32),
        scratch_shapes=[pltpu.VMEM((3,) + value.shape, F32), pltpu.SemaphoreType.DMA((2, 3))],
        compiler_params=pltpu.CompilerParams(collective_id=identity, has_side_effects=True),
        name="total",
    )(value)


def line_sum(own, inbox, sems):
    z, n = lax.axis_index("z"), lax.axis_size("z")

    def copy(way, k):
        d = k if way else n - 1 - k
        slot = jnp.where(d == z - 1, n, d) if way else d
        return pltpu.make_async_remote_copy(
            src_ref=own(d),
            dst_ref=inbox(slot),
            send_sem=sems.at[0, way, k],
            recv_sem=sems.at[1, way, k],
            device_id={"z": z + 1 - 2 * way},
            device_id_type=pl.DeviceIdType.MESH,
        )

    def add(way, k, d, slot):
        pltpu.make_async_remote_copy(
            src_ref=own(d),
            dst_ref=inbox(slot),
            send_sem=sems.at[0, way, k],
            recv_sem=sems.at[1, way, k],
            device_id={"z": z},
            device_id_type=pl.DeviceIdType.MESH,
        ).wait_recv()
        held = own(d)
        held[...] = (held[...].astype(F32) + inbox(slot)[...].astype(F32)).astype(held.dtype)

    def kick(k):
        @pl.when(z == 0)
        def _():
            copy(0, k).start()

        @pl.when(z == n - 1)
        def _():
            copy(1, k).start()

    def pass_on(way, k):
        d = k if way else n - 1 - k

        @pl.when((z > 0) & (z < n - 1) & (d < z if way else d > z))
        def _():
            add(way, k, d, d)
            copy(way, k).start()

    def end():
        @pl.when(z > 0)
        def _():
            add(0, n - 1 - z, z, z)

        @pl.when(z < n - 1)
        def _():
            add(1, z, z, n)

    def finish():
        for k in range(n - 1):
            for way in (0, 1):
                d = k if way else n - 1 - k

                @pl.when(d < z if way else d > z)
                def _(way=way):
                    copy(way, k).wait_send()

    return kick, pass_on, end, finish


def last_kernel(
    part_ref, rows_ref, gain_ref, grad_ref, little_ref, down_ref, middle_ref, weight_ref, slice_ref, cross_ref,
    out_ref, little_out, result_ref, got_ref, crossed_ref,
    held, inbox, swap, little, little_in, little_c, little_y, little_box,
    local, weight_sems, little_sems, hop_sems, swap_sems, got_sems, own_sems, cross_sems, *scratch,
):
    x, z, y, c = (lax.axis_index(a) for a in ("x", "z", "y", "c"))
    n = lax.axis_size("z")
    greet_all()
    cut = weight_ref.shape[4]
    loads = []
    for i, (ref, at) in enumerate(((weight_ref, 0), (slice_ref, cut))):
        into = held.at[:, :, :, :, pl.ds(at, ref.shape[4])]
        loads.append(pltpu.make_async_copy(ref, into, local.at[i]))
        loads[i].start()
    half = len(scratch) // 2
    begin, wide, thin, end = reduce_plane(part_ref, scratch[:half])
    begin_down, wide_down, thin_down, end_down = reduce_plane(down_ref, scratch[half:])
    begin()
    begin_down()
    for load in loads:
        load.wait()

    order = ((1, 1), (1, 0), (0, 1), (0, 0))
    sums, places = [], []
    for i, (dy, dc) in enumerate(order):
        yy, cc = (1 - y) if dy else y, (1 - c) if dc else c
        places.append((yy, cc))
        sums.append(
            line_sum(
                lambda d, yy=yy, cc=cc: held.at[d, yy, cc],
                lambda d, yy=yy, cc=cc: inbox.at[d, yy, cc],
                weight_sems.at[i],
            )
        )
    for k in range(n - 1):
        for item in sums:
            item[0](k)
    wide()
    wide_down()

    def pass_all(k):
        for item in sums:
            for near in (0, 1):

                @pl.when(z < n // 2)
                def _():
                    item[1](near, k)

                @pl.when(z >= n // 2)
                def _():
                    item[1](1 - near, k)

    pass_all(0)
    thin()
    thin_down()
    cross = remote(cross_ref, crossed_ref, cross_sems.at[0], cross_sems.at[1], "x")
    cross.start()
    for k in range(1, n - 1):
        pass_all(k)

    result_ref[...] = (middle_ref[...] + end_down()).astype(BF)
    rows = rows_ref[...].astype(F32)
    grad, gain_grad = norm_back_parts(rows, gain_ref[...], end())
    out_ref[...] = grad + grad_ref[...]

    little[...] = little_ref[...]
    piece = rows.shape[1] // (4 * n)
    for at in range(n):
        for yy in (0, 1):
            for cc in (0, 1):
                first = (4 * at + 2 * yy + cc) * piece
                little[at, yy, cc, 0:1, 0:piece] = gain_grad[:, first : first + piece]
    hop = remote(little, little_in, hop_sems.at[0, 0], hop_sems.at[1, 0], "x")
    hop.start()
    hop.wait()
    little[...] = little[...] + little_in[...]
    hop = remote(little.at[:, :, 1 - c], little_c, hop_sems.at[0, 1], hop_sems.at[1, 1], "c")
    hop.start()
    hop.wait()
    for yy in (0, 1):
        little_c[:, yy] = little_c[:, yy] + little[:, yy, c]
    hop = remote(little_c.at[:, 1 - y], little_y, hop_sems.at[0, 2], hop_sems.at[1, 2], "y")
    hop.start()
    hop.wait()
    little_y[...] = little_y[...] + little_c[:, y]
    little_sum = line_sum(lambda d: little_y.at[d], lambda d: little_box.at[d], little_sems)
    for k in range(n - 1):
        little_sum[0](k)
    for k in range(n - 1):
        for way in (0, 1):
            little_sum[1](way, k)
    little_sum[2]()
    little_out[...] = little_y[z]

    moves, crossed, kept = [], [], []

    def forward(i):
        yy, cc = places[i]
        if i < 3:
            moves[i].wait_recv()
        keep = pltpu.make_async_copy(swap.at[cc, yy], got_ref.at[x, cc, yy], own_sems.at[i])
        keep.start()
        kept.append(keep)
        move = remote(
            swap.at[cc, yy], got_ref.at[x, cc, yy], got_sems.at[0, i], got_sems.at[1, i], "x"
        )
        move.start()
        crossed.append(move)

    for i, (yy, cc) in enumerate(places):
        sums[i][2]()
        if i < 3:
            move = pltpu.make_async_remote_copy(
                src_ref=held.at[z, yy, cc],
                dst_ref=swap.at[c, y],
                send_sem=swap_sems.at[0, i],
                recv_sem=swap_sems.at[1, i],
                device_id={"y": yy, "c": cc},
                device_id_type=pl.DeviceIdType.MESH,
            )
            move.start()
            moves.append(move)
        else:
            swap[c, y] = held[z, yy, cc]
        if i > 0:
            forward(i - 1)
    forward(3)
    cross.wait()
    for copy in kept + crossed:
        copy.wait()
    for move in moves:
        move.wait_send()
    for item in sums + [little_sum]:
        item[3]()


def last_call(part, rows, gain, grad, little, down, middle, weight, slices, cross):
    n = lax.axis_size("z")
    count, width = rows.shape
    block, pack = (weight.shape[3], weight.shape[4] + slices.shape[4]), little.shape[3:]
    vmem, hbm = pl.BlockSpec(memory_space=pltpu.VMEM), pl.BlockSpec(memory_space=pl.ANY)
    dma = pltpu.SemaphoreType.DMA
    return pl.pallas_call(
        last_kernel,
        in_specs=[vmem] * 7 + [hbm] * 3,
        out_specs=[vmem, vmem, vmem, hbm, hbm],
        out_shape=[
            jax.ShapeDtypeStruct((count, width), F32),
            jax.ShapeDtypeStruct(pack, F32),
            jax.ShapeDtypeStruct((count, width), BF),
            jax.ShapeDtypeStruct((2, 2, 2) + block, BF),
            jax.ShapeDtypeStruct(cross.shape, BF),
        ],
        scratch_shapes=[
            pltpu.VMEM((n, 2, 2) + block, BF),
            pltpu.VMEM((n + 1, 2, 2) + block, BF),
            pltpu.VMEM((2, 2) + block, BF),
            pltpu.VMEM((n, 2, 2) + pack, F32),
            pltpu.VMEM((n, 2, 2) + pack, F32),
            pltpu.VMEM((n, 2) + pack, F32),
            pltpu.VMEM((n,) + pack, F32),
            pltpu.VMEM((n + 1,) + pack, F32),
            dma((2,)),
            dma((4, 2, 2, n)),
            dma((2, 2, n)),
            dma((2, 3)),
            dma((2, 3)),
            dma((2, 4)),
            dma((4,)),
            dma((2,)),
        ]
        + sum_scratch(count, width)
        + sum_scratch(count, width),
        compiler_params=pltpu.CompilerParams(
            collective_id=3, has_side_effects=True, vmem_limit_bytes=60 * 1024 * 1024
        ),
        name="last",
    )(part, rows, gain, grad, little, down, middle, weight, slices, cross)


def start_kernel(
    rows_ref, little_ref, own_ref, blocks_ref, cot_ref,
    hidden_ref, all_ref, shared_ref, weight_ref, incoming_ref,
    block, little, hidden_sems, shared_sems, cot_sems, local, little_sems, line_sems, across_sems,
):
    x, z, y, c = (lax.axis_index(a) for a in ("x", "z", "y", "c"))
    n = lax.axis_size("z")
    greet_all()
    width = own_ref.shape[1]

    def shared_at(x, z, y, c):
        cols = pl.ds(pl.multiple_of(x * width, 128), width)
        return shared_ref.at[z, y, c, :, cols]

    own_shared = pltpu.make_async_copy(own_ref, shared_at(x, z, y, c), local.at[0])
    own_shared.start()
    own_weight = pltpu.make_async_copy(blocks_ref.at[c, y], weight_ref.at[z, y, c], local.at[1])
    own_weight.start()
    own_cot = pltpu.make_async_copy(cot_ref, incoming_ref.at[y, c, x], local.at[3])
    own_cot.start()

    shared_line = line_item(lambda at: shared_at(x, at, y, c), line_sems.at[0], own_ref)
    little_line = line_item(lambda at: little.at[at], line_sems.at[1])
    shared_line[0](0)
    little[z, y, c] = little_ref[...]
    hop = remote(little.at[z, y, c], little.at[z, y, c], little_sems.at[0, 0], little_sems.at[1, 0], "c")
    hop.start()

    moves = []
    for i, (dy, dc) in enumerate(((0, 1), (1, 0), (1, 1))):
        where = {"y": (1 - y) if dy else y, "c": (1 - c) if dc else c}
        src = blocks_ref.at[where["c"], where["y"]]
        move = pltpu.make_async_remote_copy(
            src_ref=src,
            dst_ref=weight_ref.at[z, y, c],
            send_sem=across_sems.at[0, i],
            recv_sem=across_sems.at[1, i],
            device_id=where,
            device_id_type=pl.DeviceIdType.MESH,
        )
        move.start()
        moves.append(move)

    lines = []
    for i, (dy, dc) in enumerate(((0, 0), (0, 1), (1, 0), (1, 1))):
        yy, cc = (1 - y) if dy else y, (1 - c) if dc else c
        lines.append(
            line_item(
                lambda at, yy=yy, cc=cc: weight_ref.at[at, yy, cc],
                line_sems.at[2 + i],
                blocks_ref.at[c, y] if i == 0 else None,
            )
        )
    lines[0][0](0)
    hop.wait()
    second = remote(little.at[z, y], little.at[z, y], little_sems.at[0, 1], little_sems.at[1, 1], "y")
    second.start()
    second.wait()
    little_line[0](0)
    for k in range(1, n):
        shared_line[1](k - 1)
        if k < n - 1:
            shared_line[0](k)
        little_line[1](k - 1)
        if k < n - 1:
            little_line[0](k)
    for i in range(3):
        moves[i].wait_recv()
        lines[1 + i][0](0)

    rows = rows_ref[...].astype(F32)
    rows = rows * factor_of(rows)
    piece = rows.shape[1] // (4 * n)
    gain = jnp.concatenate(
        [
            little[at, yy, cc, 0:1, 0:piece]
            for at in range(n)
            for yy in (0, 1)
            for cc in (0, 1)
        ],
        axis=1,
    )
    block[...] = (rows * gain).astype(BF)
    all_ref[...] = little[...]
    count = rows.shape[0]
    own_hidden = pltpu.make_async_copy(block, hidden_ref.at[y, c, x], local.at[2])
    own_hidden.start()

    hidden_steps = gather_regions(
        lambda x, y, c: hidden_ref.at[y, c, x],
        lambda ref, i: ref.at[pl.ds(i * (count // 2), count // 2)],
        hidden_sems,
        own_hidden.wait,
        block,
    )

    def shared_region(x, y, c):
        cols = pl.ds(pl.multiple_of(x * width, 128), width)
        return shared_ref.at[:, y, c, :, cols]

    shared_steps = gather_regions(
        shared_region,
        lambda ref, i: ref.at[pl.ds(i * (n // 2), n // 2)],
        shared_sems,
        own_shared.wait,
    )
    cot_steps = gather_regions(
        lambda x, y, c: incoming_ref.at[y, c, x],
        lambda ref, i: ref.at[pl.ds(i * (count // 2), count // 2)],
        cot_sems,
        own_cot.wait,
        cot_ref,
    )
    hidden_steps[0]()
    shared_steps[0]()
    cot_steps[0]()
    for k in range(1, n):
        for send, arrive, finish in lines:
            arrive(k - 1)
            if k < n - 1:
                send(k)
        if k == 1:
            hidden_steps[1]()
            shared_steps[1]()
    cot_steps[1]()
    hidden_steps[2]()
    shared_steps[2]()
    cot_steps[2]()
    own_weight.wait()
    for move in moves:
        move.wait_send()
    for send, arrive, finish in [shared_line, little_line] + lines:
        finish()


def start_call(rows, little, own, blocks, cot):
    n, parts = lax.axis_size("z"), blocks.shape
    count, width = rows.shape
    vmem, hbm = pl.BlockSpec(memory_space=pltpu.VMEM), pl.BlockSpec(memory_space=pl.ANY)
    dma = pltpu.SemaphoreType.DMA
    return pl.pallas_call(
        start_kernel,
        in_specs=[vmem, vmem, hbm, hbm, hbm],
        out_specs=[hbm, vmem, hbm, hbm, hbm],
        out_shape=[
            jax.ShapeDtypeStruct((2, 2, 2, count, width), BF),
            jax.ShapeDtypeStruct((n, 2, 2) + little.shape, F32),
            jax.ShapeDtypeStruct((n, 2, 2, own.shape[0], 2 * own.shape[1]), BF),
            jax.ShapeDtypeStruct((n, 2, 2) + parts[2:], BF),
            jax.ShapeDtypeStruct((2, 2, 2, count, width), BF),
        ],
        scratch_shapes=[
            pltpu.VMEM((count, width), BF),
            pltpu.VMEM((n, 2, 2) + little.shape, F32),
            dma((2, 8)),
            dma((2, 8)),
            dma((2, 8)),
            dma((4,)),
            dma((2, 2)),
            dma((6, 2, 2, n - 1)),
            dma((2, 3)),
        ],
        compiler_params=pltpu.CompilerParams(
            collective_id=0, has_side_effects=True, vmem_limit_bytes=VMEM
        ),
        name="start",
    )(rows, little, own, blocks, cot)


def flip(value, *axes):
    count = 2 ** len(axes)
    pairs = [(i, count - 1 - i) for i in range(count)]
    axes = tuple(sorted(axes, key=MESH_AXES.index))
    return lax.ppermute(value, axes, pairs)


def ordered(own, other, axis):
    second = lax.axis_index(axis) == 1
    return jnp.where(second, other, own), jnp.where(second, own, other)


def column_halves(values, axis):
    at = lax.axis_index(axis)
    halves = [v.shape[1] // 2 for v in values]
    kept = [lax.dynamic_slice_in_dim(v, at * h, h, 1) for v, h in zip(values, halves)]
    away = [lax.dynamic_slice_in_dim(v, (1 - at) * h, h, 1) for v, h in zip(values, halves)]
    return kept, jnp.concatenate([v.astype(BF) for v in away], axis=1)


def column_added(kept, got):
    sums, at = [], 0
    for v in kept:
        sums.append(v.astype(F32) + got[:, at : at + v.shape[1]].astype(F32))
        at += v.shape[1]
    return sums


def part_index():
    return 4 * lax.axis_index("x") + 2 * lax.axis_index("c") + lax.axis_index("y")


def half_columns(weight):
    half = weight.shape[1] // 2
    return lax.dynamic_slice_in_dim(weight, lax.axis_index("x") * half, half, 1)


def exchange(blocks, high, low):
    h, l = lax.axis_index(high), lax.axis_index(low)

    def block(dh, dl):
        return lax.dynamic_index_in_dim(blocks, 2 * (h ^ dh) + (l ^ dl), 0, keepdims=False)

    own, by_low = block(0, 0), flip(block(0, 1), low)
    by_high, by_both = flip(block(1, 0), high), flip(block(1, 1), high, low)
    near, far = ordered(own, by_low, low), ordered(by_high, by_both, low)
    first, second = ordered(near[0], far[0], high), ordered(near[1], far[1], high)
    return [[first[0], second[0]], [first[1], second[1]]]


def fetch_units(weights):
    rows, n = weights[0].shape[0], lax.axis_size("z")
    blocks = []
    for w in weights:
        units = w.reshape(rows, n, 2, 2, 2, -1)
        units = lax.dynamic_index_in_dim(units, lax.axis_index("x"), 4, keepdims=False)
        blocks.append(units.transpose(3, 2, 0, 1, 4).reshape(4, rows, -1))
    got = exchange(jnp.concatenate(blocks, axis=2), "c", "y")
    moved = jnp.concatenate([got[0][0], got[1][0], got[0][1], got[1][1]])
    return lax.all_gather(moved, "z", axis=0, tiled=True)


def exchange_units(part):
    rows = part.shape[0] // 4
    part = part.reshape(2, 2, rows, -1).transpose(1, 0, 2, 3).reshape(4, rows, -1)
    return jnp.stack([jnp.stack(g) for g in exchange(part, "c", "y")])


def unit_shards(own, across, count):
    n, rows = lax.axis_size("z"), own.shape[2]
    whole = jnp.stack(ordered(own, across, "x"))
    whole = whole.reshape(2, 2, 2, rows, count, n, -1).transpose(4, 3, 5, 2, 1, 0, 6)
    return [whole[i].reshape(rows, -1).astype(F32) for i in range(count)]


def fetch_rows(weight):
    if lax.axis_size("z") != 4:
        whole = lax.all_gather(weight, FSDP, axis=0, tiled=True)
        rows = whole.shape[0] // PARTS
        return lax.dynamic_slice_in_dim(whole, part_index() * rows, rows, 0)
    got = exchange(lax.all_gather(half_columns(weight), "z", axis=0, tiled=False), "x", "c")
    return jnp.concatenate(
        [jnp.concatenate([got[0][c], got[1][c]], axis=1) for c in (0, 1)], axis=0
    )


def fetch_rows_of(weights):
    if lax.axis_size("z") != 4:
        return jnp.concatenate([fetch_rows(w) for w in weights])
    pieces = [w.shape[0] for w in weights]
    whole, outs, at = fetch_rows(jnp.concatenate(weights)), [], 0
    whole = whole.reshape(2, sum(pieces), -1)
    for count in pieces:
        outs.append(whole[:, at : at + count].reshape(2 * count, -1))
        at += count
    return jnp.concatenate(outs)


def rows_moved(grad, pieces):
    cols = grad.shape[1] // 2
    splits = [grad[sum(pieces[:i]) : sum(pieces[: i + 1])].astype(BF) for i in range(len(pieces))]
    if lax.axis_size("z") != 4:
        parts = []
        for g in splits:
            whole = jnp.zeros((g.shape[0] * PARTS, 2 * cols), BF)
            parts.append(
                lax.dynamic_update_slice_in_dim(whole, g, part_index() * g.shape[0], 0)
            )
        return parts
    halves = jnp.concatenate([g.reshape(2, g.shape[0] // 2, -1) for g in splits], axis=1)
    block = halves.reshape(2, -1, 2, cols).transpose(2, 0, 1, 3)
    got = exchange(block.reshape(4, -1, cols), "x", "c")
    return jnp.stack([got[0][0], got[0][1], got[1][0], got[1][1]])


def rows_sum(moved, down):
    n, width = lax.axis_size("z"), down.shape[1] // 2
    down = down.reshape(n, -1, 2, width).transpose(0, 2, 1, 3).reshape(n, -1, width)
    if n != 4:
        parts = []
        for whole in moved:
            part = lax.psum_scatter(whole, FSDP, scatter_dimension=0, tiled=True)
            parts.append(half_columns(lax.psum(part, "x")))
        return jnp.concatenate(parts + [lax.psum_scatter(down, "z")])
    return lax.psum_scatter(jnp.concatenate([moved, down], axis=1), "z")


def after(value, earlier):
    return lax.optimization_barrier((value, earlier))[0]


def packed(first, arrays):
    lead = first.shape[0]
    flat = jnp.concatenate([a.reshape(lead, -1) for a in arrays], axis=1)
    flat = jnp.pad(flat, ((0, 0), (0, -(flat.shape[1] + 128) % 1024)))
    first = jnp.pad(first, ((0, 0), (0, 128 - first.shape[1])))
    return jnp.concatenate([first, flat], axis=1).reshape(lead, -1, 128)


def shards(
    tokens,
    cotangent,
    mixer_gain,
    query_weight,
    key_weight,
    value_weight,
    attn_out_weight,
    mamba_in_weight,
    conv_weight,
    conv_bias,
    decay_log,
    step_bias,
    skip_gain,
    mamba_gain,
    mamba_out_weight,
    ffn_gain,
    gate_weight,
    up_weight,
    down_weight,
):
    token_count, model_dim = tokens.shape[1], tokens.shape[2]
    length = 2 * token_count
    inner = MH * MP
    channels = inner + 2 * NST
    part = part_index()
    wide, heads = inner // PARTS, MH // PARTS
    rows = token_count * PARTS
    seqs = rows // length
    fsdp = lax.axis_size("z") * 4

    smalls = [ffn_gain, mamba_gain, conv_bias, conv_weight]
    little = packed(mixer_gain[None].astype(F32), [v[None].astype(F32) for v in smalls])[0]
    count = query_weight.shape[0]
    kvh = HD * lax.axis_index("x")
    map_weight, step_weight = mamba_in_weight[:, 2 * inner : 2 * inner + 2 * NST], mamba_in_weight[:, 2 * inner + 2 * NST :]
    own = jnp.concatenate(
        [
            half_columns(map_weight),
            lax.dynamic_slice_in_dim(key_weight, kvh, HD, 1),
            lax.dynamic_slice_in_dim(value_weight, kvh, HD, 1),
            jnp.pad(half_columns(step_weight), ((0, 0), (0, 128 - MH // 2))),
        ],
        axis=1,
    )
    blocks = [mamba_in_weight[:, :inner], mamba_in_weight[:, inner : 2 * inner], query_weight]
    blocks = [half_columns(w).reshape(count, 2, 2, -1) for w in blocks]
    blocks = jnp.concatenate(blocks, axis=3).transpose(1, 2, 0, 3)
    token_rows = tokens.reshape(token_count, model_dim)
    grad_rows = cotangent.reshape(token_count, model_dim)
    hidden, gathered_little, shared, w_in, incoming = start_call(
        token_rows, little, own, blocks, grad_rows
    )
    hidden = hidden.reshape(rows, model_dim)
    incoming = incoming.reshape(rows, model_dim)
    w_in = w_in.reshape(model_dim, -1)
    shared = shared.reshape(model_dim, -1)
    share = shared.shape[1] // 2
    shared = jnp.concatenate(
        [
            shared[:, :NST],
            shared[:, share : share + NST],
            lax.dynamic_slice_in_dim(shared, lax.axis_index("x") * share + NST, share - NST, 1),
        ],
        axis=1,
    )
    w_out = fetch_rows_of([attn_out_weight, mamba_out_weight])
    w_attn_out, w_mamba_out = w_out[:HD], w_out[HD:]
    w_gateup = fetch_units(after((gate_weight, up_weight), hidden))
    down_half = down_weight.reshape(2, -1, model_dim)
    down_half = lax.dynamic_index_in_dim(down_half, lax.axis_index("x"), 0, keepdims=False)
    ff = gate_weight.shape[1] // PARTS

    gathered_little = gathered_little.reshape(fsdp, -1)
    gain_in = gathered_little[:, : mixer_gain.size].reshape(-1)
    got, at = [], 128
    for s in smalls:
        got.append(gathered_little[:, at : at + s.size].reshape((fsdp,) + s.shape))
        at += s.size
    gain_ffn, gain_mamba, bias_full = (g.reshape(-1) for g in got[:3])
    conv_full = got[3].transpose(1, 0, 2).reshape(4, channels)
    gain_mamba = lax.dynamic_slice_in_dim(gain_mamba, part * wide, wide, 0)

    def own_heads(v):
        return lax.dynamic_slice_in_dim(v.astype(F32), part * heads, heads, 0)

    heads_rows = jnp.stack([own_heads(v) for v in (decay_log, step_bias, skip_gain)])
    heads_rows = jnp.pad(heads_rows, ((0, 5), (0, 2 * MP - heads)))
    params = [
        lax.dynamic_slice_in_dim(conv_full, part * wide, wide, 1),
        lax.dynamic_slice_in_dim(bias_full, part * wide, wide, 0)[None],
        conv_full[:, inner:],
        bias_full[None, inner:],
        heads_rows,
    ]
    tables = rope_tables(length, HD)

    projected = mm(hidden, w_in)
    common = mm(hidden, shared).astype(BF)
    scanned, gated, squares, attended = mixer_forward(
        seqs, length, projected, common, params, tables
    )

    squares = plane_total(squares.reshape(-1, 128), 4)
    factor = lax.rsqrt(squares / inner + EPSILON).reshape(rows, 1)
    normal = gated * factor
    normed = (normal * gain_mamba).astype(BF)
    mixed = jnp.concatenate([attended, normed], axis=1)
    w_out = jnp.concatenate([w_attn_out, w_mamba_out], axis=0)
    block = (2, 2, 2, token_count, model_dim)
    mixer_sum = mm(mixed, w_out).astype(BF).reshape(block)
    second, middle, w_down = middle_calls(mixer_sum, token_rows, gain_ffn[None], down_half)
    w_down = w_down.reshape(ff, model_dim)
    second = second.reshape(rows, model_dim)
    gate_up = mm(second, w_gateup)
    gate_act, up_act = gate_up[:, :ff], gate_up[:, ff:]
    sig_g = jax.nn.sigmoid(gate_act)
    active = (gate_act * sig_g * up_act).astype(BF)

    grad_active = across(incoming, w_down)
    grad_gate = grad_active * up_act * sig_g * (1.0 + gate_act * (1.0 - sig_g))
    grad_up = grad_active * gate_act * sig_g
    grad_gateup = jnp.concatenate([grad_gate.astype(BF), grad_up.astype(BF)], axis=1)
    grad_wgateup = outer_product(second, grad_gateup)
    sum_gateup = lax.psum_scatter(grad_wgateup.astype(BF).reshape(-1, 4 * count, 2 * ff), "z")
    grad_second = across(grad_gateup, w_gateup).astype(BF).reshape(block)
    grad_mixer, grad_middle, grad_gain_ffn = middle_calls(
        grad_second, middle, gain_ffn[None], cot=grad_rows
    )
    grad_mixer = grad_mixer.reshape(rows, model_dim)
    grad_out = outer_product(mixed, grad_mixer)
    moved_out = rows_moved(grad_out, [HD, wide])
    grad_mixer, active = after((grad_mixer, active), grad_out)
    grad_down = outer_product(active, incoming).astype(BF)
    grad_mixer, active = after((grad_mixer, active), grad_down)
    sum_rows = rows_sum(moved_out, grad_down)
    grad_att = across(grad_mixer, w_attn_out).astype(BF)
    grad_normed = across(grad_mixer, w_mamba_out)
    grad_gain_mamba = jnp.sum(grad_normed * normal, axis=0)
    scaled = grad_normed * gain_mamba
    dots = jnp.sum(scaled * normal, axis=-1).reshape(-1, 128)
    if isinstance(moved_out, jax.Array):
        dots = after(dots, moved_out)
    dots = plane_total(dots, 5).reshape(rows, 1) / inner
    grad_in, grad_common, gxk, gxb, gmk, gmb, gheads = mixer_backward(
        seqs, length, projected, common, params, tables, scanned, grad_normed, gain_mamba[None],
        factor, dots, grad_att,
    )
    shares = [grad_common[:, : 2 * NST], grad_common[:, 2 * NST : 2 * NST + 2 * HD]]
    kept, away = column_halves(shares, "c")
    grad_hidden = across(after(grad_in, away), w_in)
    shares = column_added(kept, flip(away, "c"))
    kept, away = column_halves(shares, "y")
    grad_hidden = grad_hidden + across(after(grad_common, away), shared)
    grad_hidden = grad_hidden.astype(BF).reshape(block)
    shares = column_added(kept, flip(away, "y"))
    kept, away = column_halves(shares[:1], "x")
    grad_win = outer_product(hidden, after(grad_in, (away, grad_hidden))).astype(BF)
    grad_win = grad_win.reshape(-1, 2, 2, count, grad_win.shape[1])
    shares = [shares[1]] + column_added(kept, flip(away, "x"))
    slices = [v.astype(BF) for v in shares] + [grad_common[:, 2 * NST + 2 * HD :]]
    grad_slices = outer_product(hidden, jnp.concatenate(slices, axis=1)).astype(BF)
    grad_slices = grad_slices.reshape(-1, 2, 2, count, grad_slices.shape[1])
    result = mm(active, w_down).astype(BF).reshape(block)

    conv_grad = jnp.zeros((4, channels), F32)
    conv_grad = lax.dynamic_update_slice_in_dim(conv_grad, gxk, part * wide, 1)
    conv_grad = conv_grad.at[:, inner:].set(gmk)
    bias_grad = jnp.zeros((channels,), F32)
    bias_grad = lax.dynamic_update_slice_in_dim(bias_grad, gxb[0], part * wide, 0)
    bias_grad = bias_grad.at[inner:].set(gmb[0])
    gain_grad = lax.dynamic_update_slice_in_dim(
        jnp.zeros((inner,), F32), grad_gain_mamba, part * wide, 0
    )
    head_grad = lax.dynamic_update_slice_in_dim(
        jnp.zeros((3, MH), F32), gheads[:3, :heads], part * heads, 1
    )
    scattered = [grad_gain_ffn, gain_grad, bias_grad]
    little = [v.reshape(fsdp, -1) for v in scattered]
    little.append(conv_grad.reshape(4, fsdp, -1).transpose(1, 0, 2).reshape(fsdp, -1))
    little.append(jnp.broadcast_to(head_grad.reshape(1, -1), (fsdp, 3 * MH)))
    little = packed(jnp.zeros((fsdp, count), F32), little)
    little = little.reshape((-1, 2, 2) + little.shape[1:])
    moved = exchange_units(sum_gateup)
    moved = after(moved, grad_in)
    moved_across = flip(moved, "x")
    grad_hidden = after(grad_hidden, moved_across)
    tokens_grad, total, output, got_in, rows_across = last_call(
        grad_hidden, token_rows, gain_in[None], grad_middle, little, result, middle, grad_win,
        grad_slices, sum_rows,
    )
    output = output.reshape(1, token_count, model_dim)
    tokens_grad = tokens_grad.reshape(1, token_count, model_dim)
    total = total.reshape(-1)
    got, at = [total[:count]], 128
    for like in (ffn_gain, mamba_gain, conv_bias, conv_weight, head_grad):
        got.append(total[at : at + like.size].reshape(like.shape))
        at += like.size

    shard_gate, shard_up = unit_shards(moved, moved_across, 2)
    low, high = ordered(sum_rows, rows_across, "x")
    out_rows = sum_rows.shape[0] - ff // lax.axis_size("z") * model_dim // sum_rows.shape[1]
    shard_out = jnp.concatenate([low[:out_rows], high[:out_rows]], axis=1).astype(F32)
    shard_attn_out = shard_out[: attn_out_weight.shape[0]]
    shard_mamba_out = shard_out[attn_out_weight.shape[0] :]
    shard_down = jnp.concatenate([low[out_rows:], high[out_rows:]]).astype(F32)
    shard_down = shard_down.reshape(2, 2, -1, model_dim // 2).transpose(0, 2, 1, 3)
    shard_down = shard_down.reshape(-1, model_dim)

    def columns(first, width):
        return got_in[..., first : first + width]

    def by_part(first, width):
        return columns(first, width).transpose(3, 0, 1, 2, 4).reshape(count, -1)

    at = HD + 2 * wide
    kv = columns(at, HD // 2).transpose(1, 3, 0, 2, 4)
    mapped = columns(at + HD // 2, NST // 4).transpose(3, 1, 2, 0, 4).reshape(count, -1)
    stepped = columns(at + HD // 2 + NST // 4, MH // 2).astype(F32).sum(axis=(1, 2))
    stepped = stepped.transpose(1, 0, 2).reshape(count, -1)
    shard_query = by_part(2 * wide, HD).astype(F32)
    shard_key, shard_value = (kv[i].reshape(count, -1).astype(F32) for i in (0, 1))
    shard_mamba_in = jnp.concatenate(
        [v.astype(F32) for v in (by_part(0, wide), by_part(wide, wide), mapped, stepped)], axis=1
    )

    return (
        output,
        tokens_grad,
        got[0],
        shard_query,
        shard_key,
        shard_value,
        shard_attn_out,
        shard_mamba_in,
        got[4],
        got[3],
        got[5][0],
        got[5][1],
        got[5][2],
        got[2],
        shard_mamba_out,
        got[1],
        shard_gate,
        shard_up,
        shard_down,
    )


def solution(mesh):
    fsdp = mesh.shape["fsdp"]
    grid = Mesh(mesh.devices.reshape(2, fsdp // 4, 2, 2), ("x", "z", "y", "c"))
    rows, flat, whole = P(FSDP, None), P(FSDP), P()
    stream = P(FSDP, "x", None)
    weights = (
        flat, rows, rows, rows, rows, rows, P(None, FSDP), flat, whole, whole, whole,
        flat, rows, flat, rows, rows, rows,
    )
    return jax.shard_map(
        shards,
        mesh=grid,
        in_specs=(stream, stream) + weights,
        out_specs=(stream, stream) + weights,
        check_vma=False,
    )
```

time: 1020 us -> 840 us (0.82)
  Pallas kernels: 0 us -> 474 us
  waiting for transfers between devices: 297 us -> 54.1 us
  other arithmetic: 184 us -> 45.8 us
  starting transfers between devices: 96.4 us -> 12.4 us
  blocking collectives: 81.3 us -> 0 us
  local copies, waits for them, and re-layouts: 167 us -> 101 us
  matrix products: 162 us -> 130 us
    pallas_call x0 -> x8, Pallas kernels: none -> 474 us  [the longest x1 139 us: last_call(): pl.pallas_call(last_kernel, in_specs=[vmem] * 7 + [hbm] * 3, out_specs=[v...]
    ppermute x106 -> x16, waiting for transfers between devices: 287 us -> 54 us  [flip(): return lax.ppermute(value, axes, pairs)]
    all_gather x3 -> x0, blocking collectives: 81.3 us -> none  [the longest x1 39.4 us: shards(): shared = gather_inner(lax.all_gather(shared, 'z', axis=0, tiled=False))]
    ppermute x106 -> x16, starting transfers between devices: 84.8 us -> 12 us  [flip(): return lax.ppermute(value, axes, pairs)]
    dot_general x12 -> x0, matrix products: 32.5 us -> none  [the longest x1 8.18 us: core_parts(): y = jnp.einsum('bhts,bshp->bthp', mixing, xr, preferred_element_type=F32)]
    another operation x29 -> x7, other arithmetic: 33.5 us -> 2.66 us  [the longest x1 1.68 us: rows_moved(): return jnp.stack([got[0][0], got[0][1], got[1][0], got[1][1]])]
    add x28 -> x3, other arithmetic: 30.5 us -> 3.95 us  [column_added(): sums.append(v.astype(F32) + got[:, at:at + v.shape[1]].astype(F32))]
    unnamed x29 -> x5, other arithmetic: 26.4 us -> 1.41 us
  transfers between devices with their start and end apart: 116 -> 20, of which waited for: 48 -> 7; matrix products, arithmetic and copies ran while one was open for 45% -> 23% of each run, Pallas kernels for 0% -> 40%
where the time goes in v2:
time: 840 us; the launch traced here: 834 us
  Pallas kernels  474 us (56%)
  matrix products  130 us (15%)
  local copies, waits for them, and re-layouts  101 us (12%)
  waiting for transfers between devices  54.1 us (6%)
  other arithmetic  45.8 us (5%)
  between operations  15.5 us (2%)
  starting transfers between devices  12.4 us (1%)
    pallas_call x1, Pallas kernels, last_call(): pl.pallas_call(last_kernel, in_specs=[vmem] * 7 + [hbm] * 3, out_specs=[v...  139 us
    pallas_call x2, Pallas kernels, middle_calls(): pl.pallas_call(middle_kernel if cot is None else middle_back_kernel, in_s...  138 us
    pallas_call x1, Pallas kernels, start_call(): pl.pallas_call(start_kernel, in_specs=[vmem, vmem, hbm, hbm, hbm], out_sp...  132 us
    ppermute x16, waiting for transfers between devices, flip(): return lax.ppermute(value, axes, pairs)  54 us
    dot_general x6, matrix products, across(): lax.dot_general(left, right, (((1,), (1,)), ((), ())), preferred_element_...  51.6 us
    dot_general x5, matrix products, mm(): return jnp.dot(left, right, preferred_element_type=F32)  41.4 us
    dot_general x5, matrix products, outer_product(): lax.dot_general(left, right, (((0,), (0,)), ((), ())), preferred_element_...  37.4 us
    pallas_call x1, Pallas kernels, mixer_backward(): pl.pallas_call(mixer_back_kernel, grid=(seqs,), in_specs=mixer_specs(leng...  33.6 us
  transfers between devices with their start and end apart: 20, of which 7 were waited for; matrix products, arithmetic and copies ran while one was open for 23% of the time, Pallas kernels for 40%

profile of v2, /device:TPU:0, one launch (start us, length us, event | category | flops | bytes accessed | tf_op | source)
XLA Modules:
  0.0 833.6 jit_solution(14179800176030576036)
XLA Ops:
  22.0 131.7 %start.1 = (bf16[2,2,2,192,2048]{4,3,2,1,0:T(8,128)(2,1)}, f32[4,2,2,16,128]{4,3,2,1,0:T(8,128)S(1)}, bf16[4,2,2,128,1280]{4,3,2,1,0:T(8,128)(2,1)}, bf16[4,2,2,...) custom-call(bf16[192,2048]{1,0:T(8,128)(2,1)S(1)} %bitcast.247, f32[16,128]{1,0:T(8,128)S(1)} %bitcast.256, ...), custom_call_target="tpu_custom_call" | custom-call | tf_op jit(solution)/shard_map/start/pallas_call | solution.py:1044
  183.5 11.3 %convolution_convert_fusion.4.m_ref.s_ref.k_ref.v_ref = bf16[1536,896]{1,0:T(8,128)(2,1)} fusion(bf16[1536,2048]{1,0:T(8,128)(2,1)} %bitcast.329, bf16[2048,384]{1,0:T(8,128)(2,1)S(1)} %constant_dynamic-slice_fusion.3, bf16[2048,256]{1,0:T(8,128)(2,1)S(1)} %copy-done.42, bf16[2048,256]{1,0:T(8,128)(2,1)S(1)} %copy-done.41), kind=kOutput, calls=%fused_computation.7 | convolution fusion | flops 5649530880 | bytes 12713984 | tf_op jit(solution)/shard_map/dot_general | solution.py:29
  194.8 8.3 fusion.37.x_ref.z_ref.q_ref
  203.2 14.3 %mixer.1 = (bf16[1536,384]{1,0:T(8,128)(2,1)S(1)}, f32[1536,384]{1,0:T(8,128)S(1)}, f32[1536,1]{1,0:T(8,128)S(1)}, bf16[1536,128]{1,0:T(8,128)(2,1)S(1)}) custom-call(f32[1536,896]{1,0:T(8,128)} %fusion.37.x_ref.z_ref.q_ref, bf16[1536,896]{1,0:T(8,128)(2,1)} %convolution_convert_fusion.4.m_ref.s_ref.k_ref.v_ref, ...), custom_call_target="tpu_custom_call" | custom-call | tf_op jit(solution)/shard_map/mixer/pallas_call | solution.py:288
  220.8 8.6 %total.2 = f32[12,128]{1,0:T(8,128)} custom-call(f32[12,128]{1,0:T(8,128)} %bitcast.319), custom_call_target="tpu_custom_call" | custom-call | tf_op jit(solution)/shard_map/total/pallas_call | solution.py:647
  237.4 12.6 %collective-permute-done.1 = bf16[256,1024]{1,0:T(8,128)(2,1)S(1)} collective-permute-done((bf16[256,1024]{1,0:T(8,128)(2,1)S(1)}, bf16[256,1024]{1,0:T(8,128)(2,1)S(1)}, u32[]{:S(2)}, u32[]{:S(2)}) %collective-permute-start.1) | collective-permute-done | bytes 524320 | tf_op jit(solution)/shard_map/ppermute | solution.py:1077
  250.0 10.3 %collective-permute-done = bf16[256,1024]{1,0:T(8,128)(2,1)S(1)} collective-permute-done((bf16[256,1024]{1,0:T(8,128)(2,1)S(1)}, bf16[256,1024]{1,0:T(8,128)(2,1)S(1)}, u32[]{:S(2)}, u32[]{:S(2)}) %collective-permute-start) | collective-permute-done | bytes 524320 | tf_op jit(solution)/shard_map/ppermute | solution.py:1077
  262.0 5.4 convolution_convert_fusion.2
  267.3 68.6 %middle.1 = (bf16[2,2,2,192,2048]{4,3,2,1,0:T(8,128)(2,1)}, f32[192,2048]{1,0:T(8,128)S(1)}, bf16[4,128,2048]{2,1,0:T(8,128)(2,1)S(1)}) custom-call(bf16[2,2,2,192,2048]{4,3,2,1,0:T(8,128)(2,1)} %bitcast.272, bf16[192,2048]{1,0:T(8,128)(2,1)S(1)} %bitcast.248, f32[1,2048]{1,0:T(1,128)S(1)} %bitcast.254, bf16[128,2048]{1,0:T(8,128)(2,1)S(1)} %copy-done.10), custom_call_target="tpu_custom_call" | custom-call | tf_op jit(solution)/shard_map/middle/pallas_call | solution.py:622
  337.2 11.0 %fusion.38 = f32[1536,1024]{0,1:T(8,128)S(1)} fusion(bf16[1536,2048]{1,0:T(8,128)(2,1)} %bitcast.344, bf16[2048,1024]{1,0:T(8,128)(2,1)} %all-gather.4.cloned.1.call-done), kind=kOutput, calls=%fused_computation.186 | convolution fusion | flops 6442450944 | bytes 16777216 | tf_op jit(solution)/shard_map/dot_general | solution.py:29
  348.3 8.6 %multiply_convert_fusion.2 = (bf16[1536,512]{0,1:T(8,128)(2,1)S(1)}, bf16[1536,512]{0,1:T(8,128)(2,1)S(1)}, bf16[1536,512]{0,1:T(8,128)(2,1)}) fusion(f32[1536,1024]{0,1:T(8,128)S(1)} %fusion.38, bf16[1536,2048]{1,0:T(8,128)(2,1)} %bitcast.335, bf16[512,2048]{1,0:T(8,128)(2,1)S(1)} %bitcast.261), kind=kOutput, calls=%fused_computation.13 | convolution fusion | flops 3233808384 | bytes 19398656 | tf_op jit(solution)/shard_map/dot_general | solution.py:37
  356.9 9.3 %convolution_convert_fusion.3 = bf16[2048,1024]{1,0:T(8,128)(2,1)} fusion(bf16[1536,2048]{1,0:T(8,128)(2,1)S(1)} %bitcast.345, bf16[1536,512]{0,1:T(8,128)(2,1)S(1)} %get-tuple-element.238, bf16[1536,512]{0,1:T(8,128)(2,1)S(1)} %get-tuple-element.237), kind=kOutput, calls=%fused_computation.5 | convolution fusion | flops 6450839552 | bytes 13631488 | tf_op jit(solution)/shard_map/dot_general | solution.py:33
  366.3 11.6 %convolution_convert_fusion.1 = bf16[1536,2048]{1,0:T(8,128)(2,1)} fusion(bf16[2048,1024]{1,0:T(8,128)(2,1)} %all-gather.4.cloned.1.call-done, bf16[1536,512]{0,1:T(8,128)(2,1)} %copy-done.65, bf16[1536,512]{0,1:T(8,128)(2,1)} %copy-done.64), kind=kOutput, calls=%fused_computation.2 | convolution fusion | flops 6451888128 | bytes 13631488 | tf_op jit(solution)/shard_map/dot_general | solution.py:37
  378.0 69.9 %middle_back.1 = (bf16[2,2,2,192,2048]{4,3,2,1,0:T(8,128)(2,1)}, f32[192,2048]{1,0:T(8,128)S(1)}, f32[1,2048]{1,0:T(1,128)S(1)}) custom-call(bf16[2,2,2,192,2048]{4,3,2,1,0:T(8,128)(2,1)} %bitcast.271, f32[192,2048]{1,0:T(8,128)S(1)} %get-tuple-element.95.rows_ref.middle_ref, f32[1,2048]{1,0:T(1,128)S(1)} %bitcast.255, bf16[192,2048]{1,0:T(8,128)(2,1)S(1)} %bitcast.250), custom_call_target="tpu_custom_call" | custom-call | tf_op jit(solution)/shard_map/middle_back/pallas_call | solution.py:622
  447.9 7.1 fusion.3
  466.5 8.3 total.3
  480.7 33.6 %mixer_back.1 = (bf16[1536,896]{1,0:T(8,128)(2,1)}, bf16[1536,896]{1,0:T(8,128)(2,1)}, f32[4,384]{1,0:T(4,128)S(1)}, f32[1,384]{1,0:T(1,128)S(1)}, f32[4,512]{1,...) custom-call(f32[1536,896]{1,0:T(8,128)} %fusion.37.x_ref.z_ref.q_ref, ...), custom_call_target="tpu_custom_call" | custom-call | tf_op jit(solution)/shard_map/mixer_back/pallas_call | solution.py:305
  531.2 9.2 %fusion.39 = f32[1536,2048]{1,0:T(8,128)} fusion(bf16[1536,896]{1,0:T(8,128)(2,1)S(1)} %copy-done.55, bf16[2048,896]{1,0:T(8,128)(2,1)S(1)} %bitcast.347), kind=kOutput, calls=%fused_computation.187 | convolution fusion | flops 5637144576 | bytes 19005440 | tf_op jit(solution)/shard_map/dot_general | solution.py:37
  567.4 13.0 %add_convert_fusion = bf16[1536,2048]{1,0:T(8,128)(2,1)} fusion(f32[1536,2048]{1,0:T(8,128)} %fusion.39, bf16[1536,896]{1,0:T(8,128)(2,1)} %get-tuple-element.104, bf16[2048,384]{1,0:T(8,128)(2,1)} %copy-done.36, bf16[2048,256]{1,0:T(8,128)(2,1)} %get-tuple-element.241, bf16[2048,256]{1,0:T(8,128)(2,1)} %get-tuple-element.240), kind=kOutput, calls=%fused_computation | convolution fusion | flops 5654446080 | bytes 25296896 | tf_op jit(solution)/shard_map/dot_general | solution.py:37
  587.4 10.1 %convolution_convert_fusion.5 = bf16[2048,896]{1,0:T(8,128)(2,1)} fusion(bf16[1536,2048]{1,0:T(8,128)(2,1)} %bitcast.330, bf16[1536,896]{1,0:T(8,128)(2,1)S(1)} %copy-done.56), kind=kOutput, calls=%fused_computation.8 | convolution fusion | flops 5638979584 | bytes 12713984 | tf_op jit(solution)/shard_map/dot_general | solution.py:33
  601.4 6.8 collective-permute-done.12
  612.3 6.0 convolution_convert_fusion.7
  618.4 17.8 %collective-permute-done.13 = bf16[2,2,128,1024]{3,2,1,0:T(8,128)(2,1)} collective-permute-done((bf16[2,2,128,1024]{3,2,1,0:T(8,128)(2,1)S(1)}, bf16[2,2,128,1024]{3,2,1,0:T(8,128)(2,1)}, u32[]{:S(2)}, u32[]{:S(2)}) %collective-permute-start.13) | collective-permute-done | bytes 1048608 | tf_op jit(solution)/shard_map/ppermute | solution.py:1077
  636.2 139.5 %last.1 = (f32[192,2048]{1,0:T(8,128)}, f32[16,128]{1,0:T(8,128)}, bf16[192,2048]{1,0:T(8,128)(2,1)}, bf16[2,2,2,128,1152]{4,3,2,1,0:T(8,128)(2,1)}, bf16[512,1024]{1,0:T(8,128)(2,1)}) custom-call(bf16[2,2,2,192,2048]{4,3,2,1,0:T(8,128)(2,1)} %bitcast.274, bf16[192,2048]{1,0:T(8,128)(2,1)} %bitcast.246, f32[1,2048]{1,0:T(1,128)} %bitcast.318, ...), custom_call_target="tpu_custom_call" | custom-call | tf_op jit(solution)/shard_map/last/pallas_call | solution.py:866
  (373 shorter events, 185.0 us)
Async XLA Ops:
  7.2 225.5 %copy-start = (bf16[256,2048]{1,0:T(8,128)(2,1)S(1)}, bf16[256,2048]{1,0:T(8,128)(2,1)}, u32[]{:S(2)}) copy-start(bf16[256,2048]{1,0:T(8,128)(2,1)} %param.41) | copy-start | bytes 3145732
  7.2 226.3 %all-gather.6.cloned.1.call-start = ((), (), s32[]{:S(2)}) async-start(), calls=%async_computation.5 | async-start | bytes 2621440 | tf_op jit(solution)/shard_map/all_gather | solution.py:1153
  9.3 327.9 %all-gather.4.cloned.1.call-start = ((), (), s32[]{:S(2)}) async-start(), calls=%async_computation.2 | async-start | bytes 5242880 | tf_op jit(solution)/shard_map/all_gather | solution.py:1132
  163.2 11.5 %collective-permute-start.5 = (bf16[128,1024]{1,0:T(8,128)(2,1)}, bf16[128,1024]{1,0:T(8,128)(2,1)}, u32[]{:S(2)}, u32[]{:S(2)}) collective-permute-start(bf16[128,1024]{1,0:T(8,128)(2,1)} %bitcast.45), channel_id=1, source_target_pairs={{0,2},{2,0},{1,3},{3,1},{4,6},{6,4},{5,7},{7,5},{8,10},{10,8},{9,1... | collective-permute-start | bytes 786440 | tf_op jit(solution)/shard_map/ppermute | solution.py:1077
  166.4 8.4 %collective-permute-start.4 = (bf16[128,1024]{1,0:T(8,128)(2,1)}, bf16[128,1024]{1,0:T(8,128)(2,1)}, u32[]{:S(2)}, u32[]{:S(2)}) collective-permute-start(bf16[128,1024]{1,0:T(8,128)(2,1)} %bitcast.44), channel_id=1, source_target_pairs={{0,1},{1,0},{2,3},{3,2},{4,5},{5,4},{6,7},{7,6},{8,9},{9,8},{10,11... | collective-permute-start | bytes 786440 | tf_op jit(solution)/shard_map/ppermute | solution.py:1077
  167.4 10.0 %collective-permute-start.3 = (bf16[128,1024]{1,0:T(8,128)(2,1)}, bf16[128,1024]{1,0:T(8,128)(2,1)}, u32[]{:S(2)}, u32[]{:S(2)}) collective-permute-start(bf16[128,1024]{1,0:T(8,128)(2,1)} %bitcast.43), channel_id=1, source_target_pairs={{0,3},{1,2},{2,1},{3,0},{4,7},{5,6},{6,5},{7,4},{8,11},{9,10},{10,... | collective-permute-start | bytes 786440 | tf_op jit(solution)/shard_map/ppermute | solution.py:1077
  179.6 418.0 %reduce-scatter.3.cloned.1.call-start = ((), (), s32[]{:S(2)}) async-start(), calls=%async_computation.3 | async-start | bytes 5242880 | tf_op jit(solution)/shard_map/reduce_scatter | solution.py:1336
  235.1 2.3 collective-permute-start.2
  235.2 14.8 %collective-permute-start.1 = (bf16[256,1024]{1,0:T(8,128)(2,1)S(1)}, bf16[256,1024]{1,0:T(8,128)(2,1)S(1)}, u32[]{:S(2)}, u32[]{:S(2)}) collective-permute-start(bf16[256,1024]{1,0:T(8,128)(2,1)S(1)} %get-tuple-element.264), channel_id=1, source_target_pairs={{0,16},{16,0},{1,17},{17,1},{2,18},{18,2},{3,19},{19,3},{4,20},{20... | collective-permute-start | bytes 1572872 | tf_op jit(solution)/shard_map/ppermute | solution.py:1077
  236.1 24.2 %collective-permute-start = (bf16[256,1024]{1,0:T(8,128)(2,1)S(1)}, bf16[256,1024]{1,0:T(8,128)(2,1)S(1)}, u32[]{:S(2)}, u32[]{:S(2)}) collective-permute-start(bf16[256,1024]{1,0:T(8,128)(2,1)S(1)} %get-tuple-element.265), channel_id=1, source_target_pairs={{0,17},{1,16},{16,1},{17,0},{2,19},{3,18},{18,3},{19,2},{4,21},{5,... | collective-permute-start | bytes 1572872 | tf_op jit(solution)/shard_map/ppermute | solution.py:1077
  366.3 269.9 %reduce-scatter.5.cloned.1.call-start = ((), (), s32[]{:S(2)}) async-start(), calls=%async_computation.4 | async-start | bytes 5242880 | tf_op jit(solution)/shard_map/reduce_scatter | solution.py:1197
  378.0 69.9 %copy-start.22 = (bf16[1536,128]{1,0:T(8,128)(2,1)S(1)}, bf16[1536,128]{1,0:T(8,128)(2,1)}, u32[]{:S(2)}) copy-start(bf16[1536,128]{1,0:T(8,128)(2,1)} %copy-done.21) | copy-start | bytes 1179652
  378.0 69.9 %copy-start.38 = (bf16[1536,384]{1,0:T(8,128)(2,1)S(1)}, bf16[1536,384]{1,0:T(8,128)(2,1)}, u32[]{:S(2)}) copy-start(bf16[1536,384]{1,0:T(8,128)(2,1)} %copy-done.37) | copy-start | bytes 3538948
  378.0 77.1 %slice-start.6 = ((s8[6291456]{0:T(1024)(128)(4,1)}), s8[4194304]{0:T(1024)(128)(4,1)S(1)}, s32[]{:S(2)}) async-start(s8[6291456]{0:T(1024)(128)(4,1)} %bitcast.336), calls=%async_computation.12 | async-start | bytes 8388608
  527.7 26.2 %collective-permute-start.8 = (bf16[256,1024]{1,0:T(8,128)(2,1)}, bf16[256,1024]{1,0:T(8,128)(2,1)}, u32[]{:S(2)}, u32[]{:S(2)}) collective-permute-start(bf16[256,1024]{1,0:T(8,128)(2,1)} %get-tuple-element.260), channel_id=1, source_target_pairs={{0,1},{1,0},{2,3},{3,2},{4,5},{5,4},{6,7},{7,6},{8,9},{9,8},{10,11... | collective-permute-start | bytes 1572872 | tf_op jit(solution)/shard_map/ppermute | solution.py:1077
  527.8 26.2 %collective-permute-start.7 = (bf16[256,1024]{1,0:T(8,128)(2,1)}, bf16[256,1024]{1,0:T(8,128)(2,1)}, u32[]{:S(2)}, u32[]{:S(2)}) collective-permute-start(bf16[256,1024]{1,0:T(8,128)(2,1)} %get-tuple-element.261), channel_id=1, source_target_pairs={{0,16},{16,0},{1,17},{17,1},{2,18},{18,2},{3,19},{19,3},{4,20},{20... | collective-permute-start | bytes 1572872 | tf_op jit(solution)/shard_map/ppermute | solution.py:1077
  528.9 25.1 %collective-permute-start.6 = (bf16[256,1024]{1,0:T(8,128)(2,1)}, bf16[256,1024]{1,0:T(8,128)(2,1)}, u32[]{:S(2)}, u32[]{:S(2)}) collective-permute-start(bf16[256,1024]{1,0:T(8,128)(2,1)} %get-tuple-element.262), channel_id=1, source_target_pairs={{0,17},{1,16},{16,1},{17,0},{2,19},{3,18},{18,3},{19,2},{4,21},{5,... | collective-permute-start | bytes 1572872 | tf_op jit(solution)/shard_map/ppermute | solution.py:1077
  530.9 31.1 %collective-permute-start.9 = (bf16[1536,384]{1,0:T(8,128)(2,1)}, bf16[1536,384]{1,0:T(8,128)(2,1)}, u32[]{:S(2)}, u32[]{:S(2)}) collective-permute-start(bf16[1536,384]{1,0:T(8,128)(2,1)} %pad_maximum_fusion.9), channel_id=1, source_target_pairs={{0,1},{1,0},{2,3},{3,2},{4,5},{5,4},{6,7},{7,6},{8,9},{9,8},{10,11... | collective-permute-start | bytes 3538952 | tf_op jit(solution)/shard_map/ppermute | solution.py:1077
  566.1 15.8 %collective-permute-start.14 = (bf16[1536,192]{0,1:T(8,128)(2,1)}, bf16[1536,192]{0,1:T(8,128)(2,1)S(1)}, u32[]{:S(2)}, u32[]{:S(2)}) collective-permute-start(bf16[1536,192]{0,1:T(8,128)(2,1)} %copy.248), channel_id=1, source_target_pairs={{0,2},{2,0},{1,3},{3,1},{4,6},{6,4},{5,7},{7,5},{8,10},{10,8},{9,1... | collective-permute-start | bytes 1769480 | tf_op jit(solution)/shard_map/ppermute | solution.py:1077
  586.3 25.8 %collective-permute-start.15 = (bf16[1536,64]{1,0:T(8,128)(2,1)S(1)}, bf16[1536,64]{1,0:T(8,128)(2,1)S(1)}, u32[]{:S(2)}, u32[]{:S(2)}) collective-permute-start(bf16[1536,64]{1,0:T(8,128)(2,1)S(1)} %dynamic-slice_convert_fusion), channel_id=1, source_target_pairs={{0,16},{16,0},{1,17},{17,1},{2,18},{18,2},{3,19},{19,3},{4,20},{20... | collective-permute-start | bytes 589832 | tf_op jit(solution)/shard_map/ppermute | solution.py:1077
  598.9 9.3 %collective-permute-start.12 = (bf16[128,1024]{1,0:T(8,128)(2,1)S(1)}, bf16[128,1024]{1,0:T(8,128)(2,1)S(1)}, u32[]{:S(2)}, u32[]{:S(2)}) collective-permute-start(bf16[128,1024]{1,0:T(8,128)(2,1)S(1)} %get-tuple-element.276), channel_id=1, source_target_pairs={{0,2},{2,0},{1,3},{3,1},{4,6},{6,4},{5,7},{7,5},{8,10},{10,8},{9,1... | collective-permute-start | bytes 786440 | tf_op jit(solution)/shard_map/ppermute | solution.py:1077
  600.0 8.3 collective-permute-start.11
  600.0 10.5 %collective-permute-start.10 = (bf16[128,1024]{1,0:T(8,128)(2,1)S(1)}, bf16[128,1024]{1,0:T(8,128)(2,1)S(1)}, u32[]{:S(2)}, u32[]{:S(2)}) collective-permute-start(bf16[128,1024]{1,0:T(8,128)(2,1)S(1)} %get-tuple-element.278), channel_id=1, source_target_pairs={{0,3},{1,2},{2,1},{3,0},{4,7},{5,6},{6,5},{7,4},{8,11},{9,10},{10,... | collective-permute-start | bytes 786440 | tf_op jit(solution)/shard_map/ppermute | solution.py:1077
  610.8 25.4 %collective-permute-start.13 = (bf16[2,2,128,1024]{3,2,1,0:T(8,128)(2,1)S(1)}, bf16[2,2,128,1024]{3,2,1,0:T(8,128)(2,1)}, u32[]{:S(2)}, u32[]{:S(2)}) collective-permute-start(bf16[2,2,128,1024]{3,2,1,0:T(8,128)(2,1)S(1)} %pad_maximum_fusion.11), channel_id=1, source_target_pairs={{0,16},{16,0},{1,17},{17,1},{2,18},{18,2},{3,19},{19,3},{4,20},{20... | collective-permute-start | bytes 3145736 | tf_op jit(solution)/shard_map/ppermute | solution.py:1077
  (72 other events, 547.8 us)
Sparse Core Ops, SparseCore 0:
  10.2 62.4 all-gather.5
  179.7 78.6 all-gather.3
  366.4 74.5 reduce-scatter.2
  558.5 74.8 reduce-scatter.4

commit v3 on v2

--- a/solution.py
+++ b/solution.py
@@ -96,14 +96,15 @@
     return (MH // PARTS) * (2 * lax.axis_index("c") + lax.axis_index("y"))
 
 
-def scan_parts(x_ref, m_ref, s_ref, xk_ref, xb_ref, mk_ref, mb_ref, h_ref):
+def scan_parts(x_ref, m_refs, s_ref, xk_ref, xb_ref, mk_ref, mb_ref, h_ref):
     length = x_ref.shape[0]
-    xin, maps = x_ref[...].astype(BF).astype(F32), m_ref[...].astype(F32)
+    xin = x_ref[...].astype(BF).astype(F32)
+    maps = jnp.concatenate([ref[...].astype(BF).astype(F32) for ref in m_refs], axis=1)
     xs, xslope = conv_silu(xin, xk_ref[...], xb_ref[...])
     mv, mslope = conv_silu(maps, mk_ref[...], mb_ref[...])
     mv = mv.astype(BF)
     bees, cees = mv[:, :NST], mv[:, NST:]
-    raw = pltpu.roll(s_ref[...].astype(F32), 2 * MP - step_place(), 1) + h_ref[1:2]
+    raw = pltpu.roll(s_ref[...].astype(BF).astype(F32), 2 * MP - step_place(), 1) + h_ref[1:2]
     dt = jnp.maximum(raw, 0.0) + jnp.log1p(jnp.exp(-jnp.abs(raw)))
     rate = -jnp.exp(h_ref[0:1])
     t = lax.broadcasted_iota(jnp.int32, (length, length), 0)
@@ -140,11 +141,11 @@
 
 
 def mixer_kernel(
-    x_ref, m_ref, s_ref, z_ref, q_ref, k_ref, v_ref, xk_ref, xb_ref, mk_ref, mb_ref, h_ref,
+    x_ref, m0_ref, m1_ref, m2_ref, m3_ref, s_ref, z_ref, q_ref, k_ref, v_ref, xk_ref, xb_ref, mk_ref, mb_ref, h_ref,
     cos_ref, sin_ref, scan_ref, gated_ref, square_ref, att_ref,
 ):
     xin, maps, xs, xslope, mslope, bees, cees, raw, dt, rate, lower, cum, coupling = scan_parts(
-        x_ref, m_ref, s_ref, xk_ref, xb_ref, mk_ref, mb_ref, h_ref
+        x_ref, (m0_ref, m1_ref, m2_ref, m3_ref), s_ref, xk_ref, xb_ref, mk_ref, mb_ref, h_ref
     )
     cumt = cum.T
     lane = lax.broadcasted_iota(jnp.int32, (xs.shape[0], 2 * MP), 1)
@@ -167,17 +168,17 @@
     weights, total = causal_scores(
         rotated(q_ref, cos_ref, sin_ref), rotated(k_ref, cos_ref, sin_ref)
     )
-    att_ref[...] = dot((weights / total).astype(BF), v_ref[...]).astype(BF)
+    att_ref[...] = dot((weights / total).astype(BF), v_ref[...].astype(BF)).astype(BF)
 
 
 def mixer_back_kernel(
-    x_ref, m_ref, s_ref, z_ref, q_ref, k_ref, v_ref, xk_ref, xb_ref, mk_ref, mb_ref, h_ref,
+    x_ref, m0_ref, m1_ref, m2_ref, m3_ref, s_ref, z_ref, q_ref, k_ref, v_ref, xk_ref, xb_ref, mk_ref, mb_ref, h_ref,
     cos_ref, sin_ref, scan_ref, gn_ref, gain_ref, factor_ref, dots_ref, ga_ref,
-    gin_ref, gcom_ref,
+    gin_ref,
     gxk_ref, gxb_ref, gmk_ref, gmb_ref, gh_ref,
 ):
     xin, maps, xs, xslope, mslope, bees, cees, raw, dt, rate, lower, cum, coupling = scan_parts(
-        x_ref, m_ref, s_ref, xk_ref, xb_ref, mk_ref, mb_ref, h_ref
+        x_ref, (m0_ref, m1_ref, m2_ref, m3_ref), s_ref, xk_ref, xb_ref, mk_ref, mb_ref, h_ref
     )
     length, width = xs.shape
     cumt = cum.T
@@ -229,12 +230,13 @@
     gdt = gdt + gflow * rate
     graw = gdt / (1.0 + jnp.exp(-raw))
     graw = jnp.where(lane < width // MP, graw, 0.0)
-    gcom_ref[:, 2 * NST + 2 * HD :] = pltpu.roll(graw, step_place(), 1).astype(BF)
+    common = 2 * width + HD
+    gin_ref[:, common + 2 * NST + 2 * HD :] = pltpu.roll(graw, step_place(), 1).astype(BF)
     gdecay = jnp.sum(gflow * dt, axis=0, keepdims=True) * rate
     gcb = gcoup.astype(BF)
     gmaps = jnp.concatenate([dot(gcb, cees, ROWS), dot(gcb, bees)], axis=1) * mslope
     gm, gmk, gmb = conv_grads(maps, mk_ref[...], gmaps)
-    gcom_ref[:, : 2 * NST] = gm.astype(BF)
+    gin_ref[:, common : common + 2 * NST] = gm.astype(BF)
     gh = jnp.concatenate([gdecay, jnp.sum(graw, axis=0, keepdims=True), gskip], axis=0)
 
     @pl.when(pl.program_id(0) == 0)
@@ -251,15 +253,15 @@
     rq, rk = rotated(q_ref, cos_ref, sin_ref), rotated(k_ref, cos_ref, sin_ref)
     weights, total = causal_scores(rq, rk)
     probs = weights / total
-    gatt = ga_ref[...]
-    gcom_ref[:, 2 * NST + HD : 2 * NST + 2 * HD] = dot(probs.astype(BF), gatt, ROWS).astype(BF)
-    gp = dot(gatt, v_ref[...], LANES)
+    gatt = ga_ref[...].astype(BF)
+    kv = common + 2 * NST
+    gin_ref[:, kv + HD : kv + 2 * HD] = dot(probs.astype(BF), gatt, ROWS).astype(BF)
+    gp = dot(gatt, v_ref[...].astype(BF), LANES)
     gsc = (probs * (gp - jnp.sum(probs * gp, axis=1, keepdims=True))).astype(BF)
-    places = ((gin_ref, 2 * width), (gcom_ref, 2 * NST))
-    for (ref, at), grad in zip(places, (dot(gsc, rk), dot(gsc, rq, ROWS))):
+    for at, grad in ((2 * width, dot(gsc, rk)), (kv, dot(gsc, rq, ROWS))):
         grad = grad * HD ** (-0.5)
         back = grad * cos_ref[...] - pltpu.roll(grad, HD // 2, 1) * sin_ref[...]
-        ref[:, at : at + HD] = back.astype(BF)
+        gin_ref[:, at : at + HD] = back.astype(BF)
 
 
 def column_block(length, width, at):
@@ -267,22 +269,25 @@
 
 
 def mixer_specs(length, wide):
-    return [
-        column_block(length, wide, wide),
-        column_block(length, 2 * NST, 0),
-        column_block(length, 2 * MP, 2 * NST + 2 * HD),
-        column_block(length, wide, 0),
-        column_block(length, HD, 2 * wide),
-        column_block(length, HD, 2 * NST),
-        column_block(length, HD, 2 * NST + HD),
-    ]
+    maps = 2 * wide + HD
+    return (
+        [column_block(length, wide, wide)]
+        + [column_block(length, NST // 2, maps + at) for at in range(0, 2 * NST, NST // 2)]
+        + [
+            column_block(length, 2 * MP, maps + 2 * NST + 2 * HD),
+            column_block(length, wide, 0),
+            column_block(length, HD, 2 * wide),
+            column_block(length, HD, maps + 2 * NST),
+            column_block(length, HD, maps + 2 * NST + HD),
+        ]
+    )
 
 
 def whole_specs(arrays):
     return [pl.BlockSpec(a.shape, lambda i: (0, 0)) for a in arrays]
 
 
-def mixer_forward(seqs, length, projected, common, params, tables):
+def mixer_forward(seqs, length, projected, params, tables):
     wide = params[0].shape[1]
     outs = [(wide, BF), (wide, F32), (1, F32), (HD, BF)]
     return pl.pallas_call(
@@ -293,21 +298,20 @@
         out_shape=[jax.ShapeDtypeStruct((seqs * length, w), d) for w, d in outs],
         compiler_params=pltpu.CompilerParams(vmem_limit_bytes=VMEM),
         name="mixer",
-    )(projected, common, common, projected, projected, common, common, *params, *tables)
-
-
-def mixer_backward(seqs, length, projected, common, params, tables, scanned, grad_normed, gain, factor, dots, grad_att):
+    )(*[projected] * 10, *params, *tables)
+
+
+def mixer_backward(seqs, length, projected, params, tables, scanned, grad_mixed, gain, factor, dots):
     wide = params[0].shape[1]
-    outs = [2 * wide + HD, 2 * NST + 2 * HD + 2 * MP]
+    outs = [projected.shape[1]]
     sums = [(4, wide), (1, wide), (4, 2 * NST), (1, 2 * NST), (8, 2 * MP)]
-    rows = [scanned, grad_normed]
-    tail = [factor, dots, grad_att]
+    row_specs = [column_block(length, wide, 0), column_block(length, wide, 0)]
+    tail_specs = [column_block(length, 1, 0), column_block(length, 1, 0), column_block(length, HD, wide)]
     return pl.pallas_call(
         mixer_back_kernel,
         grid=(seqs,),
         in_specs=mixer_specs(length, wide) + whole_specs(params + tables)
-        + [column_block(length, a.shape[1], 0) for a in rows] + whole_specs([gain])
-        + [column_block(length, a.shape[1], 0) for a in tail],
+        + row_specs + whole_specs([gain]) + tail_specs,
         out_specs=[column_block(length, w, 0) for w in outs]
         + [pl.BlockSpec(s, lambda i: (0, 0)) for s in sums],
         out_shape=[jax.ShapeDtypeStruct((seqs * length, w), BF) for w in outs]
@@ -315,8 +319,7 @@
         compiler_params=pltpu.CompilerParams(vmem_limit_bytes=VMEM),
         name="mixer_back",
     )(
-        projected, common, common, projected, projected, common, common,
-        *params, *tables, *rows, gain, *tail,
+        *[projected] * 10, *params, *tables, scanned, grad_mixed, gain, factor, dots, grad_mixed,
     )
 
 
@@ -469,18 +472,18 @@
     ]
 
 
-def reduce_plane(part, scratch):
+def reduce_plane(part, scratch, firsts=("y", "x")):
     core, wide_in, wide_out, thin_in, thin_out, sems = scratch
     half = part.shape[4] // 2
     x, y, c = (lax.axis_index(a) for a in ("x", "y", "c"))
-    firsts, seconds = ("y", "x"), ("x", "y")
+    seconds = ["x" if axis == "y" else "y" for axis in firsts]
     cols = [slice(0, half), slice(half, 2 * half)]
 
     def chip(i, yy, xx):
         return part[yy, c, xx, :, cols[i]].astype(F32) + core[i, yy, xx].astype(F32)
 
     def kept(i, index):
-        mine = chip(i, y, index) if i == 0 else chip(i, index, x)
+        mine = chip(i, y, index) if firsts[i] == "y" else chip(i, index, x)
         return mine + wide_in[i, index].astype(F32)
 
     copies = [
@@ -500,24 +503,25 @@
         for copy in copies:
             copy.start()
 
-    def wide():
-        for i in (0, 1):
+    def wide(which=(0, 1)):
+        for i in which:
             copies[i].wait()
             for k in (0, 1):
-                wide_out[i, k] = (chip(i, 1 - y, k) if i == 0 else chip(i, k, 1 - x)).astype(BF)
+                away = chip(i, 1 - y, k) if firsts[i] == "y" else chip(i, k, 1 - x)
+                wide_out[i, k] = away.astype(BF)
             wides[i].start()
 
     def thin():
         for i in (0, 1):
             wides[i].wait()
-            thin_out[i] = kept(i, 1 - x if i == 0 else 1 - y).astype(BF)
+            thin_out[i] = kept(i, 1 - x if firsts[i] == "y" else 1 - y).astype(BF)
             thins[i].start()
 
     def end():
         outs = []
         for i in (0, 1):
             thins[i].wait()
-            outs.append(kept(i, x if i == 0 else y) + thin_in[i].astype(F32))
+            outs.append(kept(i, x if firsts[i] == "y" else y) + thin_in[i].astype(F32))
         return jnp.concatenate(outs, axis=1)
 
     return begin, wide, thin, end
@@ -720,28 +724,130 @@
     return kick, pass_on, end, finish
 
 
+def column_sums(grad_ref, first, boxes, sems, local):
+    own, by_c, for_y, by_y, for_x, by_x, out = boxes
+    x, y, c = (lax.axis_index(a) for a in ("x", "y", "c"))
+
+    def cols(side):
+        maps = pl.ds(pl.multiple_of(first + side * NST, 128), NST)
+        kv = pl.ds(pl.multiple_of(first + 2 * NST + side * HD, 128), HD)
+        return (maps, pl.ds(0, NST)), (kv, pl.ds(NST, HD))
+
+    steps = pl.ds(first + 2 * NST + 2 * HD, 128)
+    loads = [
+        pltpu.make_async_copy(grad_ref.at[:, src], own.at[:, dst], local.at[i])
+        for i, (src, dst) in enumerate(cols(c))
+    ]
+    loads.append(pltpu.make_async_copy(grad_ref.at[:, steps], out.at[:, pl.ds(128, 128)], local.at[2]))
+    across = [
+        remote(grad_ref.at[:, src], by_c.at[:, dst], sems.at[0, i], sems.at[1, i], "c")
+        for i, (src, dst) in enumerate(cols(1 - c))
+    ]
+    over_y = remote(for_y, by_y, sems.at[0, 2], sems.at[1, 2], "y")
+    over_x = remote(for_x, by_x, sems.at[0, 3], sems.at[1, 3], "x")
+
+    def begin():
+        for copy in loads + across:
+            copy.start()
+
+    def halves(value, side):
+        maps, kv = value[:, :NST], value[:, NST:]
+        maps = jnp.where(side == 0, maps[:, : NST // 2], maps[:, NST // 2 :])
+        kv = jnp.where(side == 0, kv[:, : HD // 2], kv[:, HD // 2 :])
+        return maps, kv
+
+    def second():
+        for copy in loads + across:
+            copy.wait()
+        maps, kv = halves(own[...].astype(F32) + by_c[...].astype(F32), 1 - y)
+        for_y[...] = jnp.concatenate([maps, kv, kv], axis=1).astype(BF)
+        over_y.start()
+
+    def summed():
+        got = by_y[...].astype(F32)
+        maps, kv = halves(own[...].astype(F32) + by_c[...].astype(F32), y)
+        return maps + got[:, : NST // 2], kv + got[:, NST // 2 : NST // 2 + HD // 2]
+
+    def third():
+        over_y.wait()
+        maps, kv = summed()
+        away = jnp.where(x == 0, maps[:, NST // 4 :], maps[:, : NST // 4])
+        for_x[...] = jnp.concatenate([away, away], axis=1).astype(BF)
+        over_x.start()
+
+    def end():
+        over_x.wait()
+        maps, kv = summed()
+        maps = jnp.where(x == 0, maps[:, : NST // 4], maps[:, NST // 4 :])
+        maps = maps + by_x[...].astype(F32)[:, : NST // 4]
+        out[:, 0:128] = jnp.concatenate([kv, maps], axis=1).astype(BF)
+
+    return begin, second, third, end
+
+
+def hand_out(held, swap, got, places, sems, own_sems):
+    x, y, c = (lax.axis_index(a) for a in ("x", "y", "c"))
+    moves, kept = [], []
+
+    def give(i):
+        yy, cc = places[i]
+        if i == 3:
+            swap[c, y] = held(yy, cc)[...]
+            return
+        move = pltpu.make_async_remote_copy(
+            src_ref=held(yy, cc),
+            dst_ref=swap.at[c, y],
+            send_sem=sems.at[0, i],
+            recv_sem=sems.at[1, i],
+            device_id={"y": yy, "c": cc},
+            device_id_type=pl.DeviceIdType.MESH,
+        )
+        move.start()
+        moves.append(move)
+
+    def forward(i):
+        yy, cc = places[i]
+        if i < 3:
+            moves[i].wait_recv()
+        keep = pltpu.make_async_copy(swap.at[cc, yy], got.at[x, cc, yy], own_sems.at[i])
+        move = remote(swap.at[cc, yy], got.at[x, cc, yy], sems.at[0, 3 + i], sems.at[1, 3 + i], "x")
+        for copy in (keep, move):
+            copy.start()
+            kept.append(copy)
+
+    def finish():
+        for copy in kept:
+            copy.wait()
+        for move in moves:
+            move.wait_send()
+
+    return give, forward, finish
+
+
 def last_kernel(
-    part_ref, rows_ref, gain_ref, grad_ref, little_ref, down_ref, middle_ref, weight_ref, slice_ref, cross_ref,
-    out_ref, little_out, result_ref, got_ref, crossed_ref,
-    held, inbox, swap, little, little_in, little_c, little_y, little_box,
-    local, weight_sems, little_sems, hop_sems, swap_sems, got_sems, own_sems, cross_sems, *scratch,
+    part_ref, rows_ref, gain_ref, grad_ref, little_ref, weight_ref, common_ref, hidden_ref,
+    rows_in, down_in,
+    out_ref, little_out, got_ref, few_ref, rows_out, down_out,
+    held, inbox, few, few_box, swap, few_swap, little, little_in, little_c, little_y, little_box,
+    hidden, col_own, col_c, col_y_out, col_y_in, col_x_out, col_x_in, slices,
+    local, weight_sems, few_sems, little_sems, hop_sems, swap_sems, few_swap_sems, own_sems,
+    cross_sems, col_sems, col_local, *scratch,
 ):
     x, z, y, c = (lax.axis_index(a) for a in ("x", "z", "y", "c"))
     n = lax.axis_size("z")
     greet_all()
-    cut = weight_ref.shape[4]
-    loads = []
-    for i, (ref, at) in enumerate(((weight_ref, 0), (slice_ref, cut))):
-        into = held.at[:, :, :, :, pl.ds(at, ref.shape[4])]
-        loads.append(pltpu.make_async_copy(ref, into, local.at[i]))
-        loads[i].start()
-    half = len(scratch) // 2
-    begin, wide, thin, end = reduce_plane(part_ref, scratch[:half])
-    begin_down, wide_down, thin_down, end_down = reduce_plane(down_ref, scratch[half:])
+    load = pltpu.make_async_copy(weight_ref, held, local.at[0])
+    load.start()
+    load_hidden = pltpu.make_async_copy(hidden_ref, hidden, local.at[1])
+    load_hidden.start()
+    begin, wide, thin, end = reduce_plane(part_ref, scratch)
+    boxes = (col_own, col_c, col_y_out, col_y_in, col_x_out, col_x_in, slices)
+    col_begin, col_second, col_third, col_end = column_sums(
+        common_ref, common_ref.shape[1] // 2, boxes, col_sems, col_local
+    )
+    col_begin()
     begin()
-    begin_down()
-    for load in loads:
-        load.wait()
+    load.wait()
 
     order = ((1, 1), (1, 0), (0, 1), (0, 0))
     sums, places = [], []
@@ -755,11 +861,16 @@
                 weight_sems.at[i],
             )
         )
+    few_sum = line_sum(lambda d: few.at[d], lambda d: few_box.at[d], few_sems)
     for k in range(n - 1):
         for item in sums:
             item[0](k)
-    wide()
-    wide_down()
+    crosses = []
+    for i, (src, dst) in enumerate(((rows_in, rows_out), (down_in, down_out))):
+        crosses.append(remote(src, dst, cross_sems.at[0, i], cross_sems.at[1, i], "x"))
+        crosses[i].start()
+    col_second()
+    wide((0,))
 
     def pass_all(k):
         for item in sums:
@@ -774,20 +885,28 @@
                     item[1](1 - near, k)
 
     pass_all(0)
-    thin()
-    thin_down()
-    cross = remote(cross_ref, crossed_ref, cross_sems.at[0], cross_sems.at[1], "x")
-    cross.start()
+    col_third()
+    wide((1,))
+    col_end()
+    load_hidden.wait()
+    product = dot(slices[...], hidden[...], ROWS).T.astype(BF)
+    piece = product.shape[0] // (4 * n)
+    for at in range(n):
+        for yy in (0, 1):
+            for cc in (0, 1):
+                first = (4 * at + 2 * yy + cc) * piece
+                few[at, yy, cc] = product[first : first + piece]
+    for k in range(n - 1):
+        few_sum[0](k)
     for k in range(1, n - 1):
         pass_all(k)
-
-    result_ref[...] = (middle_ref[...] + end_down()).astype(BF)
+    thin()
+
     rows = rows_ref[...].astype(F32)
     grad, gain_grad = norm_back_parts(rows, gain_ref[...], end())
     out_ref[...] = grad + grad_ref[...]
 
     little[...] = little_ref[...]
-    piece = rows.shape[1] // (4 * n)
     for at in range(n):
         for yy in (0, 1):
             for cc in (0, 1):
@@ -809,170 +928,208 @@
     little_sum = line_sum(lambda d: little_y.at[d], lambda d: little_box.at[d], little_sems)
     for k in range(n - 1):
         little_sum[0](k)
+
+    give, forward, finish = hand_out(
+        lambda yy, cc: held.at[z, yy, cc], swap, got_ref, places, swap_sems, own_sems.at[0]
+    )
+    few_give, few_forward, few_finish = hand_out(
+        lambda yy, cc: few.at[z, yy, cc], few_swap, few_ref, places, few_swap_sems, own_sems.at[1]
+    )
+    for i in range(4):
+        sums[i][2]()
+        give(i)
+        if i > 0:
+            forward(i - 1)
+        if i < n - 1:
+            for way in (0, 1):
+                few_sum[1](way, i)
+    forward(3)
+    for k in range(4, n - 1):
+        for way in (0, 1):
+            few_sum[1](way, k)
+    few_sum[2]()
+    for i in range(4):
+        few_give(i)
     for k in range(n - 1):
         for way in (0, 1):
             little_sum[1](way, k)
     little_sum[2]()
     little_out[...] = little_y[z]
-
-    moves, crossed, kept = [], [], []
-
-    def forward(i):
-        yy, cc = places[i]
-        if i < 3:
-            moves[i].wait_recv()
-        keep = pltpu.make_async_copy(swap.at[cc, yy], got_ref.at[x, cc, yy], own_sems.at[i])
-        keep.start()
-        kept.append(keep)
-        move = remote(
-            swap.at[cc, yy], got_ref.at[x, cc, yy], got_sems.at[0, i], got_sems.at[1, i], "x"
-        )
-        move.start()
-        crossed.append(move)
-
-    for i, (yy, cc) in enumerate(places):
-        sums[i][2]()
-        if i < 3:
-            move = pltpu.make_async_remote_copy(
-                src_ref=held.at[z, yy, cc],
-                dst_ref=swap.at[c, y],
-                send_sem=swap_sems.at[0, i],
-                recv_sem=swap_sems.at[1, i],
-                device_id={"y": yy, "c": cc},
-                device_id_type=pl.DeviceIdType.MESH,
-            )
-            move.start()
-            moves.append(move)
-        else:
-            swap[c, y] = held[z, yy, cc]
-        if i > 0:
-            forward(i - 1)
-    forward(3)
-    cross.wait()
-    for copy in kept + crossed:
-        copy.wait()
-    for move in moves:
-        move.wait_send()
-    for item in sums + [little_sum]:
+    for i in range(4):
+        few_forward(i)
+    for cross in crosses:
+        cross.wait()
+    finish()
+    few_finish()
+    for item in sums + [few_sum, little_sum]:
         item[3]()
 
 
-def last_call(part, rows, gain, grad, little, down, middle, weight, slices, cross):
+def last_call(part, rows, gain, grad, little, weight, common, hidden, sum_rows, sum_down):
     n = lax.axis_size("z")
     count, width = rows.shape
-    block, pack = (weight.shape[3], weight.shape[4] + slices.shape[4]), little.shape[3:]
+    total, piece = hidden.shape[0], weight.shape[3]
+    block, small, pack = weight.shape[3:], (piece, 256), little.shape[3:]
     vmem, hbm = pl.BlockSpec(memory_space=pltpu.VMEM), pl.BlockSpec(memory_space=pl.ANY)
     dma = pltpu.SemaphoreType.DMA
     return pl.pallas_call(
         last_kernel,
-        in_specs=[vmem] * 7 + [hbm] * 3,
-        out_specs=[vmem, vmem, vmem, hbm, hbm],
+        in_specs=[vmem] * 5 + [hbm] * 5,
+        out_specs=[vmem, vmem, hbm, hbm, hbm, hbm],
         out_shape=[
             jax.ShapeDtypeStruct((count, width), F32),
             jax.ShapeDtypeStruct(pack, F32),
-            jax.ShapeDtypeStruct((count, width), BF),
             jax.ShapeDtypeStruct((2, 2, 2) + block, BF),
-            jax.ShapeDtypeStruct(cross.shape, BF),
+            jax.ShapeDtypeStruct((2, 2, 2) + small, BF),
+            jax.ShapeDtypeStruct(sum_rows.shape, BF),
+            jax.ShapeDtypeStruct(sum_down.shape, BF),
         ],
         scratch_shapes=[
             pltpu.VMEM((n, 2, 2) + block, BF),
             pltpu.VMEM((n + 1, 2, 2) + block, BF),
+            pltpu.VMEM((n, 2, 2) + small, BF),
+            pltpu.VMEM((n + 1, 2, 2) + small, BF),
             pltpu.VMEM((2, 2) + block, BF),
+            pltpu.VMEM((2, 2) + small, BF),
             pltpu.VMEM((n, 2, 2) + pack, F32),
             pltpu.VMEM((n, 2, 2) + pack, F32),
             pltpu.VMEM((n, 2) + pack, F32),
             pltpu.VMEM((n,) + pack, F32),
             pltpu.VMEM((n + 1,) + pack, F32),
+            pltpu.VMEM(hidden.shape, BF),
+            pltpu.VMEM((total, NST + HD), BF),
+            pltpu.VMEM((total, NST + HD), BF),
+            pltpu.VMEM((total, 256), BF),
+            pltpu.VMEM((total, 256), BF),
+            pltpu.VMEM((total, 128), BF),
+            pltpu.VMEM((total, 128), BF),
+            pltpu.VMEM((total, 256), BF),
             dma((2,)),
             dma((4, 2, 2, n)),
             dma((2, 2, n)),
+            dma((2, 2, n)),
             dma((2, 3)),
-            dma((2, 3)),
+            dma((2, 7)),
+            dma((2, 7)),
             dma((2, 4)),
-            dma((4,)),
-            dma((2,)),
+            dma((2, 2)),
+            dma((2, 4)),
+            dma((3,)),
         ]
-        + sum_scratch(count, width)
         + sum_scratch(count, width),
         compiler_params=pltpu.CompilerParams(
-            collective_id=3, has_side_effects=True, vmem_limit_bytes=60 * 1024 * 1024
+            collective_id=3, has_side_effects=True, vmem_limit_bytes=58 * 1024 * 1024
         ),
         name="last",
-    )(part, rows, gain, grad, little, down, middle, weight, slices, cross)
+    )(part, rows, gain, grad, little, weight, common, hidden, sum_rows, sum_down)
 
 
 def start_kernel(
-    rows_ref, little_ref, own_ref, blocks_ref, cot_ref,
-    hidden_ref, all_ref, shared_ref, weight_ref, incoming_ref,
-    block, little, hidden_sems, shared_sems, cot_sems, local, little_sems, line_sems, across_sems,
+    rows_ref, little_ref, own_ref, blocks_ref, units_ref, cot_ref,
+    hidden_ref, all_ref, weight_ref, unit_ref, incoming_ref,
+    block, little, hidden_sems, map_sems, kv_sems, cot_sems, local, little_sems, line_sems, across_sems,
 ):
     x, z, y, c = (lax.axis_index(a) for a in ("x", "z", "y", "c"))
     n = lax.axis_size("z")
+    width, count = blocks_ref.shape[3], rows_ref.shape[0]
+    own_maps, own_kv = own_ref.at[:, pl.ds(0, NST)], own_ref.at[:, pl.ds(NST, 2 * HD + 128)]
     greet_all()
-    width = own_ref.shape[1]
-
-    def shared_at(x, z, y, c):
-        cols = pl.ds(pl.multiple_of(x * width, 128), width)
-        return shared_ref.at[z, y, c, :, cols]
-
-    own_shared = pltpu.make_async_copy(own_ref, shared_at(x, z, y, c), local.at[0])
-    own_shared.start()
-    own_weight = pltpu.make_async_copy(blocks_ref.at[c, y], weight_ref.at[z, y, c], local.at[1])
-    own_weight.start()
-    own_cot = pltpu.make_async_copy(cot_ref, incoming_ref.at[y, c, x], local.at[3])
-    own_cot.start()
-
-    shared_line = line_item(lambda at: shared_at(x, at, y, c), line_sems.at[0], own_ref)
+
+    def map_cols(x):
+        return pl.ds(pl.multiple_of(width + x * NST, 128), NST)
+
+    kv_cols = pl.ds(width + 2 * NST, 2 * HD + 128)
+    in_cols = pl.ds(0, width)
+
+    def moves_of(blocks, place, base):
+        moves = []
+        for i, (dy, dc) in enumerate(((0, 1), (1, 0), (1, 1))):
+            where = {"y": (1 - y) if dy else y, "c": (1 - c) if dc else c}
+            move = pltpu.make_async_remote_copy(
+                src_ref=blocks.at[where["c"], where["y"]],
+                dst_ref=place(y, c),
+                send_sem=across_sems.at[0, base + i],
+                recv_sem=across_sems.at[1, base + i],
+                device_id=where,
+                device_id_type=pl.DeviceIdType.MESH,
+            )
+            move.start()
+            moves.append(move)
+        return moves
+
+    map_line = line_item(
+        lambda at: weight_ref.at[at, y, c, :, map_cols(x)], line_sems.at[0], own_maps
+    )
+    kv_line = line_item(lambda at: weight_ref.at[at, y, c, :, kv_cols], line_sems.at[6], own_kv)
     little_line = line_item(lambda at: little.at[at], line_sems.at[1])
-    shared_line[0](0)
-    little[z, y, c] = little_ref[...]
-    hop = remote(little.at[z, y, c], little.at[z, y, c], little_sems.at[0, 0], little_sems.at[1, 0], "c")
-    hop.start()
-
-    moves = []
-    for i, (dy, dc) in enumerate(((0, 1), (1, 0), (1, 1))):
-        where = {"y": (1 - y) if dy else y, "c": (1 - c) if dc else c}
-        src = blocks_ref.at[where["c"], where["y"]]
-        move = pltpu.make_async_remote_copy(
-            src_ref=src,
-            dst_ref=weight_ref.at[z, y, c],
-            send_sem=across_sems.at[0, i],
-            recv_sem=across_sems.at[1, i],
-            device_id=where,
-            device_id_type=pl.DeviceIdType.MESH,
-        )
-        move.start()
-        moves.append(move)
-
     lines = []
     for i, (dy, dc) in enumerate(((0, 0), (0, 1), (1, 0), (1, 1))):
         yy, cc = (1 - y) if dy else y, (1 - c) if dc else c
         lines.append(
             line_item(
-                lambda at, yy=yy, cc=cc: weight_ref.at[at, yy, cc],
+                lambda at, yy=yy, cc=cc: weight_ref.at[at, yy, cc, :, in_cols],
                 line_sems.at[2 + i],
                 blocks_ref.at[c, y] if i == 0 else None,
             )
         )
+
+    little[z, y, c] = little_ref[...]
+    hop = remote(
+        little.at[z, y, c], little.at[z, y, c], little_sems.at[0, 0], little_sems.at[1, 0], "c"
+    )
+    hop.start()
+    map_line[0](0)
+    kv_line[0](0)
+    hop.wait()
+    hop = remote(little.at[z, y], little.at[z, y], little_sems.at[0, 1], little_sems.at[1, 1], "y")
+    hop.start()
+    hop.wait()
+    little_line[0](0)
     lines[0][0](0)
-    hop.wait()
-    second = remote(little.at[z, y], little.at[z, y], little_sems.at[0, 1], little_sems.at[1, 1], "y")
-    second.start()
-    second.wait()
-    little_line[0](0)
-    for k in range(1, n):
-        shared_line[1](k - 1)
-        if k < n - 1:
-            shared_line[0](k)
-        little_line[1](k - 1)
-        if k < n - 1:
-            little_line[0](k)
-    for i in range(3):
-        moves[i].wait_recv()
-        lines[1 + i][0](0)
-
+    moves = moves_of(blocks_ref, lambda y, c: weight_ref.at[z, y, c, :, in_cols], 0)
+
+    owns = [
+        pltpu.make_async_copy(own_maps, weight_ref.at[z, y, c, :, map_cols(x)], local.at[0]),
+        pltpu.make_async_copy(own_kv, weight_ref.at[z, y, c, :, kv_cols], local.at[5]),
+        pltpu.make_async_copy(
+            blocks_ref.at[c, y], weight_ref.at[z, y, c, :, in_cols], local.at[1]
+        ),
+    ]
+    own_unit = pltpu.make_async_copy(units_ref.at[c, y], unit_ref.at[y, c], local.at[2])
+    own_cot = pltpu.make_async_copy(cot_ref, incoming_ref.at[y, c, x], local.at[3])
+    own_hidden = pltpu.make_async_copy(block, hidden_ref.at[y, c, x], local.at[4])
+    for copy in owns + [own_unit, own_cot]:
+        copy.start()
+
+    def half_rows(ref, i):
+        return ref.at[pl.ds(i * (count // 2), count // 2)]
+
+    cot_steps = gather_regions(
+        lambda x, y, c: incoming_ref.at[y, c, x], half_rows, cot_sems, own_cot.wait, cot_ref
+    )
+    hidden_steps = gather_regions(
+        lambda x, y, c: hidden_ref.at[y, c, x], half_rows, hidden_sems, own_hidden.wait, block
+    )
+    map_steps = gather_regions(
+        lambda x, y, c: weight_ref.at[:, y, c, :, map_cols(x)],
+        lambda ref, i: ref.at[pl.ds(i * (n // 2), n // 2)],
+        map_sems,
+        owns[0].wait,
+    )
+
+    def kv_copy(i, y, c, axis):
+        ref = weight_ref.at[:, y, c, :, kv_cols]
+        return remote(ref, ref, kv_sems.at[0, i], kv_sems.at[1, i], axis)
+
+    cot_steps[0]()
     rows = rows_ref[...].astype(F32)
     rows = rows * factor_of(rows)
+    for k in range(1, n):
+        for send, arrive, finish in (little_line, map_line, kv_line):
+            arrive(k - 1)
+            if k < n - 1:
+                send(k)
+
     piece = rows.shape[1] // (4 * n)
     gain = jnp.concatenate(
         [
@@ -984,72 +1141,68 @@
         axis=1,
     )
     block[...] = (rows * gain).astype(BF)
+    own_hidden.start()
+    hidden_steps[0]()
+    owns[1].wait()
+    kv_copy(0, y, c, "y").start()
+    kv_copy(1, y, c, "c").start()
+    map_steps[0]()
+    for i in range(3):
+        moves[i].wait_recv()
+        lines[1 + i][0](0)
     all_ref[...] = little[...]
-    count = rows.shape[0]
-    own_hidden = pltpu.make_async_copy(block, hidden_ref.at[y, c, x], local.at[2])
-    own_hidden.start()
-
-    hidden_steps = gather_regions(
-        lambda x, y, c: hidden_ref.at[y, c, x],
-        lambda ref, i: ref.at[pl.ds(i * (count // 2), count // 2)],
-        hidden_sems,
-        own_hidden.wait,
-        block,
-    )
-
-    def shared_region(x, y, c):
-        cols = pl.ds(pl.multiple_of(x * width, 128), width)
-        return shared_ref.at[:, y, c, :, cols]
-
-    shared_steps = gather_regions(
-        shared_region,
-        lambda ref, i: ref.at[pl.ds(i * (n // 2), n // 2)],
-        shared_sems,
-        own_shared.wait,
-    )
-    cot_steps = gather_regions(
-        lambda x, y, c: incoming_ref.at[y, c, x],
-        lambda ref, i: ref.at[pl.ds(i * (count // 2), count // 2)],
-        cot_sems,
-        own_cot.wait,
-        cot_ref,
-    )
-    hidden_steps[0]()
-    shared_steps[0]()
-    cot_steps[0]()
-    for k in range(1, n):
-        for send, arrive, finish in lines:
-            arrive(k - 1)
-            if k < n - 1:
-                send(k)
-        if k == 1:
-            hidden_steps[1]()
-            shared_steps[1]()
     cot_steps[1]()
+
+    def more(k):
+        if k < n:
+            for send, arrive, finish in lines:
+                arrive(k - 1)
+                if k < n - 1:
+                    send(k)
+
+    more(1)
+    hidden_steps[1]()
+    more(2)
+    kv_copy(0, 1 - y, c, "y").wait_recv()
+    kv_copy(2, 1 - y, c, "c").start()
+    map_steps[1]()
+    moves += moves_of(units_ref, lambda y, c: unit_ref.at[y, c], 3)
+    for k in range(3, n):
+        more(k)
+    cot_steps[2]()
     hidden_steps[2]()
-    shared_steps[2]()
-    cot_steps[2]()
-    own_weight.wait()
+    map_steps[2]()
+    kv_copy(1, y, 1 - c, "c").wait_recv()
+    kv_copy(2, 1 - y, 1 - c, "c").wait_recv()
+    kv_copy(0, y, c, "y").wait_send()
+    kv_copy(1, y, c, "c").wait_send()
+    kv_copy(2, 1 - y, c, "c").wait_send()
+    owns[2].wait()
+    own_unit.wait()
+    for move in moves[3:]:
+        move.wait_recv()
     for move in moves:
         move.wait_send()
-    for send, arrive, finish in [shared_line, little_line] + lines:
+    for send, arrive, finish in [map_line, kv_line, little_line] + lines:
         finish()
 
 
-def start_call(rows, little, own, blocks, cot):
-    n, parts = lax.axis_size("z"), blocks.shape
+def start_call(rows, little, own, blocks, units, cot):
+    n = lax.axis_size("z")
     count, width = rows.shape
     vmem, hbm = pl.BlockSpec(memory_space=pltpu.VMEM), pl.BlockSpec(memory_space=pl.ANY)
     dma = pltpu.SemaphoreType.DMA
     return pl.pallas_call(
         start_kernel,
-        in_specs=[vmem, vmem, hbm, hbm, hbm],
+        in_specs=[vmem, vmem, hbm, hbm, hbm, hbm],
         out_specs=[hbm, vmem, hbm, hbm, hbm],
         out_shape=[
             jax.ShapeDtypeStruct((2, 2, 2, count, width), BF),
             jax.ShapeDtypeStruct((n, 2, 2) + little.shape, F32),
-            jax.ShapeDtypeStruct((n, 2, 2, own.shape[0], 2 * own.shape[1]), BF),
-            jax.ShapeDtypeStruct((n, 2, 2) + parts[2:], BF),
+            jax.ShapeDtypeStruct(
+                (n, 2, 2, own.shape[0], blocks.shape[3] + own.shape[1] + NST), BF
+            ),
+            jax.ShapeDtypeStruct(units.shape, BF),
             jax.ShapeDtypeStruct((2, 2, 2, count, width), BF),
         ],
         scratch_shapes=[
@@ -1057,17 +1210,159 @@
             pltpu.VMEM((n, 2, 2) + little.shape, F32),
             dma((2, 8)),
             dma((2, 8)),
+            dma((2, 3)),
             dma((2, 8)),
-            dma((4,)),
+            dma((6,)),
             dma((2, 2)),
-            dma((6, 2, 2, n - 1)),
-            dma((2, 3)),
+            dma((7, 2, 2, n - 1)),
+            dma((2, 6)),
         ],
         compiler_params=pltpu.CompilerParams(
             collective_id=0, has_side_effects=True, vmem_limit_bytes=VMEM
         ),
         name="start",
-    )(rows, little, own, blocks, cot)
+    )(rows, little, own, blocks, units, cot)
+
+
+def prepare_kernel(
+    query_ref, key_ref, value_ref, mamba_ref, gate_ref, up_ref, own_ref, blocks_ref, units_ref
+):
+    x, n = lax.axis_index("x"), lax.axis_size("z")
+    inner = MH * MP
+    wide = inner // PARTS
+
+    def half(ref, start, width, at, count):
+        return ref[:, pl.ds(pl.multiple_of(start + x * width + at, 128), count)]
+
+    own_ref[:, :NST] = half(mamba_ref, 2 * inner, NST, 0, NST)
+    own_ref[:, NST : NST + HD] = half(key_ref, 0, HD, 0, HD)
+    own_ref[:, NST + HD : NST + 2 * HD] = half(value_ref, 0, HD, 0, HD)
+    steps = mamba_ref[:, 2 * inner + 2 * NST :].astype(F32)
+    steps = jnp.where(x == 0, steps[:, : MH // 2], steps[:, MH // 2 :])
+    rest = jnp.zeros((steps.shape[0], 128 - MH // 2), F32)
+    own_ref[:, NST + 2 * HD :] = jnp.concatenate([steps, rest], axis=1).astype(BF)
+    for c in (0, 1):
+        for y in (0, 1):
+            j = 2 * c + y
+            blocks_ref[c, y, :, :wide] = half(mamba_ref, 0, inner // 2, j * wide, wide)
+            blocks_ref[c, y, :, wide : 2 * wide] = half(
+                mamba_ref, inner, inner // 2, j * wide, wide
+            )
+            blocks_ref[c, y, :, 2 * wide :] = half(query_ref, 0, 4 * HD, j * HD, HD)
+    unit = units_ref.shape[3] // 2 // n
+    for at, ref in enumerate((gate_ref, up_ref)):
+        for z in range(n):
+            for y in (0, 1):
+                for c in (0, 1):
+                    first = ((z * 2 + y) * 2 + c) * 2 * unit
+                    into = pl.ds((at * n + z) * unit, unit)
+                    units_ref[c, y, :, into] = half(ref, first, unit, 0, unit)
+
+
+def prepare(query, key, value, mamba, gate, up):
+    rows, wide = query.shape[0], MH * MP // PARTS
+    vmem = pl.BlockSpec(memory_space=pltpu.VMEM)
+    return pl.pallas_call(
+        prepare_kernel,
+        in_specs=[vmem] * 6,
+        out_specs=[vmem] * 3,
+        out_shape=[
+            jax.ShapeDtypeStruct((rows, NST + 2 * HD + 128), BF),
+            jax.ShapeDtypeStruct((2, 2, rows, 2 * wide + HD), BF),
+            jax.ShapeDtypeStruct((2, 2, rows, 2 * gate.shape[1] // PARTS), BF),
+        ],
+        compiler_params=pltpu.CompilerParams(vmem_limit_bytes=VMEM),
+        name="prepare",
+    )(query, key, value, mamba, gate, up)
+
+
+def units_kernel(own_ref, across_ref, gate_ref, up_ref):
+    x, n = lax.axis_index("x"), lax.axis_size("z")
+    unit = own_ref.shape[3] // 2 // n
+    for at, ref in enumerate((gate_ref, up_ref)):
+        for z in range(n):
+            cols = pl.ds((at * n + z) * unit, unit)
+            pieces = []
+            for y in (0, 1):
+                for c in (0, 1):
+                    own, other = own_ref[c, y, :, cols], across_ref[c, y, :, cols]
+                    pieces += [jnp.where(x == 0, own, other), jnp.where(x == 0, other, own)]
+            ref[:, 8 * unit * z : 8 * unit * (z + 1)] = jnp.concatenate(
+                [p.astype(F32) for p in pieces], axis=1
+            )
+
+
+def units_call(own, across):
+    vmem = pl.BlockSpec(memory_space=pltpu.VMEM)
+    shape = jax.ShapeDtypeStruct((own.shape[2], PARTS * own.shape[3] // 2), F32)
+    return pl.pallas_call(
+        units_kernel,
+        in_specs=[vmem] * 2,
+        out_specs=[vmem] * 2,
+        out_shape=[shape, shape],
+        compiler_params=pltpu.CompilerParams(vmem_limit_bytes=VMEM),
+        name="units",
+    )(own, across)
+
+
+def finish_kernel(
+    got_ref, few_ref, own_ref, across_ref, own_down, across_down,
+    query_ref, key_ref, value_ref, mamba_ref, out_ref, attn_ref, down_ref,
+):
+    x = lax.axis_index("x")
+    inner = MH * MP
+    wide = inner // PARTS
+    steps = []
+    for xx in (0, 1):
+        total = 0.0
+        for c in (0, 1):
+            for y in (0, 1):
+                j = 4 * xx + 2 * c + y
+                block = got_ref[xx, c, y].astype(F32)
+                mamba_ref[:, j * wide : (j + 1) * wide] = block[:, :wide]
+                mamba_ref[:, inner + j * wide : inner + (j + 1) * wide] = block[:, wide : 2 * wide]
+                query_ref[:, j * HD : (j + 1) * HD] = block[:, 2 * wide : 2 * wide + HD]
+                total = total + few_ref[xx, c, y, :, 128:].astype(F32)
+        steps.append(total[:, : MH // 2])
+    def pair(first, second, start, width):
+        return jnp.concatenate([v[:, start : start + width].astype(F32) for v in (first, second)], axis=1)
+
+    for xx in (0, 1):
+        cols = slice(xx * HD, (xx + 1) * HD)
+        key_ref[:, cols] = pair(few_ref[xx, 0, 0], few_ref[xx, 0, 1], 0, HD // 2)
+        value_ref[:, cols] = pair(few_ref[xx, 1, 0], few_ref[xx, 1, 1], 0, HD // 2)
+    for c in (0, 1):
+        for y in (0, 1):
+            first = 2 * inner + (2 * c + y) * (NST // 2)
+            mamba_ref[:, first : first + NST // 2] = pair(
+                few_ref[0, c, y], few_ref[1, c, y], HD // 2, NST // 4
+            )
+    mamba_ref[:, 2 * inner + 2 * NST :] = jnp.concatenate(steps, axis=1)
+
+    own, across = own_ref[...], across_ref[...]
+    sides = [jnp.where(x == 0, own, across), jnp.where(x == 0, across, own)]
+    half, first = own.shape[1], out_ref.shape[0]
+    second = first + attn_ref.shape[0]
+    units = down_ref.shape[0] // 2
+    for xx in (0, 1):
+        side = sides[xx].astype(F32)
+        cols = slice(xx * half, (xx + 1) * half)
+        out_ref[:, cols] = side[:first]
+        attn_ref[:, cols] = side[first:second]
+        mine = own_down[...].astype(F32), across_down[...].astype(F32)
+        down_ref[xx * units : (xx + 1) * units] = jnp.where(x == xx, *mine)
+
+
+def finish_call(got, few, own, across, own_down, across_down, shapes):
+    vmem = pl.BlockSpec(memory_space=pltpu.VMEM)
+    return pl.pallas_call(
+        finish_kernel,
+        in_specs=[vmem] * 6,
+        out_specs=[vmem] * 7,
+        out_shape=[jax.ShapeDtypeStruct(v, F32) for v in shapes],
+        compiler_params=pltpu.CompilerParams(vmem_limit_bytes=VMEM),
+        name="finish",
+    )(got, few, own, across, own_down, across_down)
 
 
 def flip(value, *axes):
@@ -1082,20 +1377,10 @@
     return jnp.where(second, other, own), jnp.where(second, own, other)
 
 
-def column_halves(values, axis):
+def halves_of(value, axis, dim):
     at = lax.axis_index(axis)
-    halves = [v.shape[1] // 2 for v in values]
-    kept = [lax.dynamic_slice_in_dim(v, at * h, h, 1) for v, h in zip(values, halves)]
-    away = [lax.dynamic_slice_in_dim(v, (1 - at) * h, h, 1) for v, h in zip(values, halves)]
-    return kept, jnp.concatenate([v.astype(BF) for v in away], axis=1)
-
-
-def column_added(kept, got):
-    sums, at = [], 0
-    for v in kept:
-        sums.append(v.astype(F32) + got[:, at : at + v.shape[1]].astype(F32))
-        at += v.shape[1]
-    return sums
+    kept = lax.dynamic_index_in_dim(value, at, dim, keepdims=False)
+    return kept, lax.dynamic_index_in_dim(value, 1 - at, dim, keepdims=False).astype(BF)
 
 
 def part_index():
@@ -1107,94 +1392,85 @@
     return lax.dynamic_slice_in_dim(weight, lax.axis_index("x") * half, half, 1)
 
 
-def exchange(blocks, high, low):
+def exchange_blocks(blocks, high, low):
     h, l = lax.axis_index(high), lax.axis_index(low)
-
-    def block(dh, dl):
-        return lax.dynamic_index_in_dim(blocks, 2 * (h ^ dh) + (l ^ dl), 0, keepdims=False)
-
-    own, by_low = block(0, 0), flip(block(0, 1), low)
-    by_high, by_both = flip(block(1, 0), high), flip(block(1, 1), high, low)
+    return [
+        lax.dynamic_index_in_dim(blocks, 2 * (h ^ dh) + (l ^ dl), 0, keepdims=False)
+        for dh in (0, 1)
+        for dl in (0, 1)
+    ]
+
+
+def exchanged(blocks, high, low, late):
+    own, for_low, for_high, for_both = blocks
+    got = [flip(for_low, low), flip(for_high, high), flip(for_both, high, low)]
+    by_low, by_high, by_both = after(got, late)
     near, far = ordered(own, by_low, low), ordered(by_high, by_both, low)
     first, second = ordered(near[0], far[0], high), ordered(near[1], far[1], high)
     return [[first[0], second[0]], [first[1], second[1]]]
 
 
-def fetch_units(weights):
-    rows, n = weights[0].shape[0], lax.axis_size("z")
-    blocks = []
+def sum_blocks(part):
+    rows = part.shape[0] // 4
+    y, c = lax.axis_index("y"), lax.axis_index("c")
+    return [
+        lax.dynamic_slice_in_dim(part, (2 * (y ^ dy) + (c ^ dc)) * rows, rows, 0)
+        for dc in (0, 1)
+        for dy in (0, 1)
+    ]
+
+
+def whole_rows(weights):
+    parts = []
     for w in weights:
-        units = w.reshape(rows, n, 2, 2, 2, -1)
-        units = lax.dynamic_index_in_dim(units, lax.axis_index("x"), 4, keepdims=False)
-        blocks.append(units.transpose(3, 2, 0, 1, 4).reshape(4, rows, -1))
-    got = exchange(jnp.concatenate(blocks, axis=2), "c", "y")
-    moved = jnp.concatenate([got[0][0], got[1][0], got[0][1], got[1][1]])
-    return lax.all_gather(moved, "z", axis=0, tiled=True)
-
-
-def exchange_units(part):
-    rows = part.shape[0] // 4
-    part = part.reshape(2, 2, rows, -1).transpose(1, 0, 2, 3).reshape(4, rows, -1)
-    return jnp.stack([jnp.stack(g) for g in exchange(part, "c", "y")])
-
-
-def unit_shards(own, across, count):
-    n, rows = lax.axis_size("z"), own.shape[2]
-    whole = jnp.stack(ordered(own, across, "x"))
-    whole = whole.reshape(2, 2, 2, rows, count, n, -1).transpose(4, 3, 5, 2, 1, 0, 6)
-    return [whole[i].reshape(rows, -1).astype(F32) for i in range(count)]
-
-
-def fetch_rows(weight):
-    if lax.axis_size("z") != 4:
-        whole = lax.all_gather(weight, FSDP, axis=0, tiled=True)
+        whole = lax.all_gather(w, FSDP, axis=0, tiled=True)
         rows = whole.shape[0] // PARTS
-        return lax.dynamic_slice_in_dim(whole, part_index() * rows, rows, 0)
-    got = exchange(lax.all_gather(half_columns(weight), "z", axis=0, tiled=False), "x", "c")
-    return jnp.concatenate(
-        [jnp.concatenate([got[0][c], got[1][c]], axis=1) for c in (0, 1)], axis=0
-    )
-
-
-def fetch_rows_of(weights):
-    if lax.axis_size("z") != 4:
-        return jnp.concatenate([fetch_rows(w) for w in weights])
-    pieces = [w.shape[0] for w in weights]
-    whole, outs, at = fetch_rows(jnp.concatenate(weights)), [], 0
-    whole = whole.reshape(2, sum(pieces), -1)
+        parts.append(lax.dynamic_slice_in_dim(whole, part_index() * rows, rows, 0))
+    return jnp.concatenate(parts)
+
+
+def joined_rows(got, pieces):
+    whole = jnp.stack([jnp.concatenate([got[0][c], got[1][c]], axis=1) for c in (0, 1)])
+    outs, at = [], 0
     for count in pieces:
         outs.append(whole[:, at : at + count].reshape(2 * count, -1))
         at += count
     return jnp.concatenate(outs)
 
 
-def rows_moved(grad, pieces):
-    cols = grad.shape[1] // 2
-    splits = [grad[sum(pieces[:i]) : sum(pieces[: i + 1])].astype(BF) for i in range(len(pieces))]
+def rows_blocks(grad, pieces):
+    cols, grad = grad.shape[1] // 2, grad.astype(BF)
     if lax.axis_size("z") != 4:
         parts = []
-        for g in splits:
-            whole = jnp.zeros((g.shape[0] * PARTS, 2 * cols), BF)
+        for i, count in enumerate(pieces):
+            g = grad[sum(pieces[:i]) : sum(pieces[: i + 1])]
+            whole = jnp.zeros((count * PARTS, 2 * cols), BF)
             parts.append(
                 lax.dynamic_update_slice_in_dim(whole, g, part_index() * g.shape[0], 0)
             )
         return parts
-    halves = jnp.concatenate([g.reshape(2, g.shape[0] // 2, -1) for g in splits], axis=1)
-    block = halves.reshape(2, -1, 2, cols).transpose(2, 0, 1, 3)
-    got = exchange(block.reshape(4, -1, cols), "x", "c")
-    return jnp.stack([got[0][0], got[0][1], got[1][0], got[1][1]])
-
-
-def rows_sum(moved, down):
-    n, width = lax.axis_size("z"), down.shape[1] // 2
-    down = down.reshape(n, -1, 2, width).transpose(0, 2, 1, 3).reshape(n, -1, width)
-    if n != 4:
+    x, c = lax.axis_index("x"), lax.axis_index("c")
+    blocks = []
+    for dx in (0, 1):
+        for dc in (0, 1):
+            block, at = [], 0
+            for count in pieces:
+                start = (at + (c ^ dc) * (count // 2), (x ^ dx) * cols)
+                block.append(lax.dynamic_slice(grad, start, (count // 2, cols)))
+                at += count
+            blocks.append(jnp.concatenate(block))
+    return blocks
+
+
+def rows_sum(moved):
+    if lax.axis_size("z") != 4:
         parts = []
         for whole in moved:
             part = lax.psum_scatter(whole, FSDP, scatter_dimension=0, tiled=True)
             parts.append(half_columns(lax.psum(part, "x")))
-        return jnp.concatenate(parts + [lax.psum_scatter(down, "z")])
-    return lax.psum_scatter(jnp.concatenate([moved, down], axis=1), "z")
+        return jnp.concatenate(parts)
+    moved = jnp.stack([moved[0][0], moved[0][1], moved[1][0], moved[1][1]])
+    return lax.psum_scatter(moved, "z")
 
 
 def after(value, earlier):
@@ -1243,41 +1519,25 @@
     smalls = [ffn_gain, mamba_gain, conv_bias, conv_weight]
     little = packed(mixer_gain[None].astype(F32), [v[None].astype(F32) for v in smalls])[0]
     count = query_weight.shape[0]
-    kvh = HD * lax.axis_index("x")
-    map_weight, step_weight = mamba_in_weight[:, 2 * inner : 2 * inner + 2 * NST], mamba_in_weight[:, 2 * inner + 2 * NST :]
-    own = jnp.concatenate(
-        [
-            half_columns(map_weight),
-            lax.dynamic_slice_in_dim(key_weight, kvh, HD, 1),
-            lax.dynamic_slice_in_dim(value_weight, kvh, HD, 1),
-            jnp.pad(half_columns(step_weight), ((0, 0), (0, 128 - MH // 2))),
-        ],
-        axis=1,
-    )
-    blocks = [mamba_in_weight[:, :inner], mamba_in_weight[:, inner : 2 * inner], query_weight]
-    blocks = [half_columns(w).reshape(count, 2, 2, -1) for w in blocks]
-    blocks = jnp.concatenate(blocks, axis=3).transpose(1, 2, 0, 3)
+    own, blocks, units = prepare(
+        query_weight, key_weight, value_weight, mamba_in_weight, gate_weight, up_weight
+    )
     token_rows = tokens.reshape(token_count, model_dim)
     grad_rows = cotangent.reshape(token_count, model_dim)
-    hidden, gathered_little, shared, w_in, incoming = start_call(
-        token_rows, little, own, blocks, grad_rows
+    hidden, gathered_little, w_in, units, incoming = start_call(
+        token_rows, little, own, blocks, units, grad_rows
     )
     hidden = hidden.reshape(rows, model_dim)
     incoming = incoming.reshape(rows, model_dim)
     w_in = w_in.reshape(model_dim, -1)
-    shared = shared.reshape(model_dim, -1)
-    share = shared.shape[1] // 2
-    shared = jnp.concatenate(
-        [
-            shared[:, :NST],
-            shared[:, share : share + NST],
-            lax.dynamic_slice_in_dim(shared, lax.axis_index("x") * share + NST, share - NST, 1),
-        ],
-        axis=1,
-    )
-    w_out = fetch_rows_of([attn_out_weight, mamba_out_weight])
-    w_attn_out, w_mamba_out = w_out[:HD], w_out[HD:]
-    w_gateup = fetch_units(after((gate_weight, up_weight), hidden))
+    fast = lax.axis_size("z") == 4
+    out_weights = [mamba_out_weight, attn_out_weight]
+    out_pieces = [w.shape[0] for w in out_weights]
+    if fast:
+        out_blocks = half_columns(jnp.concatenate(out_weights))
+        out_blocks = lax.all_gather(out_blocks, "z", axis=0, tiled=False)
+        out_blocks = exchange_blocks(out_blocks, "x", "c")
+    w_gateup = lax.all_gather(units.reshape(4 * count, -1), "z", axis=0, tiled=True)
     down_half = down_weight.reshape(2, -1, model_dim)
     down_half = lax.dynamic_index_in_dim(down_half, lax.axis_index("x"), 0, keepdims=False)
     ff = gate_weight.shape[1] // PARTS
@@ -1306,18 +1566,18 @@
     ]
     tables = rope_tables(length, HD)
 
-    projected = mm(hidden, w_in)
-    common = mm(hidden, shared).astype(BF)
-    scanned, gated, squares, attended = mixer_forward(
-        seqs, length, projected, common, params, tables
-    )
-
+    projected = mm(after(hidden, out_blocks) if fast else hidden, w_in)
+    scanned, gated, squares, attended = mixer_forward(seqs, length, projected, params, tables)
+
+    if fast:
+        w_out = joined_rows(exchanged(out_blocks, "x", "c", squares), out_pieces)
+    else:
+        w_out = whole_rows(out_weights)
     squares = plane_total(squares.reshape(-1, 128), 4)
     factor = lax.rsqrt(squares / inner + EPSILON).reshape(rows, 1)
     normal = gated * factor
     normed = (normal * gain_mamba).astype(BF)
-    mixed = jnp.concatenate([attended, normed], axis=1)
-    w_out = jnp.concatenate([w_attn_out, w_mamba_out], axis=0)
+    mixed = jnp.concatenate([normed, attended], axis=1)
     block = (2, 2, 2, token_count, model_dim)
     mixer_sum = mm(mixed, w_out).astype(BF).reshape(block)
     second, middle, w_down = middle_calls(mixer_sum, token_rows, gain_ffn[None], down_half)
@@ -1339,40 +1599,60 @@
         grad_second, middle, gain_ffn[None], cot=grad_rows
     )
     grad_mixer = grad_mixer.reshape(rows, model_dim)
-    grad_out = outer_product(mixed, grad_mixer)
-    moved_out = rows_moved(grad_out, [HD, wide])
-    grad_mixer, active = after((grad_mixer, active), grad_out)
-    grad_down = outer_product(active, incoming).astype(BF)
-    grad_mixer, active = after((grad_mixer, active), grad_down)
-    sum_rows = rows_sum(moved_out, grad_down)
-    grad_att = across(grad_mixer, w_attn_out).astype(BF)
-    grad_normed = across(grad_mixer, w_mamba_out)
+    grad_mixed = across(grad_mixer, w_out)
+    grad_normed = grad_mixed[:, :wide]
     grad_gain_mamba = jnp.sum(grad_normed * normal, axis=0)
     scaled = grad_normed * gain_mamba
-    dots = jnp.sum(scaled * normal, axis=-1).reshape(-1, 128)
-    if isinstance(moved_out, jax.Array):
-        dots = after(dots, moved_out)
-    dots = plane_total(dots, 5).reshape(rows, 1) / inner
-    grad_in, grad_common, gxk, gxb, gmk, gmb, gheads = mixer_backward(
-        seqs, length, projected, common, params, tables, scanned, grad_normed, gain_mamba[None],
-        factor, dots, grad_att,
-    )
-    shares = [grad_common[:, : 2 * NST], grad_common[:, 2 * NST : 2 * NST + 2 * HD]]
-    kept, away = column_halves(shares, "c")
-    grad_hidden = across(after(grad_in, away), w_in)
-    shares = column_added(kept, flip(away, "c"))
-    kept, away = column_halves(shares, "y")
-    grad_hidden = grad_hidden + across(after(grad_common, away), shared)
-    grad_hidden = grad_hidden.astype(BF).reshape(block)
-    shares = column_added(kept, flip(away, "y"))
-    kept, away = column_halves(shares[:1], "x")
-    grad_win = outer_product(hidden, after(grad_in, (away, grad_hidden))).astype(BF)
+    dots = plane_total(jnp.sum(scaled * normal, axis=-1).reshape(-1, 128), 5)
+    grad_mixer, active, sum_gateup = after((grad_mixer, active, sum_gateup), dots)
+    grad_out = outer_product(mixed, grad_mixer)
+    row_blocks = rows_blocks(grad_out, [wide, HD])
+    active = after(active, row_blocks)
+    sides = active.reshape(2, 2, 2 * token_count, ff)
+    result_kept, result_away = (
+        mm(v, w_down).astype(BF).reshape(2, 2, token_count, model_dim)
+        for v in halves_of(sides, "c", 1)
+    )
+    result_got = flip(result_away, "c")
+    grad_down = outer_product(after(active, result_away), incoming).astype(BF)
+    sum_down = lax.psum_scatter(
+        grad_down.reshape(-1, ff // lax.axis_size("z"), model_dim), "z"
+    )
+    gateup_blocks = sum_blocks(sum_gateup)
+    dots = after(dots, (gateup_blocks, grad_down))
+    row_sums = exchanged(row_blocks, "x", "c", dots) if fast else row_blocks
+    result_got = after(result_got, dots)
+    half = model_dim // 2
+    lefts = [halves_of(v[..., :half], "y", 0) for v in (result_kept, result_got)]
+    rights = [halves_of(v[..., half:], "x", 1) for v in (result_kept, result_got)]
+    left, right = ((a[1].astype(F32) + b[1].astype(F32)).astype(BF) for a, b in (lefts, rights))
+    dots = after(dots, (left, right)).reshape(rows, 1) / inner
+
+    grad_in, gxk, gxb, gmk, gmb, gheads = mixer_backward(
+        seqs, length, projected, params, tables, scanned, grad_mixed, gain_mamba[None], factor, dots
+    )
+    sum_rows = rows_sum(after(row_sums, grad_in))
+    moved = exchanged(gateup_blocks, "c", "y", grad_in)
+    moved = jnp.stack([jnp.stack(g) for g in moved])
+    moved_across = flip(moved, "x")
+    left, right = after((flip(left, "y"), flip(right, "x")), grad_in)
+    lefts = [halves_of(v, "x", 0) for v in (lefts[0][0], lefts[1][0], left)]
+    rights = [halves_of(v, "y", 0) for v in (rights[0][0], rights[1][0], right)]
+
+    def three(values, index):
+        return sum(v[index].astype(F32) for v in values)
+
+    left, right = three(lefts, 1).astype(BF), three(rights, 1).astype(BF)
+    grad_in = after(grad_in, (moved, left, right))
+    grad_hidden = across(grad_in, w_in).astype(BF).reshape(block)
+    grad_win = outer_product(hidden, grad_in[:, : 2 * wide + HD]).astype(BF)
     grad_win = grad_win.reshape(-1, 2, 2, count, grad_win.shape[1])
-    shares = [shares[1]] + column_added(kept, flip(away, "x"))
-    slices = [v.astype(BF) for v in shares] + [grad_common[:, 2 * NST + 2 * HD :]]
-    grad_slices = outer_product(hidden, jnp.concatenate(slices, axis=1)).astype(BF)
-    grad_slices = grad_slices.reshape(-1, 2, 2, count, grad_slices.shape[1])
-    result = mm(active, w_down).astype(BF).reshape(block)
+    left, right = after((flip(left, "x"), flip(right, "y")), grad_win)
+    result = jnp.concatenate(
+        [three(lefts, 0) + left.astype(F32), three(rights, 0) + right.astype(F32)], axis=1
+    )
+    output = (middle + result).astype(BF).reshape(1, token_count, model_dim)
+    shard_gate, shard_up = units_call(moved, after(moved_across, grad_win))
 
     conv_grad = jnp.zeros((4, channels), F32)
     conv_grad = lax.dynamic_update_slice_in_dim(conv_grad, gxk, part * wide, 1)
@@ -1392,15 +1672,10 @@
     little.append(jnp.broadcast_to(head_grad.reshape(1, -1), (fsdp, 3 * MH)))
     little = packed(jnp.zeros((fsdp, count), F32), little)
     little = little.reshape((-1, 2, 2) + little.shape[1:])
-    moved = exchange_units(sum_gateup)
-    moved = after(moved, grad_in)
-    moved_across = flip(moved, "x")
-    grad_hidden = after(grad_hidden, moved_across)
-    tokens_grad, total, output, got_in, rows_across = last_call(
-        grad_hidden, token_rows, gain_in[None], grad_middle, little, result, middle, grad_win,
-        grad_slices, sum_rows,
-    )
-    output = output.reshape(1, token_count, model_dim)
+    tokens_grad, total, got_in, got_few, rows_across, down_across = last_call(
+        grad_hidden, token_rows, gain_in[None], grad_middle, little, grad_win, grad_in, hidden,
+        sum_rows, sum_down,
+    )
     tokens_grad = tokens_grad.reshape(1, token_count, model_dim)
     total = total.reshape(-1)
     got, at = [total[:count]], 128
@@ -1408,31 +1683,13 @@
         got.append(total[at : at + like.size].reshape(like.shape))
         at += like.size
 
-    shard_gate, shard_up = unit_shards(moved, moved_across, 2)
-    low, high = ordered(sum_rows, rows_across, "x")
-    out_rows = sum_rows.shape[0] - ff // lax.axis_size("z") * model_dim // sum_rows.shape[1]
-    shard_out = jnp.concatenate([low[:out_rows], high[:out_rows]], axis=1).astype(F32)
-    shard_attn_out = shard_out[: attn_out_weight.shape[0]]
-    shard_mamba_out = shard_out[attn_out_weight.shape[0] :]
-    shard_down = jnp.concatenate([low[out_rows:], high[out_rows:]]).astype(F32)
-    shard_down = shard_down.reshape(2, 2, -1, model_dim // 2).transpose(0, 2, 1, 3)
-    shard_down = shard_down.reshape(-1, model_dim)
-
-    def columns(first, width):
-        return got_in[..., first : first + width]
-
-    def by_part(first, width):
-        return columns(first, width).transpose(3, 0, 1, 2, 4).reshape(count, -1)
-
-    at = HD + 2 * wide
-    kv = columns(at, HD // 2).transpose(1, 3, 0, 2, 4)
-    mapped = columns(at + HD // 2, NST // 4).transpose(3, 1, 2, 0, 4).reshape(count, -1)
-    stepped = columns(at + HD // 2 + NST // 4, MH // 2).astype(F32).sum(axis=(1, 2))
-    stepped = stepped.transpose(1, 0, 2).reshape(count, -1)
-    shard_query = by_part(2 * wide, HD).astype(F32)
-    shard_key, shard_value = (kv[i].reshape(count, -1).astype(F32) for i in (0, 1))
-    shard_mamba_in = jnp.concatenate(
-        [v.astype(F32) for v in (by_part(0, wide), by_part(wide, wide), mapped, stepped)], axis=1
+    weights = [query_weight, key_weight, value_weight, mamba_in_weight]
+    weights += [mamba_out_weight, attn_out_weight, down_weight]
+    (
+        shard_query, shard_key, shard_value, shard_mamba_in,
+        shard_mamba_out, shard_attn_out, shard_down,
+    ) = finish_call(
+        got_in, got_few, sum_rows, rows_across, sum_down, down_across, [w.shape for w in weights]
     )
 
     return (

time: 840 us -> 721 us (0.86)
  waiting for transfers between devices: 54.1 us -> 15.1 us
  local copies, waits for them, and re-layouts: 101 us -> 66.3 us
  Pallas kernels: 474 us -> 452 us
  other arithmetic: 45.8 us -> 30.5 us
  matrix products: 130 us -> 119 us
    ppermute x16 -> x15, waiting for transfers between devices: 54 us -> 10.4 us  [flip(): return lax.ppermute(value, axes, pairs)]
    pallas_call x2 -> x5, Pallas kernels: 271 us -> 247 us  [the longest x1 120 us: last_call(): pl.pallas_call(last_kernel, in_specs=[vmem] * 5 + [hbm] * 5, out_specs=[v...]
    slice x19 -> x2, local copies, waits for them, and re-layouts: 14.3 us -> 2.62 us  [shards(): v[..., half:]]
    concatenate x10 -> x4, other arithmetic: 13.4 us -> 4.41 us  [the longest x3 2.48 us: rows_blocks(): blocks.append(jnp.concatenate(block))]
    reshape x6 -> x1, local copies, waits for them, and re-layouts: 12.2 us -> 3.59 us  [shards(): sides = active.reshape(2, 2, 2 * token_count, ff)]
    dot_general x6 -> x4, matrix products: 51.6 us -> 44.6 us  [across(): lax.dot_general(left, right, (((1,), (1,)), ((), ())), preferred_element_...]
    dot_general x5 -> x4, matrix products: 37.4 us -> 32.3 us  [outer_product(): lax.dot_general(left, right, (((0,), (0,)), ((), ())), preferred_element_...]
    unnamed x164 -> x160, local copies, waits for them, and re-layouts: 25.3 us -> 26.1 us
  transfers between devices with their start and end apart: 20 -> 20, of which waited for: 7 -> 3; matrix products, arithmetic and copies ran while one was open for 23% -> 18% of each run, Pallas kernels for 40% -> 46%
where the time goes in v3:
time: 721 us; the launch traced here: 712 us
  Pallas kernels  452 us (63%)
  matrix products  119 us (17%)
  local copies, waits for them, and re-layouts  66.3 us (9%)
  other arithmetic  30.5 us (4%)
  between operations  15.4 us (2%)
  waiting for transfers between devices  15.1 us (2%)
  starting transfers between devices  14.2 us (2%)
    pallas_call x2, Pallas kernels, middle_calls(): pl.pallas_call(middle_kernel if cot is None else middle_back_kernel, in_s...  139 us
    pallas_call x1, Pallas kernels, last_call(): pl.pallas_call(last_kernel, in_specs=[vmem] * 5 + [hbm] * 5, out_specs=[v...  120 us
    pallas_call x1, Pallas kernels, start_call(): pl.pallas_call(start_kernel, in_specs=[vmem, vmem, hbm, hbm, hbm, hbm], o...  119 us
    dot_general x4, matrix products, across(): lax.dot_general(left, right, (((1,), (1,)), ((), ())), preferred_element_...  44.6 us
    dot_general x5, matrix products, mm(): return jnp.dot(left, right, preferred_element_type=F32)  41.7 us
    pallas_call x1, Pallas kernels, mixer_backward(): pl.pallas_call(mixer_back_kernel, grid=(seqs,), in_specs=mixer_specs(leng...  34.3 us
    dot_general x4, matrix products, outer_product(): lax.dot_general(left, right, (((0,), (0,)), ((), ())), preferred_element_...  32.3 us
    unnamed x160, local copies, waits for them, and re-layouts  26.1 us
  transfers between devices with their start and end apart: 20, of which 3 were waited for; matrix products, arithmetic and copies ran while one was open for 18% of the time, Pallas kernels for 46%

profile of v3, /device:TPU:0, one launch (start us, length us, event | category | flops | bytes accessed | tf_op | source)
XLA Modules:
  0.0 711.6 jit_solution(16308304398688897366)
XLA Ops:
  19.9 119.0 %start.1 = (bf16[2,2,2,192,2048]{4,3,2,1,0:T(8,128)(2,1)}, f32[4,2,2,16,128]{4,3,2,1,0:T(8,128)S(1)}, bf16[4,2,2,128,1792]{4,3,2,1,0:T(8,128)(2,1)}, bf16[2,2,12...) custom-call(bf16[192,2048]{1,0:T(8,128)(2,1)S(1)} %bitcast.160, f32[16,128]{1,0:T(8,128)S(1)} %bitcast.174, ...), custom_call_target="tpu_custom_call" | custom-call | tf_op jit(solution)/shard_map/start/pallas_call | solution.py:1195
  152.4 17.4 %fusion.32.x_ref.m0_ref.m1_ref.m2_ref.m3_ref.s_ref.z_ref.q_ref.k_ref.v_ref = f32[1536,1792]{1,0:T(8,128)} fusion(bf16[1536,2048]{1,0:T(8,128)(2,1)} %bitcast.184, bf16[2048,1792]{1,0:T(8,128)(2,1)} %bitcast.225), kind=kOutput, calls=%fused_computation.133 | convolution fusion | flops 11274289152 | bytes 24641536 | tf_op jit(solution)/shard_map/dot_general | solution.py:29
  169.9 14.7 %mixer.1 = (bf16[1536,384]{1,0:T(8,128)(2,1)S(1)}, f32[1536,384]{1,0:T(8,128)S(1)}, f32[1536,1]{1,0:T(8,128)S(1)}, bf16[1536,128]{1,0:T(8,128)(2,1)S(1)}) custom-call(f32[1536,1792]{1,0:T(8,128)} %fusion.32.x_ref.m0_ref.m1_ref.m2_ref.m3_ref.s_ref.z_ref.q_ref.k_ref.v_ref, f32[1536,1792]{1,0:T(8,128)} %fusion.32.x_ref.m0_ref.m1_ref.m2_ref.m3_ref.s_ref.z_ref.q_ref.k_ref.v_ref, ...), custom_call_target="tpu_custom_call" | custom-call | tf_op jit(solution)/shard_map/mixer/pallas_call | solution.py:293
  189.2 9.0 %total.2 = f32[12,128]{1,0:T(8,128)} custom-call(f32[12,128]{1,0:T(8,128)} %bitcast.215), custom_call_target="tpu_custom_call" | custom-call | tf_op jit(solution)/shard_map/total/pallas_call | solution.py:651
  204.1 5.3 convolution_convert_fusion.2
  209.5 68.8 %middle.1 = (bf16[2,2,2,192,2048]{4,3,2,1,0:T(8,128)(2,1)}, f32[192,2048]{1,0:T(8,128)S(1)}, bf16[4,128,2048]{2,1,0:T(8,128)(2,1)S(1)}) custom-call(bf16[2,2,2,192,2048]{4,3,2,1,0:T(8,128)(2,1)} %bitcast.183, bf16[192,2048]{1,0:T(8,128)(2,1)S(1)} %bitcast.161, f32[1,2048]{1,0:T(1,128)S(1)} %bitcast.172, bf16[128,2048]{1,0:T(8,128)(2,1)S(1)} %copy-done.10), custom_call_target="tpu_custom_call" | custom-call | tf_op jit(solution)/shard_map/middle/pallas_call | solution.py:626
  280.7 10.6 %fusion.33 = f32[1536,1024]{0,1:T(8,128)S(1)} fusion(bf16[1536,2048]{1,0:T(8,128)(2,1)} %bitcast.231, bf16[2048,1024]{1,0:T(8,128)(2,1)} %all-gather.4.cloned.1.call-done), kind=kOutput, calls=%fused_computation.134 | convolution fusion | flops 6442450944 | bytes 16777216 | tf_op jit(solution)/shard_map/dot_general | solution.py:29
  291.3 8.6 %multiply_convert_fusion.2 = (bf16[1536,512]{0,1:T(8,128)(2,1)S(1)}, bf16[1536,512]{0,1:T(8,128)(2,1)S(1)}, bf16[1536,512]{0,1:T(8,128)(2,1)}) fusion(f32[1536,1024]{0,1:T(8,128)S(1)} %fusion.33, bf16[1536,2048]{1,0:T(8,128)(2,1)} %bitcast.227, bf16[512,2048]{1,0:T(8,128)(2,1)S(1)} %bitcast.180), kind=kOutput, calls=%fused_computation.10 | convolution fusion | flops 3233808384 | bytes 19398656 | tf_op jit(solution)/shard_map/dot_general | solution.py:37
  299.9 9.5 %convolution_convert_fusion.3 = bf16[2048,1024]{1,0:T(8,128)(2,1)} fusion(bf16[1536,2048]{1,0:T(8,128)(2,1)S(1)} %bitcast.232, bf16[1536,512]{0,1:T(8,128)(2,1)S(1)} %get-tuple-element.237, bf16[1536,512]{0,1:T(8,128)(2,1)S(1)} %get-tuple-element.236), kind=kOutput, calls=%fused_computation.3 | convolution fusion | flops 6450839552 | bytes 13631488 | tf_op jit(solution)/shard_map/dot_general | solution.py:33
  309.5 11.4 %convolution_convert_fusion.1 = bf16[1536,2048]{1,0:T(8,128)(2,1)} fusion(bf16[2048,1024]{1,0:T(8,128)(2,1)} %all-gather.4.cloned.1.call-done, bf16[1536,512]{0,1:T(8,128)(2,1)} %copy-done.70, bf16[1536,512]{0,1:T(8,128)(2,1)} %copy-done.69), kind=kOutput, calls=%fused_computation.1 | convolution fusion | flops 6451888128 | bytes 13631488 | tf_op jit(solution)/shard_map/dot_general | solution.py:37
  320.9 70.1 %middle_back.1 = (bf16[2,2,2,192,2048]{4,3,2,1,0:T(8,128)(2,1)}, f32[192,2048]{1,0:T(8,128)S(1)}, f32[1,2048]{1,0:T(1,128)S(1)}) custom-call(bf16[2,2,2,192,2048]{4,3,2,1,0:T(8,128)(2,1)} %bitcast.182, f32[192,2048]{1,0:T(8,128)S(1)} %copy-done.4, f32[1,2048]{1,0:T(1,128)S(1)} %bitcast.173, bf16[192,2048]{1,0:T(8,128)(2,1)S(1)} %bitcast.165), custom_call_target="tpu_custom_call" | custom-call | tf_op jit(solution)/shard_map/middle_back/pallas_call | solution.py:626
  391.1 6.3 fusion.3.gn_ref.ga_ref
  399.1 8.0 %total.3 = f32[12,128]{1,0:T(8,128)} custom-call(f32[12,128]{1,0:T(8,128)} %bitcast.214), custom_call_target="tpu_custom_call" | custom-call | tf_op jit(solution)/shard_map/total/pallas_call | solution.py:651
  407.2 6.6 convolution_convert_fusion.8
  420.7 4.9 constant_dynamic-slice_fusion.5
  425.6 4.8 copy.53
  430.5 4.7 convolution_convert_fusion.5
  435.2 7.8 %convolution_convert_fusion.7 = bf16[512,2048]{1,0:T(8,128)(2,1)} fusion(bf16[1536,512]{0,1:T(8,128)(2,1)S(1)} %copy-done.52, bf16[1536,2048]{1,0:T(8,128)(2,1)} %bitcast.228), kind=kOutput, calls=%fused_computation.12 | convolution fusion | flops 3222274048 | bytes 9961472 | tf_op jit(solution)/shard_map/dot_general | solution.py:33
  460.9 8.0 %collective-permute-done.13 = bf16[256,1024]{1,0:T(8,128)(2,1)} collective-permute-done((bf16[256,1024]{1,0:T(8,128)(2,1)}, bf16[256,1024]{1,0:T(8,128)(2,1)}, u32[]{:S(2)}, u32[]{:S(2)}) %collective-permute-start.13) | collective-permute-done | bytes 524320 | tf_op jit(solution)/shard_map/ppermute | solution.py:1372
  479.8 34.3 %mixer_back.1 = (bf16[1536,1792]{1,0:T(8,128)(2,1)}, f32[4,384]{1,0:T(4,128)S(1)}, f32[1,384]{1,0:T(1,128)S(1)}, f32[4,512]{1,0:T(4,128)S(1)}, f32[1,512]{1,0:T(1,128)S(1)}, /*index=5*/f32[8,128]{1,0:T(8,128)S(1)}) custom-call(f32[1536,1792]{1,0:T(8,128)} %fusion.32.x_ref.m0_ref.m1_ref.m2_ref.m3_ref.s_ref.z_ref.q_ref.k_ref.v_ref, ...), custom_call_target="tpu_custom_call" | custom-call | tf_op jit(solution)/shard_map/mixer_back/pallas_call | solution.py:310
  525.8 18.3 %convolution_convert_fusion = bf16[1536,2048]{1,0:T(8,128)(2,1)} fusion(bf16[1536,1792]{1,0:T(8,128)(2,1)} %get-tuple-element.144.common_ref, bf16[2048,1792]{1,0:T(8,128)(2,1)} %bitcast.226), kind=kOutput, calls=%fused_computation | convolution fusion | flops 11277434880 | bytes 19136512 | tf_op jit(solution)/shard_map/dot_general | solution.py:37
  544.1 8.4 %convolution_convert_fusion.4 = bf16[2048,896]{1,0:T(8,128)(2,1)} fusion(bf16[1536,2048]{1,0:T(8,128)(2,1)S(1)} %bitcast.188, bf16[1536,1792]{1,0:T(8,128)(2,1)S(1)} %bitcast.191), kind=kOutput, calls=%fused_computation.4 | convolution fusion | flops 5638979584 | bytes 12713984 | tf_op jit(solution)/shard_map/dot_general | solution.py:33
  563.7 119.9 %last.1 = (f32[192,2048]{1,0:T(8,128)}, f32[16,128]{1,0:T(8,128)}, bf16[2,2,2,128,896]{4,3,2,1,0:T(8,128)(2,1)}, bf16[2,2,2,128,256]{4,3,2,1,0:T(8,128)(2,1)}, b...) custom-call(bf16[2,2,2,192,2048]{4,3,2,1,0:T(8,128)(2,1)} %bitcast.189, bf16[192,2048]{1,0:T(8,128)(2,1)} %bitcast.159, ...), custom_call_target="tpu_custom_call" | custom-call | tf_op jit(solution)/shard_map/last/pallas_call | solution.py:975
  698.5 5.2 copy.57
  (301 shorter events, 114.7 us)
Async XLA Ops:
  7.2 138.6 %copy-start = (bf16[256,2048]{1,0:T(8,128)(2,1)S(1)}, bf16[256,2048]{1,0:T(8,128)(2,1)}, u32[]{:S(2)}) copy-start(bf16[256,2048]{1,0:T(8,128)(2,1)} %param.41) | copy-start | bytes 3145732
  7.2 139.4 %all-gather.6.cloned.1.call-start = ((), (), s32[]{:S(2)}) async-start(), calls=%async_computation.7 | async-start | bytes 2621440 | tf_op jit(solution)/shard_map/all_gather | solution.py:1538
  9.2 271.5 %all-gather.4.cloned.1.call-start = ((), (), s32[]{:S(2)}) async-start(), calls=%async_computation.3 | async-start | bytes 5242880 | tf_op jit(solution)/shard_map/all_gather | solution.py:1540
  19.9 120.4 %copy-start.68 = (bf16[48]{0:T(256)(128)(2,1)S(1)}, bf16[48]{0:T(256)(128)(2,1)}, u32[]{:S(2)}) copy-start(bf16[48]{0:T(256)(128)(2,1)} %param.35) | copy-start | bytes 292
  139.9 267.2 %reduce-scatter.4.cloned.1.call-start = ((), (), s32[]{:S(2)}) async-start(), calls=%async_computation.4 | async-start | bytes 5242880 | tf_op jit(solution)/shard_map/reduce_scatter | solution.py:1596
  149.7 50.9 %collective-permute-start.2 = (bf16[256,1024]{1,0:T(8,128)(2,1)}, bf16[256,1024]{1,0:T(8,128)(2,1)}, u32[]{:S(2)}, u32[]{:S(2)}) collective-permute-start(bf16[256,1024]{1,0:T(8,128)(2,1)} %get-tuple-element.260), channel_id=1, source_target_pairs={{0,17},{1,16},{16,1},{17,0},{2,19},{3,18},{18,3},{19,2},{4,21},{5,... | collective-permute-start | bytes 1572872 | tf_op jit(solution)/shard_map/ppermute | solution.py:1372
  151.8 48.8 %collective-permute-start.1 = (bf16[256,1024]{1,0:T(8,128)(2,1)}, bf16[256,1024]{1,0:T(8,128)(2,1)}, u32[]{:S(2)}, u32[]{:S(2)}) collective-permute-start(bf16[256,1024]{1,0:T(8,128)(2,1)} %get-tuple-element.261), channel_id=1, source_target_pairs={{0,16},{16,0},{1,17},{17,1},{2,18},{18,2},{3,19},{19,3},{4,20},{20... | collective-permute-start | bytes 1572872 | tf_op jit(solution)/shard_map/ppermute | solution.py:1372
  152.4 48.2 %collective-permute-start = (bf16[256,1024]{1,0:T(8,128)(2,1)}, bf16[256,1024]{1,0:T(8,128)(2,1)}, u32[]{:S(2)}, u32[]{:S(2)}) collective-permute-start(bf16[256,1024]{1,0:T(8,128)(2,1)} %get-tuple-element.262), channel_id=1, source_target_pairs={{0,1},{1,0},{2,3},{3,2},{4,5},{5,4},{6,7},{7,6},{8,9},{9,8},{10,11... | collective-permute-start | bytes 1572872 | tf_op jit(solution)/shard_map/ppermute | solution.py:1372
  309.4 249.6 %reduce-scatter.8.cloned.1.call-start = ((), (), s32[]{:S(2)}) async-start(), calls=%async_computation.6 | async-start | bytes 2621440 | tf_op jit(solution)/shard_map/reduce_scatter | solution.py:1618
  435.2 37.5 %collective-permute-start.3 = (bf16[2,2,192,2048]{3,2,1,0:T(8,128)(2,1)}, bf16[2,2,192,2048]{3,2,1,0:T(8,128)(2,1)}, u32[]{:S(2)}, u32[]{:S(2)}) collective-permute-start(bf16[2,2,192,2048]{3,2,1,0:T(8,128)(2,1)} %bitcast.40), channel_id=1, source_target_pairs={{0,1},{1,0},{2,3},{3,2},{4,5},{5,4},{6,7},{7,6},{8,9},{9,8},{10,11... | collective-permute-start | bytes 9437192 | tf_op jit(solution)/shard_map/ppermute | solution.py:1372
  443.0 120.6 %reduce-scatter.6.cloned.1.call-start = ((), (), s32[]{:S(2)}) async-start(), calls=%async_computation.5 | async-start | bytes 2621440 | tf_op jit(solution)/shard_map/reduce_scatter | solution.py:1473
  443.9 13.2 %collective-permute-start.11 = (bf16[256,1024]{1,0:T(8,128)(2,1)}, bf16[256,1024]{1,0:T(8,128)(2,1)}, u32[]{:S(2)}, u32[]{:S(2)}) collective-permute-start(bf16[256,1024]{1,0:T(8,128)(2,1)} %pad_maximum_fusion.13), channel_id=1, source_target_pairs={{0,1},{1,0},{2,3},{3,2},{4,5},{5,4},{6,7},{7,6},{8,9},{9,8},{10,11... | collective-permute-start | bytes 1572872 | tf_op jit(solution)/shard_map/ppermute | solution.py:1372
  444.3 15.1 %collective-permute-start.12 = (bf16[256,1024]{1,0:T(8,128)(2,1)}, bf16[256,1024]{1,0:T(8,128)(2,1)}, u32[]{:S(2)}, u32[]{:S(2)}) collective-permute-start(bf16[256,1024]{1,0:T(8,128)(2,1)} %pad_maximum_fusion.14), channel_id=1, source_target_pairs={{0,16},{16,0},{1,17},{17,1},{2,18},{18,2},{3,19},{19,3},{4,20},{20... | collective-permute-start | bytes 1572872 | tf_op jit(solution)/shard_map/ppermute | solution.py:1372
  445.7 23.2 %collective-permute-start.13 = (bf16[256,1024]{1,0:T(8,128)(2,1)}, bf16[256,1024]{1,0:T(8,128)(2,1)}, u32[]{:S(2)}, u32[]{:S(2)}) collective-permute-start(bf16[256,1024]{1,0:T(8,128)(2,1)} %pad_maximum_fusion.15), channel_id=1, source_target_pairs={{0,17},{1,16},{16,1},{17,0},{2,19},{3,18},{18,3},{19,2},{4,21},{5,... | collective-permute-start | bytes 1572872 | tf_op jit(solution)/shard_map/ppermute | solution.py:1372
  447.9 66.1 %collective-permute-start.10 = (bf16[128,1024]{1,0:T(8,128)(2,1)}, bf16[128,1024]{1,0:T(8,128)(2,1)}, u32[]{:S(2)}, u32[]{:S(2)}) collective-permute-start(bf16[128,1024]{1,0:T(8,128)(2,1)} %get-tuple-element.269), channel_id=1, source_target_pairs={{0,3},{1,2},{2,1},{3,0},{4,7},{5,6},{6,5},{7,4},{8,11},{9,10},{10,... | collective-permute-start | bytes 786440 | tf_op jit(solution)/shard_map/ppermute | solution.py:1372
  457.0 57.0 %collective-permute-start.9 = (bf16[128,1024]{1,0:T(8,128)(2,1)}, bf16[128,1024]{1,0:T(8,128)(2,1)}, u32[]{:S(2)}, u32[]{:S(2)}) collective-permute-start(bf16[128,1024]{1,0:T(8,128)(2,1)} %get-tuple-element.270), channel_id=1, source_target_pairs={{0,1},{1,0},{2,3},{3,2},{4,5},{5,4},{6,7},{7,6},{8,9},{9,8},{10,11... | collective-permute-start | bytes 786440 | tf_op jit(solution)/shard_map/ppermute | solution.py:1372
  459.4 54.6 %collective-permute-start.8 = (bf16[128,1024]{1,0:T(8,128)(2,1)}, bf16[128,1024]{1,0:T(8,128)(2,1)}, u32[]{:S(2)}, u32[]{:S(2)}) collective-permute-start(bf16[128,1024]{1,0:T(8,128)(2,1)} %get-tuple-element.271), channel_id=1, source_target_pairs={{0,2},{2,0},{1,3},{3,1},{4,6},{6,4},{5,7},{7,5},{8,10},{10,8},{9,1... | collective-permute-start | bytes 786440 | tf_op jit(solution)/shard_map/ppermute | solution.py:1372
  476.1 44.4 %collective-permute-start.4 = (bf16[2,192,1024]{2,1,0:T(8,128)(2,1)}, bf16[2,192,1024]{2,1,0:T(8,128)(2,1)}, u32[]{:S(2)}, u32[]{:S(2)}) collective-permute-start(bf16[2,192,1024]{2,1,0:T(8,128)(2,1)} %fusion.4), channel_id=1, source_target_pairs={{0,2},{2,0},{1,3},{3,1},{4,6},{6,4},{5,7},{7,5},{8,10},{10,8},{9,1... | collective-permute-start | bytes 2359304 | tf_op jit(solution)/shard_map/ppermute | solution.py:1372
  478.8 41.8 %collective-permute-start.5 = (bf16[2,192,1024]{2,1,0:T(8,128)(2,1)}, bf16[2,192,1024]{2,1,0:T(8,128)(2,1)}, u32[]{:S(2)}, u32[]{:S(2)}) collective-permute-start(bf16[2,192,1024]{2,1,0:T(8,128)(2,1)} %fusion.5), channel_id=1, source_target_pairs={{0,16},{16,0},{1,17},{17,1},{2,18},{18,2},{3,19},{19,3},{4,20},{20... | collective-permute-start | bytes 2359304 | tf_op jit(solution)/shard_map/ppermute | solution.py:1372
  517.3 35.2 %collective-permute-start.14 = (bf16[2,2,128,1024]{3,2,1,0:T(8,128)(2,1)S(1)}, bf16[2,2,128,1024]{3,2,1,0:T(8,128)(2,1)S(1)}, u32[]{:S(2)}, u32[]{:S(2)}) collective-permute-start(bf16[2,2,128,1024]{3,2,1,0:T(8,128)(2,1)S(1)} %pad_maximum_fusion.8.own_ref), channel_id=1, source_target_pairs={{0,16},{16,0},{1,17},{17,1},{2,18},{18,2},{3,19},{19,3},{4,20},{20... | collective-permute-start | bytes 3145736 | tf_op jit(solution)/shard_map/ppermute | solution.py:1372
  522.0 32.9 %collective-permute-start.7 = (bf16[192,1024]{1,0:T(8,128)(2,1)S(1)}, bf16[192,1024]{1,0:T(8,128)(2,1)S(1)}, u32[]{:S(2)}, u32[]{:S(2)}) collective-permute-start(bf16[192,1024]{1,0:T(8,128)(2,1)S(1)} %fusion.8), channel_id=1, source_target_pairs={{0,2},{2,0},{1,3},{3,1},{4,6},{6,4},{5,7},{7,5},{8,10},{10,8},{9,1... | collective-permute-start | bytes 1179656 | tf_op jit(solution)/shard_map/ppermute | solution.py:1372
  524.9 30.0 %collective-permute-start.6 = (bf16[192,1024]{1,0:T(8,128)(2,1)S(1)}, bf16[192,1024]{1,0:T(8,128)(2,1)S(1)}, u32[]{:S(2)}, u32[]{:S(2)}) collective-permute-start(bf16[192,1024]{1,0:T(8,128)(2,1)S(1)} %fusion.9), channel_id=1, source_target_pairs={{0,16},{16,0},{1,17},{17,1},{2,18},{18,2},{3,19},{19,3},{4,20},{20... | collective-permute-start | bytes 1179656 | tf_op jit(solution)/shard_map/ppermute | solution.py:1372
  563.6 126.6 %copy-start.8 = (bf16[1,128,2048]{2,1,0:T(8,128)(2,1)S(1)}, bf16[1,128,2048]{2,1,0:T(8,128)(2,1)}, u32[]{:S(2)}) copy-start(bf16[1,128,2048]{2,1,0:T(8,128)(2,1)} %reduce-scatter.8.cloned.1.call-done) | copy-start | bytes 1572868
  563.7 126.6 %copy-start.9 = (bf16[1,256,1024]{2,1,0:T(8,128)(2,1)S(1)}, bf16[1,256,1024]{2,1,0:T(8,128)(2,1)}, u32[]{:S(2)}) copy-start(bf16[1,256,1024]{2,1,0:T(8,128)(2,1)} %reduce-scatter.6.cloned.1.call-done) | copy-start | bytes 1572868
  (71 other events, 844.5 us)
Sparse Core Ops, SparseCore 0:
  10.2 62.7 all-gather.5
  140.0 83.5 all-gather.3
  309.6 75.9 reduce-scatter.3
  443.2 43.2 reduce-scatter.7
  520.7 42.9 reduce-scatter.5

commit v4 on v3

--- a/solution.py
+++ b/solution.py
@@ -724,8 +724,8 @@
     return kick, pass_on, end, finish
 
 
-def column_sums(grad_ref, first, boxes, sems, local):
-    own, by_c, for_y, by_y, for_x, by_x, out = boxes
+def column_sums(grad_ref, grad, first, boxes, sems):
+    by_c, for_y, by_y, for_x, by_x, out = boxes
     x, y, c = (lax.axis_index(a) for a in ("x", "y", "c"))
 
     def cols(side):
@@ -733,12 +733,9 @@
         kv = pl.ds(pl.multiple_of(first + 2 * NST + side * HD, 128), HD)
         return (maps, pl.ds(0, NST)), (kv, pl.ds(NST, HD))
 
-    steps = pl.ds(first + 2 * NST + 2 * HD, 128)
-    loads = [
-        pltpu.make_async_copy(grad_ref.at[:, src], own.at[:, dst], local.at[i])
-        for i, (src, dst) in enumerate(cols(c))
-    ]
-    loads.append(pltpu.make_async_copy(grad_ref.at[:, steps], out.at[:, pl.ds(128, 128)], local.at[2]))
+    def own():
+        return jnp.concatenate([grad[:, src] for src, _ in cols(c)], axis=1).astype(F32)
+
     across = [
         remote(grad_ref.at[:, src], by_c.at[:, dst], sems.at[0, i], sems.at[1, i], "c")
         for i, (src, dst) in enumerate(cols(1 - c))
@@ -747,7 +744,7 @@
     over_x = remote(for_x, by_x, sems.at[0, 3], sems.at[1, 3], "x")
 
     def begin():
-        for copy in loads + across:
+        for copy in across:
             copy.start()
 
     def halves(value, side):
@@ -757,15 +754,15 @@
         return maps, kv
 
     def second():
-        for copy in loads + across:
+        for copy in across:
             copy.wait()
-        maps, kv = halves(own[...].astype(F32) + by_c[...].astype(F32), 1 - y)
+        maps, kv = halves(own() + by_c[...].astype(F32), 1 - y)
         for_y[...] = jnp.concatenate([maps, kv, kv], axis=1).astype(BF)
         over_y.start()
 
     def summed():
         got = by_y[...].astype(F32)
-        maps, kv = halves(own[...].astype(F32) + by_c[...].astype(F32), y)
+        maps, kv = halves(own() + by_c[...].astype(F32), y)
         return maps + got[:, : NST // 2], kv + got[:, NST // 2 : NST // 2 + HD // 2]
 
     def third():
@@ -781,6 +778,7 @@
         maps = jnp.where(x == 0, maps[:, : NST // 4], maps[:, NST // 4 :])
         maps = maps + by_x[...].astype(F32)[:, : NST // 4]
         out[:, 0:128] = jnp.concatenate([kv, maps], axis=1).astype(BF)
+        out[:, 128:256] = grad[:, first + 2 * NST + 2 * HD :]
 
     return begin, second, third, end
 
@@ -825,29 +823,33 @@
 
 
 def last_kernel(
-    part_ref, rows_ref, gain_ref, grad_ref, little_ref, weight_ref, common_ref, hidden_ref,
-    rows_in, down_in,
-    out_ref, little_out, got_ref, few_ref, rows_out, down_out,
+    rows_ref, gain_ref, grad_ref, little_ref, weight_ref, common_ref, hidden_ref, project_ref,
+    rows_in, out_ref, little_out, got_ref, few_ref, rows_out,
     held, inbox, few, few_box, swap, few_swap, little, little_in, little_c, little_y, little_box,
-    hidden, col_own, col_c, col_y_out, col_y_in, col_x_out, col_x_in, slices,
+    hidden, common, project, part, col_c, col_y_out, col_y_in, col_x_out, col_x_in, slices,
     local, weight_sems, few_sems, little_sems, hop_sems, swap_sems, few_swap_sems, own_sems,
-    cross_sems, col_sems, col_local, *scratch,
+    cross_sems, col_sems, *scratch,
 ):
     x, z, y, c = (lax.axis_index(a) for a in ("x", "z", "y", "c"))
     n = lax.axis_size("z")
     greet_all()
-    load = pltpu.make_async_copy(weight_ref, held, local.at[0])
-    load.start()
-    load_hidden = pltpu.make_async_copy(hidden_ref, hidden, local.at[1])
-    load_hidden.start()
-    begin, wide, thin, end = reduce_plane(part_ref, scratch)
-    boxes = (col_own, col_c, col_y_out, col_y_in, col_x_out, col_x_in, slices)
+    pairs = ((weight_ref, held), (common_ref, common), (project_ref, project), (hidden_ref, hidden))
+    loads = [pltpu.make_async_copy(*pair, local.at[i]) for i, pair in enumerate(pairs)]
+    for load in loads:
+        load.start()
+    begin, wide, thin, end = reduce_plane(part, scratch)
+    boxes = (col_c, col_y_out, col_y_in, col_x_out, col_x_in, slices)
     col_begin, col_second, col_third, col_end = column_sums(
-        common_ref, common_ref.shape[1] // 2, boxes, col_sems, col_local
+        common_ref, common, common_ref.shape[1] // 2, boxes, col_sems
     )
     col_begin()
-    begin()
-    load.wait()
+    count = rows_ref.shape[0]
+
+    def product_of(cc, yy):
+        for xx in (0, 1):
+            first = pl.multiple_of((4 * yy + 2 * cc + xx) * count, 16)
+            block = common[pl.ds(first, count), :]
+            part[yy, cc, xx] = dot(block, project[...], LANES).astype(BF)
 
     order = ((1, 1), (1, 0), (0, 1), (0, 0))
     sums, places = [], []
@@ -862,33 +864,44 @@
             )
         )
     few_sum = line_sum(lambda d: few.at[d], lambda d: few_box.at[d], few_sems)
+    cross = remote(rows_in, rows_out, cross_sems.at[0], cross_sems.at[1], "x")
+    loads[0].wait()
     for k in range(n - 1):
         for item in sums:
             item[0](k)
-    crosses = []
-    for i, (src, dst) in enumerate(((rows_in, rows_out), (down_in, down_out))):
-        crosses.append(remote(src, dst, cross_sems.at[0, i], cross_sems.at[1, i], "x"))
-        crosses[i].start()
+
+    def pass_on(item, k, far):
+        @pl.when(z < n // 2)
+        def _():
+            item[1](far, k)
+
+        @pl.when(z >= n // 2)
+        def _():
+            item[1](1 - far, k)
+
+    loads[1].wait()
     col_second()
-    wide((0,))
-
-    def pass_all(k):
-        for item in sums:
-            for near in (0, 1):
-
-                @pl.when(z < n // 2)
-                def _():
-                    item[1](near, k)
-
-                @pl.when(z >= n // 2)
-                def _():
-                    item[1](1 - near, k)
-
-    pass_all(0)
+    loads[2].wait()
+    product_of(1 - c, 0)
+    pass_on(sums[0], 0, 0)
+    product_of(1 - c, 1)
+    begin()
+    pass_on(sums[1], 0, 0)
+    pass_on(sums[0], 0, 1)
+    product_of(c, 0)
+    pass_on(sums[2], 0, 0)
+    pass_on(sums[1], 0, 1)
+    product_of(c, 1)
+    pass_on(sums[3], 0, 0)
+    pass_on(sums[2], 0, 1)
+    wide()
+    pass_on(sums[3], 0, 1)
     col_third()
-    wide((1,))
+    if n > 2:
+        for i in (0, 1, 2, 3):
+            pass_on(sums[i], 1, 0)
     col_end()
-    load_hidden.wait()
+    loads[3].wait()
     product = dot(slices[...], hidden[...], ROWS).T.astype(BF)
     piece = product.shape[0] // (4 * n)
     for at in range(n):
@@ -899,13 +912,16 @@
     for k in range(n - 1):
         few_sum[0](k)
     for k in range(1, n - 1):
-        pass_all(k)
+        for item in sums:
+            for far in (0, 1):
+                if k > 1 or far == 1:
+                    pass_on(item, k, far)
     thin()
+    cross.start()
 
     rows = rows_ref[...].astype(F32)
     grad, gain_grad = norm_back_parts(rows, gain_ref[...], end())
     out_ref[...] = grad + grad_ref[...]
-
     little[...] = little_ref[...]
     for at in range(n):
         for yy in (0, 1):
@@ -914,39 +930,43 @@
                 little[at, yy, cc, 0:1, 0:piece] = gain_grad[:, first : first + piece]
     hop = remote(little, little_in, hop_sems.at[0, 0], hop_sems.at[1, 0], "x")
     hop.start()
+
+    give, forward, finish = hand_out(
+        lambda yy, cc: held.at[z, yy, cc], swap, got_ref, places, swap_sems, own_sems.at[0]
+    )
+    few_give, few_forward, few_finish = hand_out(
+        lambda yy, cc: few.at[z, yy, cc], few_swap, few_ref, places, few_swap_sems, own_sems.at[1]
+    )
+    for i in (0, 1):
+        sums[i][2]()
+        give(i)
     hop.wait()
     little[...] = little[...] + little_in[...]
     hop = remote(little.at[:, :, 1 - c], little_c, hop_sems.at[0, 1], hop_sems.at[1, 1], "c")
     hop.start()
+    forward(0)
+    sums[2][2]()
+    give(2)
+    forward(1)
     hop.wait()
     for yy in (0, 1):
         little_c[:, yy] = little_c[:, yy] + little[:, yy, c]
     hop = remote(little_c.at[:, 1 - y], little_y, hop_sems.at[0, 2], hop_sems.at[1, 2], "y")
     hop.start()
+    sums[3][2]()
+    give(3)
+    forward(2)
+    forward(3)
+    pass_on(few_sum, 0, 0)
     hop.wait()
     little_y[...] = little_y[...] + little_c[:, y]
     little_sum = line_sum(lambda d: little_y.at[d], lambda d: little_box.at[d], little_sems)
     for k in range(n - 1):
         little_sum[0](k)
-
-    give, forward, finish = hand_out(
-        lambda yy, cc: held.at[z, yy, cc], swap, got_ref, places, swap_sems, own_sems.at[0]
-    )
-    few_give, few_forward, few_finish = hand_out(
-        lambda yy, cc: few.at[z, yy, cc], few_swap, few_ref, places, few_swap_sems, own_sems.at[1]
-    )
-    for i in range(4):
-        sums[i][2]()
-        give(i)
-        if i > 0:
-            forward(i - 1)
-        if i < n - 1:
-            for way in (0, 1):
-                few_sum[1](way, i)
-    forward(3)
-    for k in range(4, n - 1):
-        for way in (0, 1):
-            few_sum[1](way, k)
+    for k in range(n - 1):
+        for far in (0, 1):
+            if k > 0 or far == 1:
+                pass_on(few_sum, k, far)
     few_sum[2]()
     for i in range(4):
         few_give(i)
@@ -957,15 +977,14 @@
     little_out[...] = little_y[z]
     for i in range(4):
         few_forward(i)
-    for cross in crosses:
-        cross.wait()
+    cross.wait()
     finish()
     few_finish()
     for item in sums + [few_sum, little_sum]:
         item[3]()
 
 
-def last_call(part, rows, gain, grad, little, weight, common, hidden, sum_rows, sum_down):
+def last_call(rows, gain, grad, little, weight, common, hidden, project, sum_rows):
     n = lax.axis_size("z")
     count, width = rows.shape
     total, piece = hidden.shape[0], weight.shape[3]
@@ -974,15 +993,14 @@
     dma = pltpu.SemaphoreType.DMA
     return pl.pallas_call(
         last_kernel,
-        in_specs=[vmem] * 5 + [hbm] * 5,
-        out_specs=[vmem, vmem, hbm, hbm, hbm, hbm],
+        in_specs=[vmem] * 4 + [hbm] * 5,
+        out_specs=[vmem, vmem, hbm, hbm, hbm],
         out_shape=[
             jax.ShapeDtypeStruct((count, width), F32),
             jax.ShapeDtypeStruct(pack, F32),
             jax.ShapeDtypeStruct((2, 2, 2) + block, BF),
             jax.ShapeDtypeStruct((2, 2, 2) + small, BF),
             jax.ShapeDtypeStruct(sum_rows.shape, BF),
-            jax.ShapeDtypeStruct(sum_down.shape, BF),
         ],
         scratch_shapes=[
             pltpu.VMEM((n, 2, 2) + block, BF),
@@ -997,14 +1015,16 @@
             pltpu.VMEM((n,) + pack, F32),
             pltpu.VMEM((n + 1,) + pack, F32),
             pltpu.VMEM(hidden.shape, BF),
-            pltpu.VMEM((total, NST + HD), BF),
+            pltpu.VMEM(common.shape, BF),
+            pltpu.VMEM(project.shape, BF),
+            pltpu.VMEM((2, 2, 2, count, width), BF),
             pltpu.VMEM((total, NST + HD), BF),
             pltpu.VMEM((total, 256), BF),
             pltpu.VMEM((total, 256), BF),
             pltpu.VMEM((total, 128), BF),
             pltpu.VMEM((total, 128), BF),
             pltpu.VMEM((total, 256), BF),
-            dma((2,)),
+            dma((4,)),
             dma((4, 2, 2, n)),
             dma((2, 2, n)),
             dma((2, 2, n)),
@@ -1012,16 +1032,15 @@
             dma((2, 7)),
             dma((2, 7)),
             dma((2, 4)),
-            dma((2, 2)),
+            dma((2,)),
             dma((2, 4)),
-            dma((3,)),
         ]
         + sum_scratch(count, width),
         compiler_params=pltpu.CompilerParams(
-            collective_id=3, has_side_effects=True, vmem_limit_bytes=58 * 1024 * 1024
+            collective_id=3, has_side_effects=True, vmem_limit_bytes=61 * 1024 * 1024
         ),
         name="last",
-    )(part, rows, gain, grad, little, weight, common, hidden, sum_rows, sum_down)
+    )(rows, gain, grad, little, weight, common, hidden, project, sum_rows)
 
 
 def start_kernel(
@@ -1231,22 +1250,26 @@
     inner = MH * MP
     wide = inner // PARTS
 
+    def turned(start, width, at, count):
+        rows = mamba_ref[pl.ds(pl.multiple_of(start + x * width + at, 128), count), :]
+        return rows.astype(F32).T.astype(BF)
+
     def half(ref, start, width, at, count):
         return ref[:, pl.ds(pl.multiple_of(start + x * width + at, 128), count)]
 
-    own_ref[:, :NST] = half(mamba_ref, 2 * inner, NST, 0, NST)
+    own_ref[:, :NST] = turned(2 * inner, NST, 0, NST)
     own_ref[:, NST : NST + HD] = half(key_ref, 0, HD, 0, HD)
     own_ref[:, NST + HD : NST + 2 * HD] = half(value_ref, 0, HD, 0, HD)
-    steps = mamba_ref[:, 2 * inner + 2 * NST :].astype(F32)
-    steps = jnp.where(x == 0, steps[:, : MH // 2], steps[:, MH // 2 :])
-    rest = jnp.zeros((steps.shape[0], 128 - MH // 2), F32)
-    own_ref[:, NST + 2 * HD :] = jnp.concatenate([steps, rest], axis=1).astype(BF)
+    steps = mamba_ref[2 * inner + 2 * NST :, :].astype(F32)
+    steps = jnp.where(x == 0, steps[: MH // 2], steps[MH // 2 :])
+    rest = jnp.zeros((128 - MH // 2, steps.shape[1]), F32)
+    own_ref[:, NST + 2 * HD :] = jnp.concatenate([steps, rest], axis=0).T.astype(BF)
     for c in (0, 1):
         for y in (0, 1):
             j = 2 * c + y
-            blocks_ref[c, y, :, :wide] = half(mamba_ref, 0, inner // 2, j * wide, wide)
-            blocks_ref[c, y, :, wide : 2 * wide] = half(
-                mamba_ref, inner, inner // 2, j * wide, wide
+            blocks_ref[c, y, :, :wide] = turned(0, inner // 2, j * wide, wide)
+            blocks_ref[c, y, :, wide : 2 * wide] = turned(
+                inner, inner // 2, j * wide, wide
             )
             blocks_ref[c, y, :, 2 * wide :] = half(query_ref, 0, 4 * HD, j * HD, HD)
     unit = units_ref.shape[3] // 2 // n
@@ -1273,7 +1296,7 @@
         ],
         compiler_params=pltpu.CompilerParams(vmem_limit_bytes=VMEM),
         name="prepare",
-    )(query, key, value, mamba, gate, up)
+    )(query, key, value, mamba.T, gate, up)
 
 
 def units_kernel(own_ref, across_ref, gate_ref, up_ref):
@@ -1319,8 +1342,8 @@
             for y in (0, 1):
                 j = 4 * xx + 2 * c + y
                 block = got_ref[xx, c, y].astype(F32)
-                mamba_ref[:, j * wide : (j + 1) * wide] = block[:, :wide]
-                mamba_ref[:, inner + j * wide : inner + (j + 1) * wide] = block[:, wide : 2 * wide]
+                mamba_ref[j * wide : (j + 1) * wide, :] = block[:, :wide].T
+                mamba_ref[inner + j * wide : inner + (j + 1) * wide, :] = block[:, wide : 2 * wide].T
                 query_ref[:, j * HD : (j + 1) * HD] = block[:, 2 * wide : 2 * wide + HD]
                 total = total + few_ref[xx, c, y, :, 128:].astype(F32)
         steps.append(total[:, : MH // 2])
@@ -1334,10 +1357,11 @@
     for c in (0, 1):
         for y in (0, 1):
             first = 2 * inner + (2 * c + y) * (NST // 2)
-            mamba_ref[:, first : first + NST // 2] = pair(
+            mamba_ref[first : first + NST // 2, :] = pair(
                 few_ref[0, c, y], few_ref[1, c, y], HD // 2, NST // 4
-            )
-    mamba_ref[:, 2 * inner + 2 * NST :] = jnp.concatenate(steps, axis=1)
+            ).T
+    rest = jnp.zeros((steps[0].shape[0], 128 - MH), F32)
+    mamba_ref[2 * inner + 2 * NST :, :] = jnp.concatenate(steps + [rest], axis=1).T[:MH]
 
     own, across = own_ref[...], across_ref[...]
     sides = [jnp.where(x == 0, own, across), jnp.where(x == 0, across, own)]
@@ -1462,6 +1486,12 @@
     return blocks
 
 
+def rows_stack(moved):
+    if lax.axis_size("z") != 4:
+        return moved
+    return jnp.stack([moved[0][0], moved[0][1], moved[1][0], moved[1][1]])
+
+
 def rows_sum(moved):
     if lax.axis_size("z") != 4:
         parts = []
@@ -1469,7 +1499,6 @@
             part = lax.psum_scatter(whole, FSDP, scatter_dimension=0, tiled=True)
             parts.append(half_columns(lax.psum(part, "x")))
         return jnp.concatenate(parts)
-    moved = jnp.stack([moved[0][0], moved[0][1], moved[1][0], moved[1][1]])
     return lax.psum_scatter(moved, "z")
 
 
@@ -1594,44 +1623,43 @@
     grad_gateup = jnp.concatenate([grad_gate.astype(BF), grad_up.astype(BF)], axis=1)
     grad_wgateup = outer_product(second, grad_gateup)
     sum_gateup = lax.psum_scatter(grad_wgateup.astype(BF).reshape(-1, 4 * count, 2 * ff), "z")
+    grad_down = outer_product(active, incoming).astype(BF)
+    sum_down = lax.psum_scatter(
+        grad_down.reshape(-1, ff // lax.axis_size("z"), model_dim), "z"
+    )
+    result = mm(active, w_down).astype(BF).reshape(block)
+    grad_gateup = after(grad_gateup, (grad_down, result))
     grad_second = across(grad_gateup, w_gateup).astype(BF).reshape(block)
     grad_mixer, grad_middle, grad_gain_ffn = middle_calls(
         grad_second, middle, gain_ffn[None], cot=grad_rows
     )
     grad_mixer = grad_mixer.reshape(rows, model_dim)
-    grad_mixed = across(grad_mixer, w_out)
+    result_kept, result_away = halves_of(after(result, grad_mixer), "c", 1)
+    result_got = flip(result_away, "c")
+    grad_out = outer_product(mixed, after(grad_mixer, result_away))
+    row_blocks = rows_blocks(grad_out, [wide, HD])
+    grad_mixed = across(after(grad_mixer, row_blocks), w_out)
     grad_normed = grad_mixed[:, :wide]
     grad_gain_mamba = jnp.sum(grad_normed * normal, axis=0)
     scaled = grad_normed * gain_mamba
-    dots = plane_total(jnp.sum(scaled * normal, axis=-1).reshape(-1, 128), 5)
-    grad_mixer, active, sum_gateup = after((grad_mixer, active, sum_gateup), dots)
-    grad_out = outer_product(mixed, grad_mixer)
-    row_blocks = rows_blocks(grad_out, [wide, HD])
-    active = after(active, row_blocks)
-    sides = active.reshape(2, 2, 2 * token_count, ff)
-    result_kept, result_away = (
-        mm(v, w_down).astype(BF).reshape(2, 2, token_count, model_dim)
-        for v in halves_of(sides, "c", 1)
-    )
-    result_got = flip(result_away, "c")
-    grad_down = outer_product(after(active, result_away), incoming).astype(BF)
-    sum_down = lax.psum_scatter(
-        grad_down.reshape(-1, ff // lax.axis_size("z"), model_dim), "z"
-    )
-    gateup_blocks = sum_blocks(sum_gateup)
-    dots = after(dots, (gateup_blocks, grad_down))
-    row_sums = exchanged(row_blocks, "x", "c", dots) if fast else row_blocks
+    dots = jnp.sum(scaled * normal, axis=-1).reshape(-1, 128)
     result_got = after(result_got, dots)
     half = model_dim // 2
     lefts = [halves_of(v[..., :half], "y", 0) for v in (result_kept, result_got)]
     rights = [halves_of(v[..., half:], "x", 1) for v in (result_kept, result_got)]
     left, right = ((a[1].astype(F32) + b[1].astype(F32)).astype(BF) for a, b in (lefts, rights))
-    dots = after(dots, (left, right)).reshape(rows, 1) / inner
+    dots = plane_total(after(dots, (left, right)), 5)
+    left, right, sum_gateup = after((left, right, sum_gateup), dots)
+    gateup_blocks = sum_blocks(sum_gateup)
+    row_sums = exchanged(row_blocks, "x", "c", dots) if fast else row_blocks
+    row_sums = rows_stack(row_sums)
+    down_across = flip(sum_down, "x")
+    dots = after(dots, (gateup_blocks, left, right, row_sums, sum_down)).reshape(rows, 1) / inner
 
     grad_in, gxk, gxb, gmk, gmb, gheads = mixer_backward(
         seqs, length, projected, params, tables, scanned, grad_mixed, gain_mamba[None], factor, dots
     )
-    sum_rows = rows_sum(after(row_sums, grad_in))
+    sum_rows = rows_sum(row_sums)
     moved = exchanged(gateup_blocks, "c", "y", grad_in)
     moved = jnp.stack([jnp.stack(g) for g in moved])
     moved_across = flip(moved, "x")
@@ -1644,12 +1672,11 @@
 
     left, right = three(lefts, 1).astype(BF), three(rights, 1).astype(BF)
     grad_in = after(grad_in, (moved, left, right))
-    grad_hidden = across(grad_in, w_in).astype(BF).reshape(block)
     grad_win = outer_product(hidden, grad_in[:, : 2 * wide + HD]).astype(BF)
     grad_win = grad_win.reshape(-1, 2, 2, count, grad_win.shape[1])
-    left, right = after((flip(left, "x"), flip(right, "y")), grad_win)
+    got_left, got_right = after((flip(left, "x"), flip(right, "y")), grad_win)
     result = jnp.concatenate(
-        [three(lefts, 0) + left.astype(F32), three(rights, 0) + right.astype(F32)], axis=1
+        [three(lefts, 0) + got_left.astype(F32), three(rights, 0) + got_right.astype(F32)], axis=1
     )
     output = (middle + result).astype(BF).reshape(1, token_count, model_dim)
     shard_gate, shard_up = units_call(moved, after(moved_across, grad_win))
@@ -1672,9 +1699,9 @@
     little.append(jnp.broadcast_to(head_grad.reshape(1, -1), (fsdp, 3 * MH)))
     little = packed(jnp.zeros((fsdp, count), F32), little)
     little = little.reshape((-1, 2, 2) + little.shape[1:])
-    tokens_grad, total, got_in, got_few, rows_across, down_across = last_call(
-        grad_hidden, token_rows, gain_in[None], grad_middle, little, grad_win, grad_in, hidden,
-        sum_rows, sum_down,
+    tokens_grad, total, got_in, got_few, rows_across = last_call(
+        token_rows, gain_in[None], grad_middle, little, grad_win, after(grad_in, (left, right)),
+        hidden, w_in, sum_rows,
     )
     tokens_grad = tokens_grad.reshape(1, token_count, model_dim)
     total = total.reshape(-1)
@@ -1683,7 +1710,7 @@
         got.append(total[at : at + like.size].reshape(like.shape))
         at += like.size
 
-    weights = [query_weight, key_weight, value_weight, mamba_in_weight]
+    weights = [query_weight, key_weight, value_weight, mamba_in_weight.T]
     weights += [mamba_out_weight, attn_out_weight, down_weight]
     (
         shard_query, shard_key, shard_value, shard_mamba_in,
@@ -1700,7 +1727,7 @@
         shard_key,
         shard_value,
         shard_attn_out,
-        shard_mamba_in,
+        shard_mamba_in.T,
         got[4],
         got[3],
         got[5][0],

time: 721 us -> 662 us (0.918)
  matrix products: 119 us -> 96.6 us
  local copies, waits for them, and re-layouts: 66.3 us -> 47.2 us
  waiting for transfers between devices: 15.1 us -> 0.13 us
    dot_general x4 -> x3, matrix products: 44.6 us -> 26.4 us  [across(): lax.dot_general(left, right, (((1,), (1,)), ((), ())), preferred_element_...]
    dynamic_slice x3 -> x0, local copies, waits for them, and re-layouts: 13 us -> none  [the longest x2 8.15 us: halves_of(): kept = lax.dynamic_index_in_dim(value, at, dim, keepdims=False)]
    ppermute x15 -> x16, waiting for transfers between devices: 10.4 us -> 0.04 us  [flip(): return lax.ppermute(value, axes, pairs)]
    unnamed x160 -> x142, local copies, waits for them, and re-layouts: 26.1 us -> 20.4 us
    dot_general x5 -> x4, matrix products: 41.7 us -> 39.1 us  [mm(): return jnp.dot(left, right, preferred_element_type=F32)]
  transfers between devices with their start and end apart: 20 -> 21, of which waited for: 3 -> 0; matrix products, arithmetic and copies ran while one was open for 18% -> 19% of each run, Pallas kernels for 46% -> 68%
where the time goes in v4:
time: 662 us; the launch traced here: 659 us
  Pallas kernels  452 us (68%)
  matrix products  96.6 us (15%)
  local copies, waits for them, and re-layouts  47.2 us (7%)
  other arithmetic  33.1 us (5%)
  between operations  15.1 us (2%)
  starting transfers between devices  14.1 us (2%)
    pallas_call x2, Pallas kernels, middle_calls(): pl.pallas_call(middle_kernel if cot is None else middle_back_kernel, in_s...  139 us
    pallas_call x1, Pallas kernels, start_call(): pl.pallas_call(start_kernel, in_specs=[vmem, vmem, hbm, hbm, hbm, hbm], o...  120 us
    pallas_call x1, Pallas kernels, last_call(): pl.pallas_call(last_kernel, in_specs=[vmem] * 4 + [hbm] * 5, out_specs=[v...  118 us
    dot_general x4, matrix products, mm(): return jnp.dot(left, right, preferred_element_type=F32)  39.1 us
    pallas_call x1, Pallas kernels, mixer_backward(): pl.pallas_call(mixer_back_kernel, grid=(seqs,), in_specs=mixer_specs(leng...  34.2 us
    dot_general x4, matrix products, outer_product(): lax.dot_general(left, right, (((0,), (0,)), ((), ())), preferred_element_...  31 us
    dot_general x3, matrix products, across(): lax.dot_general(left, right, (((1,), (1,)), ((), ())), preferred_element_...  26.4 us
    unnamed x142, local copies, waits for them, and re-layouts  20.4 us
  transfers between devices with their start and end apart: 21, of which 0 were waited for; matrix products, arithmetic and copies ran while one was open for 19% of the time, Pallas kernels for 68%

profile of v4, /device:TPU:0, one launch (start us, length us, event | category | flops | bytes accessed | tf_op | source)
XLA Modules:
  0.0 658.5 jit_solution(10607034105170081691)
XLA Ops:
  19.5 119.8 %start.1 = (bf16[2,2,2,192,2048]{4,3,2,1,0:T(8,128)(2,1)}, f32[4,2,2,16,128]{4,3,2,1,0:T(8,128)S(1)}, bf16[4,2,2,128,1792]{4,3,2,1,0:T(8,128)(2,1)}, bf16[2,2,12...) custom-call(bf16[192,2048]{1,0:T(8,128)(2,1)S(1)} %bitcast.157, f32[16,128]{1,0:T(8,128)S(1)} %bitcast.171, ...), custom_call_target="tpu_custom_call" | custom-call | tf_op jit(solution)/shard_map/start/pallas_call | solution.py:1214
  147.2 3.1 dynamic-slice_bitcast_fusion.6
  152.7 17.5 %fusion.28.x_ref.m0_ref.m1_ref.m2_ref.m3_ref.s_ref.z_ref.q_ref.k_ref.v_ref = f32[1536,1792]{1,0:T(8,128)} fusion(bf16[1536,2048]{1,0:T(8,128)(2,1)} %bitcast.183, bf16[2048,1792]{1,0:T(8,128)(2,1)} %bitcast.178), kind=kOutput, calls=%fused_computation.127 | convolution fusion | flops 11274289152 | bytes 24641536 | tf_op jit(solution)/shard_map/dot_general | solution.py:29
  170.2 14.7 %mixer.1 = (bf16[1536,384]{1,0:T(8,128)(2,1)S(1)}, f32[1536,384]{1,0:T(8,128)S(1)}, f32[1536,1]{1,0:T(8,128)S(1)}, bf16[1536,128]{1,0:T(8,128)(2,1)S(1)}) custom-call(f32[1536,1792]{1,0:T(8,128)} %fusion.28.x_ref.m0_ref.m1_ref.m2_ref.m3_ref.s_ref.z_ref.q_ref.k_ref.v_ref, f32[1536,1792]{1,0:T(8,128)} %fusion.28.x_ref.m0_ref.m1_ref.m2_ref.m3_ref.s_ref.z_ref.q_ref.k_ref.v_ref, ...), custom_call_target="tpu_custom_call" | custom-call | tf_op jit(solution)/shard_map/mixer/pallas_call | solution.py:293
  189.6 9.0 %total.2 = f32[12,128]{1,0:T(8,128)} custom-call(f32[12,128]{1,0:T(8,128)} %bitcast.205), custom_call_target="tpu_custom_call" | custom-call | tf_op jit(solution)/shard_map/total/pallas_call | solution.py:651
  204.4 5.4 convolution_convert_fusion.2
  209.9 68.8 %middle.1 = (bf16[2,2,2,192,2048]{4,3,2,1,0:T(8,128)(2,1)}, f32[192,2048]{1,0:T(8,128)S(1)}, bf16[4,128,2048]{2,1,0:T(8,128)(2,1)S(1)}) custom-call(bf16[2,2,2,192,2048]{4,3,2,1,0:T(8,128)(2,1)} %bitcast.182, bf16[192,2048]{1,0:T(8,128)(2,1)S(1)} %bitcast.158, f32[1,2048]{1,0:T(1,128)S(1)} %bitcast.169, bf16[128,2048]{1,0:T(8,128)(2,1)S(1)} %copy-done.9), custom_call_target="tpu_custom_call" | custom-call | tf_op jit(solution)/shard_map/middle/pallas_call | solution.py:626
  281.1 10.6 %fusion.29 = f32[1536,1024]{0,1:T(8,128)S(1)} fusion(bf16[1536,2048]{1,0:T(8,128)(2,1)} %bitcast.221, bf16[2048,1024]{1,0:T(8,128)(2,1)} %all-gather.4.cloned.1.call-done), kind=kOutput, calls=%fused_computation.128 | convolution fusion | flops 6442450944 | bytes 16777216 | tf_op jit(solution)/shard_map/dot_general | solution.py:29
  291.7 8.6 %multiply_convert_fusion.1 = (bf16[1536,512]{0,1:T(8,128)(2,1)S(1)}, bf16[1536,512]{0,1:T(8,128)(2,1)S(1)}, bf16[1536,512]{0,1:T(8,128)(2,1)}) fusion(f32[1536,1024]{0,1:T(8,128)S(1)} %fusion.29, bf16[1536,2048]{1,0:T(8,128)(2,1)} %bitcast.215, bf16[512,2048]{1,0:T(8,128)(2,1)S(1)} %bitcast.176), kind=kOutput, calls=%fused_computation.9 | convolution fusion | flops 3233808384 | bytes 19398656 | tf_op jit(solution)/shard_map/dot_general | solution.py:37
  300.3 9.4 %convolution_convert_fusion.3 = bf16[2048,1024]{1,0:T(8,128)(2,1)} fusion(bf16[1536,2048]{1,0:T(8,128)(2,1)S(1)} %bitcast.222, bf16[1536,512]{0,1:T(8,128)(2,1)S(1)} %get-tuple-element.176, bf16[1536,512]{0,1:T(8,128)(2,1)S(1)} %get-tuple-element.175), kind=kOutput, calls=%fused_computation.3 | convolution fusion | flops 6450839552 | bytes 13631488 | tf_op jit(solution)/shard_map/dot_general | solution.py:33
  312.3 5.6 convolution_convert_fusion.1
  318.0 4.6 convolution_convert_fusion.6
  322.6 11.1 %convolution_convert_fusion = bf16[1536,2048]{1,0:T(8,128)(2,1)} fusion(bf16[1536,1024]{0,1:T(8,128)(2,1)S(1)} %pad_maximum_fusion, bf16[2048,1024]{1,0:T(8,128)(2,1)} %all-gather.4.cloned.1.call-done), kind=kOutput, calls=%fused_computation | convolution fusion | flops 6445596672 | bytes 13631488 | tf_op jit(solution)/shard_map/dot_general | solution.py:37
  333.7 69.7 %middle_back.1 = (bf16[2,2,2,192,2048]{4,3,2,1,0:T(8,128)(2,1)}, f32[192,2048]{1,0:T(8,128)S(1)}, f32[1,2048]{1,0:T(1,128)S(1)}) custom-call(bf16[2,2,2,192,2048]{4,3,2,1,0:T(8,128)(2,1)} %bitcast.181, f32[192,2048]{1,0:T(8,128)S(1)} %copy-done.4, f32[1,2048]{1,0:T(1,128)S(1)} %bitcast.170, bf16[192,2048]{1,0:T(8,128)(2,1)S(1)} %bitcast.162), custom_call_target="tpu_custom_call" | custom-call | tf_op jit(solution)/shard_map/middle_back/pallas_call | solution.py:626
  403.5 3.3 dynamic-slice_bitcast_fusion.1
  407.7 6.6 %convolution_convert_fusion.5 = bf16[512,2048]{1,0:T(8,128)(2,1)S(1)} fusion(bf16[1536,2048]{1,0:T(8,128)(2,1)} %bitcast.219, bf16[1536,128]{1,0:T(8,128)(2,1)S(1)} %copy-done.37, bf16[1536,384]{1,0:T(8,128)(2,1)} %copy-done.51), kind=kOutput, calls=%fused_computation.12 | convolution fusion | flops 3225419776 | bytes 9961472 | tf_op jit(solution)/shard_map/dot_general | solution.py:33
  420.5 6.7 %fusion.3.gn_ref.ga_ref = f32[1536,512]{1,0:T(8,128)S(1)} fusion(bf16[1536,2048]{1,0:T(8,128)(2,1)} %bitcast.220, bf16[128,2048]{1,0:T(8,128)(2,1)S(1)} %bitcast.197, bf16[384,2048]{1,0:T(8,128)(2,1)S(1)} %bitcast.192), kind=kOutput, calls=%fused_computation.28 | convolution fusion | flops 3225419776 | bytes 11534336 | tf_op jit(solution)/shard_map/dot_general | solution.py:37
  434.2 8.6 %total.3 = f32[12,128]{1,0:T(8,128)} custom-call(f32[12,128]{1,0:T(8,128)} %bitcast.204), custom_call_target="tpu_custom_call" | custom-call | tf_op jit(solution)/shard_map/total/pallas_call | solution.py:651
  453.9 34.2 %mixer_back.1 = (bf16[1536,1792]{1,0:T(8,128)(2,1)}, f32[4,384]{1,0:T(4,128)S(1)}, f32[1,384]{1,0:T(1,128)S(1)}, f32[4,512]{1,0:T(4,128)S(1)}, f32[1,512]{1,0:T(1,128)S(1)}, /*index=5*/f32[8,128]{1,0:T(8,128)S(1)}) custom-call(f32[1536,1792]{1,0:T(8,128)} %fusion.28.x_ref.m0_ref.m1_ref.m2_ref.m3_ref.s_ref.z_ref.q_ref.k_ref.v_ref, ...), custom_call_target="tpu_custom_call" | custom-call | tf_op jit(solution)/shard_map/mixer_back/pallas_call | solution.py:310
  493.5 2.6 fusion.8
  500.2 10.4 %convolution_convert_fusion.4 = bf16[2048,896]{1,0:T(8,128)(2,1)} fusion(bf16[1536,2048]{1,0:T(8,128)(2,1)} %bitcast.184, bf16[1536,1792]{1,0:T(8,128)(2,1)S(1)} %copy-done.44), kind=kOutput, calls=%fused_computation.4 | convolution fusion | flops 5638979584 | bytes 12713984 | tf_op jit(solution)/shard_map/dot_general | solution.py:33
  510.6 118.0 %last.1 = (f32[192,2048]{1,0:T(8,128)}, f32[16,128]{1,0:T(8,128)}, bf16[2,2,2,128,896]{4,3,2,1,0:T(8,128)(2,1)}, bf16[2,2,2,128,256]{4,3,2,1,0:T(8,128)(2,1)}, bf16[256,1024]{1,0:T(8,128)(2,1)}) custom-call(bf16[192,2048]{1,0:T(8,128)(2,1)} %bitcast.156, f32[1,2048]{1,0:T(1,128)} %bitcast.206, f32[192,2048]{1,0:T(8,128)} %copy-done.11, ...), custom_call_target="tpu_custom_call" | custom-call | tf_op jit(solution)/shard_map/last/pallas_call | solution.py:994
  638.9 3.9 finish.1
  647.2 3.5 units.1
  (280 shorter events, 87.7 us)
Async XLA Ops:
  7.2 139.1 %copy-start = (bf16[256,2048]{1,0:T(8,128)(2,1)S(1)}, bf16[256,2048]{1,0:T(8,128)(2,1)}, u32[]{:S(2)}) copy-start(bf16[256,2048]{1,0:T(8,128)(2,1)} %param.41) | copy-start | bytes 3145732
  7.2 140.0 %all-gather.6.cloned.1.call-start = ((), (), s32[]{:S(2)}) async-start(), calls=%async_computation.7 | async-start | bytes 2621440 | tf_op jit(solution)/shard_map/all_gather | solution.py:1567
  9.2 271.9 %all-gather.4.cloned.1.call-start = ((), (), s32[]{:S(2)}) async-start(), calls=%async_computation.3 | async-start | bytes 5242880 | tf_op jit(solution)/shard_map/all_gather | solution.py:1569
  140.3 307.0 %reduce-scatter.4.cloned.1.call-start = ((), (), s32[]{:S(2)}) async-start(), calls=%async_computation.4 | async-start | bytes 5242880 | tf_op jit(solution)/shard_map/reduce_scatter | solution.py:1625
  150.3 50.7 %collective-permute-start.2 = (bf16[256,1024]{1,0:T(8,128)(2,1)}, bf16[256,1024]{1,0:T(8,128)(2,1)}, u32[]{:S(2)}, u32[]{:S(2)}) collective-permute-start(bf16[256,1024]{1,0:T(8,128)(2,1)} %get-tuple-element.201), channel_id=1, source_target_pairs={{0,17},{1,16},{16,1},{17,0},{2,19},{3,18},{18,3},{19,2},{4,21},{5,... | collective-permute-start | bytes 1572872 | tf_op jit(solution)/shard_map/ppermute | solution.py:1396
  152.1 48.8 %collective-permute-start.1 = (bf16[256,1024]{1,0:T(8,128)(2,1)}, bf16[256,1024]{1,0:T(8,128)(2,1)}, u32[]{:S(2)}, u32[]{:S(2)}) collective-permute-start(bf16[256,1024]{1,0:T(8,128)(2,1)} %get-tuple-element.202), channel_id=1, source_target_pairs={{0,16},{16,0},{1,17},{17,1},{2,18},{18,2},{3,19},{19,3},{4,20},{20... | collective-permute-start | bytes 1572872 | tf_op jit(solution)/shard_map/ppermute | solution.py:1396
  152.7 48.3 %collective-permute-start = (bf16[256,1024]{1,0:T(8,128)(2,1)}, bf16[256,1024]{1,0:T(8,128)(2,1)}, u32[]{:S(2)}, u32[]{:S(2)}) collective-permute-start(bf16[256,1024]{1,0:T(8,128)(2,1)} %get-tuple-element.203), channel_id=1, source_target_pairs={{0,1},{1,0},{2,3},{3,2},{4,5},{5,4},{6,7},{7,6},{8,9},{9,8},{10,11... | collective-permute-start | bytes 1572872 | tf_op jit(solution)/shard_map/ppermute | solution.py:1396
  309.7 143.8 %reduce-scatter.6.cloned.1.call-start = ((), (), s32[]{:S(2)}) async-start(), calls=%async_computation.5 | async-start | bytes 2621440 | tf_op jit(solution)/shard_map/reduce_scatter | solution.py:1627
  406.8 22.1 %collective-permute-start.3 = (bf16[2,2,192,2048]{3,2,1,0:T(8,128)(2,1)}, bf16[2,2,192,2048]{3,2,1,0:T(8,128)(2,1)}, u32[]{:S(2)}, u32[]{:S(2)}) collective-permute-start(bf16[2,2,192,2048]{3,2,1,0:T(8,128)(2,1)} %get-tuple-element.178), channel_id=1, source_target_pairs={{0,1},{1,0},{2,3},{3,2},{4,5},{5,4},{6,7},{7,6},{8,9},{9,8},{10,11... | collective-permute-start | bytes 9437192 | tf_op jit(solution)/shard_map/ppermute | solution.py:1396
  407.2 103.4 %reduce-scatter.8.cloned.1.call-start = ((), (), s32[]{:S(2)}) async-start(), calls=%async_computation.6 | async-start | bytes 2621440 | tf_op jit(solution)/shard_map/reduce_scatter | solution.py:1502
  415.4 27.4 %collective-permute-start.6 = (bf16[256,1024]{1,0:T(8,128)(2,1)}, bf16[256,1024]{1,0:T(8,128)(2,1)}, u32[]{:S(2)}, u32[]{:S(2)}) collective-permute-start(bf16[256,1024]{1,0:T(8,128)(2,1)} %pad_maximum_fusion.11), channel_id=1, source_target_pairs={{0,1},{1,0},{2,3},{3,2},{4,5},{5,4},{6,7},{7,6},{8,9},{9,8},{10,11... | collective-permute-start | bytes 1572872 | tf_op jit(solution)/shard_map/ppermute | solution.py:1396
  416.4 26.5 %collective-permute-start.7 = (bf16[256,1024]{1,0:T(8,128)(2,1)}, bf16[256,1024]{1,0:T(8,128)(2,1)}, u32[]{:S(2)}, u32[]{:S(2)}) collective-permute-start(bf16[256,1024]{1,0:T(8,128)(2,1)} %pad_maximum_fusion.12), channel_id=1, source_target_pairs={{0,16},{16,0},{1,17},{17,1},{2,18},{18,2},{3,19},{19,3},{4,20},{20... | collective-permute-start | bytes 1572872 | tf_op jit(solution)/shard_map/ppermute | solution.py:1396
  418.0 24.8 %collective-permute-start.8 = (bf16[256,1024]{1,0:T(8,128)(2,1)}, bf16[256,1024]{1,0:T(8,128)(2,1)}, u32[]{:S(2)}, u32[]{:S(2)}) collective-permute-start(bf16[256,1024]{1,0:T(8,128)(2,1)} %pad_maximum_fusion.13), channel_id=1, source_target_pairs={{0,17},{1,16},{16,1},{17,0},{2,19},{3,18},{18,3},{19,2},{4,21},{5,... | collective-permute-start | bytes 1572872 | tf_op jit(solution)/shard_map/ppermute | solution.py:1396
  449.3 40.5 %collective-permute-start.13 = (bf16[128,1024]{1,0:T(8,128)(2,1)S(1)}, bf16[128,1024]{1,0:T(8,128)(2,1)}, u32[]{:S(2)}, u32[]{:S(2)}) collective-permute-start(bf16[128,1024]{1,0:T(8,128)(2,1)S(1)} %get-tuple-element.208), channel_id=1, source_target_pairs={{0,3},{1,2},{2,1},{3,0},{4,7},{5,6},{6,5},{7,4},{8,11},{9,10},{10,... | collective-permute-start | bytes 786440 | tf_op jit(solution)/shard_map/ppermute | solution.py:1396
  449.4 41.4 %collective-permute-start.12 = (bf16[128,1024]{1,0:T(8,128)(2,1)}, bf16[128,1024]{1,0:T(8,128)(2,1)}, u32[]{:S(2)}, u32[]{:S(2)}) collective-permute-start(bf16[128,1024]{1,0:T(8,128)(2,1)} %get-tuple-element.209), channel_id=1, source_target_pairs={{0,1},{1,0},{2,3},{3,2},{4,5},{5,4},{6,7},{7,6},{8,9},{9,8},{10,11... | collective-permute-start | bytes 786440 | tf_op jit(solution)/shard_map/ppermute | solution.py:1396
  450.3 40.5 %collective-permute-start.11 = (bf16[128,1024]{1,0:T(8,128)(2,1)}, bf16[128,1024]{1,0:T(8,128)(2,1)}, u32[]{:S(2)}, u32[]{:S(2)}) collective-permute-start(bf16[128,1024]{1,0:T(8,128)(2,1)} %get-tuple-element.210), channel_id=1, source_target_pairs={{0,2},{2,0},{1,3},{3,1},{4,6},{6,4},{5,7},{7,5},{8,10},{10,8},{9,1... | collective-permute-start | bytes 786440 | tf_op jit(solution)/shard_map/ppermute | solution.py:1396
  451.5 42.0 %collective-permute-start.4 = (bf16[2,192,1024]{2,1,0:T(8,128)(2,1)}, bf16[2,192,1024]{2,1,0:T(8,128)(2,1)}, u32[]{:S(2)}, u32[]{:S(2)}) collective-permute-start(bf16[2,192,1024]{2,1,0:T(8,128)(2,1)} %fusion.4), channel_id=1, source_target_pairs={{0,2},{2,0},{1,3},{3,1},{4,6},{6,4},{5,7},{7,5},{8,10},{10,8},{9,1... | collective-permute-start | bytes 2359304 | tf_op jit(solution)/shard_map/ppermute | solution.py:1396
  452.4 41.1 %collective-permute-start.5 = (bf16[2,192,1024]{2,1,0:T(8,128)(2,1)}, bf16[2,192,1024]{2,1,0:T(8,128)(2,1)}, u32[]{:S(2)}, u32[]{:S(2)}) collective-permute-start(bf16[2,192,1024]{2,1,0:T(8,128)(2,1)} %fusion.5), channel_id=1, source_target_pairs={{0,16},{16,0},{1,17},{17,1},{2,18},{18,2},{3,19},{19,3},{4,20},{20... | collective-permute-start | bytes 2359304 | tf_op jit(solution)/shard_map/ppermute | solution.py:1396
  489.8 145.5 %collective-permute-start.14 = (bf16[128,2048]{1,0:T(8,128)(2,1)}, bf16[128,2048]{1,0:T(8,128)(2,1)S(1)}, u32[]{:S(2)}, u32[]{:S(2)}) collective-permute-start(bf16[128,2048]{1,0:T(8,128)(2,1)} %bitcast.166), channel_id=1, source_target_pairs={{0,16},{16,0},{1,17},{17,1},{2,18},{18,2},{3,19},{19,3},{4,20},{20... | collective-permute-start | bytes 1572872 | tf_op jit(solution)/shard_map/ppermute | solution.py:1396
  492.4 154.8 %collective-permute-start.15 = (bf16[2,2,128,1024]{3,2,1,0:T(8,128)(2,1)S(1)}, bf16[2,2,128,1024]{3,2,1,0:T(8,128)(2,1)}, u32[]{:S(2)}, u32[]{:S(2)}) collective-permute-start(bf16[2,2,128,1024]{3,2,1,0:T(8,128)(2,1)S(1)} %pad_maximum_fusion.6.own_ref), channel_id=1, source_target_pairs={{0,16},{16,0},{1,17},{17,1},{2,18},{18,2},{3,19},{19,3},{4,20},{20... | collective-permute-start | bytes 3145736 | tf_op jit(solution)/shard_map/ppermute | solution.py:1396
  496.0 146.8 %collective-permute-start.10 = (bf16[192,1024]{1,0:T(8,128)(2,1)}, bf16[192,1024]{1,0:T(8,128)(2,1)S(1)}, u32[]{:S(2)}, u32[]{:S(2)}) collective-permute-start(bf16[192,1024]{1,0:T(8,128)(2,1)} %fusion.8), channel_id=1, source_target_pairs={{0,2},{2,0},{1,3},{3,1},{4,6},{6,4},{5,7},{7,5},{8,10},{10,8},{9,1... | collective-permute-start | bytes 1179656 | tf_op jit(solution)/shard_map/ppermute | solution.py:1396
  499.3 143.5 %collective-permute-start.9 = (bf16[192,1024]{1,0:T(8,128)(2,1)}, bf16[192,1024]{1,0:T(8,128)(2,1)}, u32[]{:S(2)}, u32[]{:S(2)}) collective-permute-start(bf16[192,1024]{1,0:T(8,128)(2,1)} %fusion.9), channel_id=1, source_target_pairs={{0,16},{16,0},{1,17},{17,1},{2,18},{18,2},{3,19},{19,3},{4,20},{20... | collective-permute-start | bytes 1179656 | tf_op jit(solution)/shard_map/ppermute | solution.py:1396
  510.6 124.7 %copy-start.8 = (bf16[1,256,1024]{2,1,0:T(8,128)(2,1)S(1)}, bf16[1,256,1024]{2,1,0:T(8,128)(2,1)}, u32[]{:S(2)}) copy-start(bf16[1,256,1024]{2,1,0:T(8,128)(2,1)} %reduce-scatter.8.cloned.1.call-done) | copy-start | bytes 1572868
  510.6 124.7 %copy-start.18 = (bf16[1,128,2048]{2,1,0:T(8,128)(2,1)S(1)}, bf16[1,128,2048]{2,1,0:T(8,128)(2,1)}, u32[]{:S(2)}) copy-start(bf16[1,128,2048]{2,1,0:T(8,128)(2,1)} %reduce-scatter.6.cloned.1.call-done) | copy-start | bytes 1572868
  (64 other events, 713.4 us)
Sparse Core Ops, SparseCore 0:
  10.2 63.3 all-gather.5
  140.4 83.0 all-gather.3
  309.9 75.8 reduce-scatter.3
  407.3 42.7 reduce-scatter.5
  452.9 43.2 reduce-scatter.7

commit v5 on v4

--- a/solution.py
+++ b/solution.py
@@ -591,13 +591,38 @@
 
 
 def middle_back_kernel(
-    part_ref, rows_ref, gain_ref, cot_ref, out_ref, grad_ref, gain_grad_ref,
-    block, sems, local, *scratch,
+    part_ref, rows_ref, gain_ref, cot_ref, active_ref, down_ref, incoming_ref,
+    out_ref, grad_ref, gain_grad_ref, down_grad_ref, kept_ref, got_ref,
+    block, sems, local, incoming, down_grad, result, more_sems, *scratch,
 ):
     greet(("x", "y", "c"))
     begin, wide, thin, end = reduce_plane(part_ref, scratch)
     begin()
+    load = pltpu.make_async_copy(incoming_ref, incoming, more_sems.at[0])
+    load.start()
     wide()
+    copies, c = [], lax.axis_index("c")
+    count = active_ref.shape[0] // 4
+    for side in (1, 0):
+        for yy in (0, 1):
+            rows = pl.multiple_of((2 * yy + ((1 - c) if side else c)) * count, 16)
+            into = result.at[side, yy]
+            into[...] = dot(active_ref[pl.ds(rows, count), :], down_ref[...]).astype(BF)
+            if side:
+                copy = remote(into, got_ref.at[yy], more_sems.at[1 + yy], more_sems.at[9 + yy], "c")
+            else:
+                copy = pltpu.make_async_copy(into, kept_ref.at[yy], more_sems.at[3 + yy])
+            copy.start()
+            copies.append(copy)
+    load.wait()
+    units = active_ref.shape[1] // 4
+    for i in range(4):
+        rows = pl.ds(i * units, units)
+        down_grad[rows, :] = dot(active_ref[:, rows], incoming[...], ROWS).astype(BF)
+        copies.append(
+            pltpu.make_async_copy(down_grad.at[rows], down_grad_ref.at[rows], more_sems.at[5 + i])
+        )
+        copies[4 + i].start()
     thin()
     grad, gain_grad_ref[...] = norm_back_parts(rows_ref[...], gain_ref[...], end())
     grad = grad + cot_ref[...].astype(F32)
@@ -605,9 +630,11 @@
     block[...] = grad.astype(BF)
     for step in gathered(block, out_ref, sems, local.at[0]):
         step()
-
-
-def middle_calls(part, rows, gain, down=None, cot=None):
+    for copy in copies:
+        copy.wait()
+
+
+def middle_calls(part, rows, gain, down, cot=None, active=None, incoming=None):
     n = lax.axis_size("z")
     count, width = rows.shape
     vmem, hbm = pl.BlockSpec(memory_space=pltpu.VMEM), pl.BlockSpec(memory_space=pl.ANY)
@@ -620,9 +647,14 @@
         out_specs = [hbm, vmem, hbm]
         scratch += [dma((2, 2, n))]
     else:
-        inputs, specs = [part, rows, gain, cot], [vmem] * 4
-        out += [jax.ShapeDtypeStruct((1, width), F32)]
-        out_specs = [hbm, vmem, vmem]
+        inputs = [part, rows, gain, cot, active, down, incoming]
+        specs = [vmem] * 6 + [hbm]
+        half = (2, incoming.shape[0] // 4, width)
+        out += [jax.ShapeDtypeStruct((1, width), F32), jax.ShapeDtypeStruct(down.shape, BF)]
+        out += [jax.ShapeDtypeStruct(half, BF)] * 2
+        out_specs = [hbm, vmem, vmem, hbm, hbm, hbm]
+        scratch += [pltpu.VMEM(v, BF) for v in (incoming.shape, down.shape, (2,) + half)]
+        scratch += [dma((11,))]
     return pl.pallas_call(
         middle_kernel if cot is None else middle_back_kernel,
         in_specs=specs,
@@ -1121,7 +1153,8 @@
         copy.start()
 
     def half_rows(ref, i):
-        return ref.at[pl.ds(i * (count // 2), count // 2)]
+        first = count // 4 // 16 * 16
+        return ref.at[pl.ds(i * first, count - first if i else first)]
 
     cot_steps = gather_regions(
         lambda x, y, c: incoming_ref.at[y, c, x], half_rows, cot_sems, own_cot.wait, cot_ref
@@ -1623,30 +1656,26 @@
     grad_gateup = jnp.concatenate([grad_gate.astype(BF), grad_up.astype(BF)], axis=1)
     grad_wgateup = outer_product(second, grad_gateup)
     sum_gateup = lax.psum_scatter(grad_wgateup.astype(BF).reshape(-1, 4 * count, 2 * ff), "z")
-    grad_down = outer_product(active, incoming).astype(BF)
+    grad_second = across(grad_gateup, w_gateup).astype(BF).reshape(block)
+    grad_mixer, grad_middle, grad_gain_ffn, grad_down, *results = middle_calls(
+        grad_second, middle, gain_ffn[None], w_down, grad_rows, active, incoming
+    )
     sum_down = lax.psum_scatter(
         grad_down.reshape(-1, ff // lax.axis_size("z"), model_dim), "z"
     )
-    result = mm(active, w_down).astype(BF).reshape(block)
-    grad_gateup = after(grad_gateup, (grad_down, result))
-    grad_second = across(grad_gateup, w_gateup).astype(BF).reshape(block)
-    grad_mixer, grad_middle, grad_gain_ffn = middle_calls(
-        grad_second, middle, gain_ffn[None], cot=grad_rows
-    )
+    results = [v.reshape(2, 2, token_count, model_dim) for v in results]
     grad_mixer = grad_mixer.reshape(rows, model_dim)
-    result_kept, result_away = halves_of(after(result, grad_mixer), "c", 1)
-    result_got = flip(result_away, "c")
-    grad_out = outer_product(mixed, after(grad_mixer, result_away))
+    grad_out = outer_product(mixed, grad_mixer)
     row_blocks = rows_blocks(grad_out, [wide, HD])
     grad_mixed = across(after(grad_mixer, row_blocks), w_out)
     grad_normed = grad_mixed[:, :wide]
     grad_gain_mamba = jnp.sum(grad_normed * normal, axis=0)
     scaled = grad_normed * gain_mamba
     dots = jnp.sum(scaled * normal, axis=-1).reshape(-1, 128)
-    result_got = after(result_got, dots)
+    results = after(results, dots)
     half = model_dim // 2
-    lefts = [halves_of(v[..., :half], "y", 0) for v in (result_kept, result_got)]
-    rights = [halves_of(v[..., half:], "x", 1) for v in (result_kept, result_got)]
+    lefts = [halves_of(v[..., :half], "y", 0) for v in results]
+    rights = [halves_of(v[..., half:], "x", 1) for v in results]
     left, right = ((a[1].astype(F32) + b[1].astype(F32)).astype(BF) for a, b in (lefts, rights))
     dots = plane_total(after(dots, (left, right)), 5)
     left, right, sum_gateup = after((left, right, sum_gateup), dots)

time: 662 us -> 646 us (0.976)
  matrix products: 96.6 us -> 82.7 us
    dot_general x4 -> x3, matrix products: 39.1 us -> 32.9 us  [mm(): return jnp.dot(left, right, preferred_element_type=F32)]
    dot_general x4 -> x3, matrix products: 31 us -> 26 us  [outer_product(): lax.dot_general(left, right, (((0,), (0,)), ((), ())), preferred_element_...]
    unnamed x142 -> x146, local copies, waits for them, and re-layouts: 20.4 us -> 24.3 us
  transfers between devices with their start and end apart: 21 -> 20, of which waited for: 0 -> 0; matrix products, arithmetic and copies ran while one was open for 19% -> 17% of each run, Pallas kernels for 68% -> 70%
where the time goes in v5:
time: 646 us; the launch traced here: 642 us
  Pallas kernels  453 us (70%)
  matrix products  82.7 us (13%)
  local copies, waits for them, and re-layouts  46.9 us (7%)
  other arithmetic  30.9 us (5%)
  between operations  15.1 us (2%)
  starting transfers between devices  13.5 us (2%)
    pallas_call x2, Pallas kernels, middle_calls(): pl.pallas_call(middle_kernel if cot is None else middle_back_kernel, in_s...  140 us
    pallas_call x1, Pallas kernels, last_call(): pl.pallas_call(last_kernel, in_specs=[vmem] * 4 + [hbm] * 5, out_specs=[v...  117 us
    pallas_call x1, Pallas kernels, start_call(): pl.pallas_call(start_kernel, in_specs=[vmem, vmem, hbm, hbm, hbm, hbm], o...  117 us
    pallas_call x1, Pallas kernels, mixer_backward(): pl.pallas_call(mixer_back_kernel, grid=(seqs,), in_specs=mixer_specs(leng...  34 us
    dot_general x3, matrix products, mm(): return jnp.dot(left, right, preferred_element_type=F32)  32.9 us
    dot_general x3, matrix products, outer_product(): lax.dot_general(left, right, (((0,), (0,)), ((), ())), preferred_element_...  26 us
    unnamed x146, local copies, waits for them, and re-layouts  24.3 us
    dot_general x3, matrix products, across(): lax.dot_general(left, right, (((1,), (1,)), ((), ())), preferred_element_...  23.8 us
  transfers between devices with their start and end apart: 20, of which 0 were waited for; matrix products, arithmetic and copies ran while one was open for 17% of the time, Pallas kernels for 70%

profile of v5, /device:TPU:0, one launch (start us, length us, event | category | flops | bytes accessed | tf_op | source)
XLA Modules:
  0.0 642.1 jit_solution(17854818302765870206)
XLA Ops:
  17.3 2.1 prepare.1
  19.5 117.1 %start.1 = (bf16[2,2,2,192,2048]{4,3,2,1,0:T(8,128)(2,1)}, f32[4,2,2,16,128]{4,3,2,1,0:T(8,128)S(1)}, bf16[4,2,2,128,1792]{4,3,2,1,0:T(8,128)(2,1)}, bf16[2,2,12...) custom-call(bf16[192,2048]{1,0:T(8,128)(2,1)S(1)} %bitcast.149, f32[16,128]{1,0:T(8,128)S(1)} %bitcast.165, ...), custom_call_target="tpu_custom_call" | custom-call | tf_op jit(solution)/shard_map/start/pallas_call | solution.py:1247
  144.5 3.1 dynamic-slice_bitcast_fusion.4
  149.6 17.4 %fusion.30.x_ref.m0_ref.m1_ref.m2_ref.m3_ref.s_ref.z_ref.q_ref.k_ref.v_ref = f32[1536,1792]{1,0:T(8,128)} fusion(bf16[1536,2048]{1,0:T(8,128)(2,1)} %bitcast.173, bf16[2048,1792]{1,0:T(8,128)(2,1)} %bitcast.170), kind=kOutput, calls=%fused_computation.125 | convolution fusion | flops 11274289152 | bytes 24641536 | tf_op jit(solution)/shard_map/dot_general | solution.py:29
  167.1 14.6 %mixer.1 = (bf16[1536,384]{1,0:T(8,128)(2,1)S(1)}, f32[1536,384]{1,0:T(8,128)S(1)}, f32[1536,1]{1,0:T(8,128)S(1)}, bf16[1536,128]{1,0:T(8,128)(2,1)S(1)}) custom-call(f32[1536,1792]{1,0:T(8,128)} %fusion.30.x_ref.m0_ref.m1_ref.m2_ref.m3_ref.s_ref.z_ref.q_ref.k_ref.v_ref, f32[1536,1792]{1,0:T(8,128)} %fusion.30.x_ref.m0_ref.m1_ref.m2_ref.m3_ref.s_ref.z_ref.q_ref.k_ref.v_ref, ...), custom_call_target="tpu_custom_call" | custom-call | tf_op jit(solution)/shard_map/mixer/pallas_call | solution.py:293
  186.5 9.0 %total.2 = f32[12,128]{1,0:T(8,128)} custom-call(f32[12,128]{1,0:T(8,128)} %bitcast.200), custom_call_target="tpu_custom_call" | custom-call | tf_op jit(solution)/shard_map/total/pallas_call | solution.py:683
  201.3 5.4 convolution_convert_fusion.1
  206.7 68.9 %middle.1 = (bf16[2,2,2,192,2048]{4,3,2,1,0:T(8,128)(2,1)}, f32[192,2048]{1,0:T(8,128)S(1)}, bf16[4,128,2048]{2,1,0:T(8,128)(2,1)S(1)}) custom-call(bf16[2,2,2,192,2048]{4,3,2,1,0:T(8,128)(2,1)} %bitcast.172, bf16[192,2048]{1,0:T(8,128)(2,1)S(1)} %bitcast.150, f32[1,2048]{1,0:T(1,128)S(1)} %bitcast.163, bf16[128,2048]{1,0:T(8,128)(2,1)S(1)} %copy-done.9), custom_call_target="tpu_custom_call" | custom-call | tf_op jit(solution)/shard_map/middle/pallas_call | solution.py:658
  278.1 10.1 %fusion.31 = f32[1536,1024]{1,0:T(8,128)S(1)} fusion(bf16[1536,2048]{1,0:T(8,128)(2,1)} %bitcast.212, bf16[2048,1024]{1,0:T(8,128)(2,1)} %all-gather.4.cloned.1.call-done), kind=kOutput, calls=%fused_computation.126 | convolution fusion | flops 6442450944 | bytes 16777216 | tf_op jit(solution)/shard_map/dot_general | solution.py:29
  288.2 9.0 %multiply_convert_fusion.2 = (bf16[1536,512]{1,0:T(8,128)(2,1)S(1)}, bf16[1536,512]{1,0:T(8,128)(2,1)S(1)}, bf16[1536,512]{1,0:T(8,128)(2,1)}) fusion(f32[1536,1024]{1,0:T(8,128)S(1)} %fusion.31, bf16[1536,2048]{1,0:T(8,128)(2,1)} %bitcast.176, bf16[512,2048]{1,0:T(8,128)(2,1)S(1)} %bitcast.158), kind=kOutput, calls=%fused_computation.7 | convolution fusion | flops 3233808384 | bytes 19398656 | tf_op jit(solution)/shard_map/dot_general | solution.py:37
  297.3 8.8 %convolution_convert_fusion.2 = bf16[2048,1024]{1,0:T(8,128)(2,1)} fusion(bf16[1536,2048]{1,0:T(8,128)(2,1)S(1)} %bitcast.215, bf16[1536,512]{1,0:T(8,128)(2,1)S(1)} %get-tuple-element.178, bf16[1536,512]{1,0:T(8,128)(2,1)S(1)} %get-tuple-element.177), kind=kOutput, calls=%fused_computation.2 | convolution fusion | flops 6450839552 | bytes 13631488 | tf_op jit(solution)/shard_map/dot_general | solution.py:33
  306.4 11.3 %convolution_convert_fusion = bf16[1536,2048]{1,0:T(8,128)(2,1)} fusion(bf16[2048,1024]{1,0:T(8,128)(2,1)} %all-gather.4.cloned.1.call-done, bf16[1536,512]{1,0:T(8,128)(2,1)} %copy-done.66, bf16[1536,512]{1,0:T(8,128)(2,1)} %copy-done.65), kind=kOutput, calls=%fused_computation | convolution fusion | flops 6451888128 | bytes 13631488 | tf_op jit(solution)/shard_map/dot_general | solution.py:37
  317.7 71.1 %middle_back.1 = (bf16[2,2,2,192,2048]{4,3,2,1,0:T(8,128)(2,1)}, f32[192,2048]{1,0:T(8,128)S(1)}, f32[1,2048]{1,0:T(1,128)S(1)}, bf16[512,2048]{1,0:T(8,128)(2,1...) custom-call(bf16[2,2,2,192,2048]{4,3,2,1,0:T(8,128)(2,1)} %bitcast.178, f32[192,2048]{1,0:T(8,128)S(1)} %copy-done.4, ...), custom_call_target="tpu_custom_call" | custom-call | tf_op jit(solution)/shard_map/middle_back/pallas_call | solution.py:658
  391.1 6.9 %convolution_convert_fusion.4 = bf16[512,2048]{1,0:T(8,128)(2,1)S(1)} fusion(bf16[1536,2048]{1,0:T(8,128)(2,1)} %bitcast.210, bf16[1536,128]{1,0:T(8,128)(2,1)} %copy-done.37, bf16[1536,384]{1,0:T(8,128)(2,1)} %copy-done.51), kind=kOutput, calls=%fused_computation.9 | convolution fusion | flops 3225419776 | bytes 9961472 | tf_op jit(solution)/shard_map/dot_general | solution.py:33
  403.2 3.5 fusion.3.gn_ref.ga_ref
  415.8 11.3 %total.3 = f32[12,128]{1,0:T(8,128)} custom-call(f32[12,128]{1,0:T(8,128)} %bitcast.199), custom_call_target="tpu_custom_call" | custom-call | tf_op jit(solution)/shard_map/total/pallas_call | solution.py:683
  431.7 2.1 constant_dynamic-slice_fusion
  438.3 34.0 %mixer_back.1 = (bf16[1536,1792]{1,0:T(8,128)(2,1)}, f32[4,384]{1,0:T(4,128)S(1)}, f32[1,384]{1,0:T(1,128)S(1)}, f32[4,512]{1,0:T(4,128)S(1)}, f32[1,512]{1,0:T(1,128)S(1)}, /*index=5*/f32[8,128]{1,0:T(8,128)S(1)}) custom-call(f32[1536,1792]{1,0:T(8,128)} %fusion.30.x_ref.m0_ref.m1_ref.m2_ref.m3_ref.s_ref.z_ref.q_ref.k_ref.v_ref, ...), custom_call_target="tpu_custom_call" | custom-call | tf_op jit(solution)/shard_map/mixer_back/pallas_call | solution.py:310
  477.7 2.6 fusion.8
  481.4 2.2 fusion.9
  484.5 10.4 %convolution_convert_fusion.3 = bf16[2048,896]{1,0:T(8,128)(2,1)} fusion(bf16[1536,2048]{1,0:T(8,128)(2,1)} %bitcast.174, bf16[1536,1792]{1,0:T(8,128)(2,1)S(1)} %copy-done.44), kind=kOutput, calls=%fused_computation.3 | convolution fusion | flops 5638979584 | bytes 12713984 | tf_op jit(solution)/shard_map/dot_general | solution.py:33
  494.9 117.4 %last.1 = (f32[192,2048]{1,0:T(8,128)}, f32[16,128]{1,0:T(8,128)}, bf16[2,2,2,128,896]{4,3,2,1,0:T(8,128)(2,1)}, bf16[2,2,2,128,256]{4,3,2,1,0:T(8,128)(2,1)}, bf16[256,1024]{1,0:T(8,128)(2,1)}) custom-call(bf16[192,2048]{1,0:T(8,128)(2,1)} %bitcast.148, f32[1,2048]{1,0:T(1,128)} %bitcast.201, f32[192,2048]{1,0:T(8,128)} %copy-done.13, ...), custom_call_target="tpu_custom_call" | custom-call | tf_op jit(solution)/shard_map/last/pallas_call | solution.py:1026
  622.5 3.9 finish.1
  630.8 3.5 units.1
  (278 shorter events, 81.5 us)
Async XLA Ops:
  7.2 136.4 %copy-start = (bf16[256,2048]{1,0:T(8,128)(2,1)S(1)}, bf16[256,2048]{1,0:T(8,128)(2,1)}, u32[]{:S(2)}) copy-start(bf16[256,2048]{1,0:T(8,128)(2,1)} %param.41) | copy-start | bytes 3145732
  7.2 137.3 %all-gather.6.cloned.1.call-start = ((), (), s32[]{:S(2)}) async-start(), calls=%async_computation.7 | async-start | bytes 2621440 | tf_op jit(solution)/shard_map/all_gather | solution.py:1600
  9.2 268.9 %all-gather.4.cloned.1.call-start = ((), (), s32[]{:S(2)}) async-start(), calls=%async_computation.3 | async-start | bytes 5242880 | tf_op jit(solution)/shard_map/all_gather | solution.py:1602
  19.5 118.7 %copy-start.64 = (bf16[48]{0:T(256)(128)(2,1)S(1)}, bf16[48]{0:T(256)(128)(2,1)}, u32[]{:S(2)}) copy-start(bf16[48]{0:T(256)(128)(2,1)} %param.35) | copy-start | bytes 292
  137.5 294.2 %reduce-scatter.4.cloned.1.call-start = ((), (), s32[]{:S(2)}) async-start(), calls=%async_computation.4 | async-start | bytes 5242880 | tf_op jit(solution)/shard_map/reduce_scatter | solution.py:1658
  147.6 50.3 %collective-permute-start.2 = (bf16[256,1024]{1,0:T(8,128)(2,1)}, bf16[256,1024]{1,0:T(8,128)(2,1)}, u32[]{:S(2)}, u32[]{:S(2)}) collective-permute-start(bf16[256,1024]{1,0:T(8,128)(2,1)} %get-tuple-element.201), channel_id=1, source_target_pairs={{0,17},{1,16},{16,1},{17,0},{2,19},{3,18},{18,3},{19,2},{4,21},{5,... | collective-permute-start | bytes 1572872 | tf_op jit(solution)/shard_map/ppermute | solution.py:1429
  149.0 48.8 %collective-permute-start.1 = (bf16[256,1024]{1,0:T(8,128)(2,1)}, bf16[256,1024]{1,0:T(8,128)(2,1)}, u32[]{:S(2)}, u32[]{:S(2)}) collective-permute-start(bf16[256,1024]{1,0:T(8,128)(2,1)} %get-tuple-element.202), channel_id=1, source_target_pairs={{0,16},{16,0},{1,17},{17,1},{2,18},{18,2},{3,19},{19,3},{4,20},{20... | collective-permute-start | bytes 1572872 | tf_op jit(solution)/shard_map/ppermute | solution.py:1429
  149.6 48.3 %collective-permute-start = (bf16[256,1024]{1,0:T(8,128)(2,1)}, bf16[256,1024]{1,0:T(8,128)(2,1)}, u32[]{:S(2)}, u32[]{:S(2)}) collective-permute-start(bf16[256,1024]{1,0:T(8,128)(2,1)} %get-tuple-element.203), channel_id=1, source_target_pairs={{0,1},{1,0},{2,3},{3,2},{4,5},{5,4},{6,7},{7,6},{8,9},{9,8},{10,11... | collective-permute-start | bytes 1572872 | tf_op jit(solution)/shard_map/ppermute | solution.py:1429
  306.1 131.9 %reduce-scatter.6.cloned.1.call-start = ((), (), s32[]{:S(2)}) async-start(), calls=%async_computation.5 | async-start | bytes 2621440 | tf_op jit(solution)/shard_map/reduce_scatter | solution.py:1663
  390.6 104.3 %reduce-scatter.8.cloned.1.call-start = ((), (), s32[]{:S(2)}) async-start(), calls=%async_computation.6 | async-start | bytes 2621440 | tf_op jit(solution)/shard_map/reduce_scatter | solution.py:1535
  399.7 27.4 %collective-permute-start.5 = (bf16[256,1024]{1,0:T(8,128)(2,1)}, bf16[256,1024]{1,0:T(8,128)(2,1)}, u32[]{:S(2)}, u32[]{:S(2)}) collective-permute-start(bf16[256,1024]{1,0:T(8,128)(2,1)} %pad_maximum_fusion.13), channel_id=1, source_target_pairs={{0,1},{1,0},{2,3},{3,2},{4,5},{5,4},{6,7},{7,6},{8,9},{9,8},{10,11... | collective-permute-start | bytes 1572872 | tf_op jit(solution)/shard_map/ppermute | solution.py:1429
  400.9 26.2 %collective-permute-start.6 = (bf16[256,1024]{1,0:T(8,128)(2,1)}, bf16[256,1024]{1,0:T(8,128)(2,1)}, u32[]{:S(2)}, u32[]{:S(2)}) collective-permute-start(bf16[256,1024]{1,0:T(8,128)(2,1)} %pad_maximum_fusion.14), channel_id=1, source_target_pairs={{0,16},{16,0},{1,17},{17,1},{2,18},{18,2},{3,19},{19,3},{4,20},{20... | collective-permute-start | bytes 1572872 | tf_op jit(solution)/shard_map/ppermute | solution.py:1429
  402.7 24.4 %collective-permute-start.7 = (bf16[256,1024]{1,0:T(8,128)(2,1)}, bf16[256,1024]{1,0:T(8,128)(2,1)}, u32[]{:S(2)}, u32[]{:S(2)}) collective-permute-start(bf16[256,1024]{1,0:T(8,128)(2,1)} %pad_maximum_fusion.15), channel_id=1, source_target_pairs={{0,17},{1,16},{16,1},{17,0},{2,19},{3,18},{18,3},{19,2},{4,21},{5,... | collective-permute-start | bytes 1572872 | tf_op jit(solution)/shard_map/ppermute | solution.py:1429
  433.8 40.3 %collective-permute-start.12 = (bf16[128,1024]{1,0:T(8,128)(2,1)S(1)}, bf16[128,1024]{1,0:T(8,128)(2,1)}, u32[]{:S(2)}, u32[]{:S(2)}) collective-permute-start(bf16[128,1024]{1,0:T(8,128)(2,1)S(1)} %get-tuple-element.208), channel_id=1, source_target_pairs={{0,3},{1,2},{2,1},{3,0},{4,7},{5,6},{6,5},{7,4},{8,11},{9,10},{10,... | collective-permute-start | bytes 786440 | tf_op jit(solution)/shard_map/ppermute | solution.py:1429
  433.8 41.3 %collective-permute-start.11 = (bf16[128,1024]{1,0:T(8,128)(2,1)}, bf16[128,1024]{1,0:T(8,128)(2,1)}, u32[]{:S(2)}, u32[]{:S(2)}) collective-permute-start(bf16[128,1024]{1,0:T(8,128)(2,1)} %get-tuple-element.209), channel_id=1, source_target_pairs={{0,1},{1,0},{2,3},{3,2},{4,5},{5,4},{6,7},{7,6},{8,9},{9,8},{10,11... | collective-permute-start | bytes 786440 | tf_op jit(solution)/shard_map/ppermute | solution.py:1429
  434.8 40.3 %collective-permute-start.10 = (bf16[128,1024]{1,0:T(8,128)(2,1)}, bf16[128,1024]{1,0:T(8,128)(2,1)}, u32[]{:S(2)}, u32[]{:S(2)}) collective-permute-start(bf16[128,1024]{1,0:T(8,128)(2,1)} %get-tuple-element.210), channel_id=1, source_target_pairs={{0,2},{2,0},{1,3},{3,1},{4,6},{6,4},{5,7},{7,5},{8,10},{10,8},{9,1... | collective-permute-start | bytes 786440 | tf_op jit(solution)/shard_map/ppermute | solution.py:1429
  436.0 41.8 %collective-permute-start.3 = (bf16[2,192,1024]{2,1,0:T(8,128)(2,1)}, bf16[2,192,1024]{2,1,0:T(8,128)(2,1)}, u32[]{:S(2)}, u32[]{:S(2)}) collective-permute-start(bf16[2,192,1024]{2,1,0:T(8,128)(2,1)} %fusion.4), channel_id=1, source_target_pairs={{0,2},{2,0},{1,3},{3,1},{4,6},{6,4},{5,7},{7,5},{8,10},{10,8},{9,1... | collective-permute-start | bytes 2359304 | tf_op jit(solution)/shard_map/ppermute | solution.py:1429
  436.9 40.9 %collective-permute-start.4 = (bf16[2,192,1024]{2,1,0:T(8,128)(2,1)}, bf16[2,192,1024]{2,1,0:T(8,128)(2,1)}, u32[]{:S(2)}, u32[]{:S(2)}) collective-permute-start(bf16[2,192,1024]{2,1,0:T(8,128)(2,1)} %fusion.5), channel_id=1, source_target_pairs={{0,16},{16,0},{1,17},{17,1},{2,18},{18,2},{3,19},{19,3},{4,20},{20... | collective-permute-start | bytes 2359304 | tf_op jit(solution)/shard_map/ppermute | solution.py:1429
  474.1 144.8 %collective-permute-start.13 = (bf16[128,2048]{1,0:T(8,128)(2,1)}, bf16[128,2048]{1,0:T(8,128)(2,1)S(1)}, u32[]{:S(2)}, u32[]{:S(2)}) collective-permute-start(bf16[128,2048]{1,0:T(8,128)(2,1)} %bitcast.160), channel_id=1, source_target_pairs={{0,16},{16,0},{1,17},{17,1},{2,18},{18,2},{3,19},{19,3},{4,20},{20... | collective-permute-start | bytes 1572872 | tf_op jit(solution)/shard_map/ppermute | solution.py:1429
  476.7 154.1 %collective-permute-start.14 = (bf16[2,2,128,1024]{3,2,1,0:T(8,128)(2,1)S(1)}, bf16[2,2,128,1024]{3,2,1,0:T(8,128)(2,1)}, u32[]{:S(2)}, u32[]{:S(2)}) collective-permute-start(bf16[2,2,128,1024]{3,2,1,0:T(8,128)(2,1)S(1)} %pad_maximum_fusion.8.own_ref), channel_id=1, source_target_pairs={{0,16},{16,0},{1,17},{17,1},{2,18},{18,2},{3,19},{19,3},{4,20},{20... | collective-permute-start | bytes 3145736 | tf_op jit(solution)/shard_map/ppermute | solution.py:1429
  480.3 146.2 %collective-permute-start.9 = (bf16[192,1024]{1,0:T(8,128)(2,1)}, bf16[192,1024]{1,0:T(8,128)(2,1)S(1)}, u32[]{:S(2)}, u32[]{:S(2)}) collective-permute-start(bf16[192,1024]{1,0:T(8,128)(2,1)} %fusion.8), channel_id=1, source_target_pairs={{0,2},{2,0},{1,3},{3,1},{4,6},{6,4},{5,7},{7,5},{8,10},{10,8},{9,1... | collective-permute-start | bytes 1179656 | tf_op jit(solution)/shard_map/ppermute | solution.py:1429
  483.6 142.9 %collective-permute-start.8 = (bf16[192,1024]{1,0:T(8,128)(2,1)}, bf16[192,1024]{1,0:T(8,128)(2,1)}, u32[]{:S(2)}, u32[]{:S(2)}) collective-permute-start(bf16[192,1024]{1,0:T(8,128)(2,1)} %fusion.9), channel_id=1, source_target_pairs={{0,16},{16,0},{1,17},{17,1},{2,18},{18,2},{3,19},{19,3},{4,20},{20... | collective-permute-start | bytes 1179656 | tf_op jit(solution)/shard_map/ppermute | solution.py:1429
  494.9 124.0 %copy-start.8 = (bf16[1,256,1024]{2,1,0:T(8,128)(2,1)S(1)}, bf16[1,256,1024]{2,1,0:T(8,128)(2,1)}, u32[]{:S(2)}) copy-start(bf16[1,256,1024]{2,1,0:T(8,128)(2,1)} %reduce-scatter.8.cloned.1.call-done) | copy-start | bytes 1572868
  494.9 124.0 %copy-start.21 = (bf16[1,128,2048]{2,1,0:T(8,128)(2,1)S(1)}, bf16[1,128,2048]{2,1,0:T(8,128)(2,1)}, u32[]{:S(2)}) copy-start(bf16[1,128,2048]{2,1,0:T(8,128)(2,1)} %reduce-scatter.6.cloned.1.call-done) | copy-start | bytes 1572868
  (65 other events, 634.5 us)
Sparse Core Ops, SparseCore 0:
  10.2 63.3 all-gather.5
  137.7 83.7 all-gather.3
  306.2 75.7 reduce-scatter.3
  390.7 42.7 reduce-scatter.5
  436.2 43.1 reduce-scatter.7

commit v6 on v5

--- a/solution.py
+++ b/solution.py
@@ -554,18 +554,29 @@
     return factor * (scaled - normal * inner), jnp.sum(grad * normal, axis=0, keepdims=True)
 
 
+def fill_part(part, left_ref, right_ref, dims, cc):
+    count = part.shape[3]
+    for yy in (0, 1):
+        for xx in (0, 1):
+            first = pl.multiple_of((4 * yy + 2 * cc + xx) * count, 16)
+            product = dot(left_ref[pl.ds(first, count), :], right_ref[...], dims)
+            part[yy, cc, xx] = product.astype(BF)
+
+
 def middle_kernel(
-    part_ref, rows_ref, gain_ref, down_ref, out_ref, middle_ref, whole_ref,
-    block, sems, local, down_sems, *scratch,
+    left_ref, right_ref, rows_ref, gain_ref, down_ref, out_ref, middle_ref, whole_ref,
+    block, sems, local, down_sems, part, *scratch,
 ):
-    z, n = lax.axis_index("z"), lax.axis_size("z")
+    z, n, c = lax.axis_index("z"), lax.axis_size("z"), lax.axis_index("c")
     greet_all()
-    begin, wide, thin, end = reduce_plane(part_ref, scratch)
-    begin()
+    begin, wide, thin, end = reduce_plane(part, scratch)
     own = pltpu.make_async_copy(down_ref, whole_ref.at[z], local.at[1])
     own.start()
     send, arrive, finish = line_item(lambda at: whole_ref.at[at], down_sems, down_ref)
     send(0)
+    fill_part(part, left_ref, right_ref, ((1,), (0,)), 1 - c)
+    begin()
+    fill_part(part, left_ref, right_ref, ((1,), (0,)), c)
 
     def more(k):
         if k < n:
@@ -591,17 +602,20 @@
 
 
 def middle_back_kernel(
-    part_ref, rows_ref, gain_ref, cot_ref, active_ref, down_ref, incoming_ref,
+    left_ref, right_ref, rows_ref, gain_ref, cot_ref, active_ref, down_ref, incoming_ref,
     out_ref, grad_ref, gain_grad_ref, down_grad_ref, kept_ref, got_ref,
-    block, sems, local, incoming, down_grad, result, more_sems, *scratch,
+    block, sems, local, part, incoming, down_grad, result, more_sems, *scratch,
 ):
+    c = lax.axis_index("c")
     greet(("x", "y", "c"))
-    begin, wide, thin, end = reduce_plane(part_ref, scratch)
-    begin()
     load = pltpu.make_async_copy(incoming_ref, incoming, more_sems.at[0])
     load.start()
+    begin, wide, thin, end = reduce_plane(part, scratch)
+    fill_part(part, left_ref, right_ref, LANES, 1 - c)
+    begin()
+    fill_part(part, left_ref, right_ref, LANES, c)
     wide()
-    copies, c = [], lax.axis_index("c")
+    copies = []
     count = active_ref.shape[0] // 4
     for side in (1, 0):
         for yy in (0, 1):
@@ -634,7 +648,7 @@
         copy.wait()
 
 
-def middle_calls(part, rows, gain, down, cot=None, active=None, incoming=None):
+def middle_calls(left, right, rows, gain, down, cot=None, active=None, incoming=None):
     n = lax.axis_size("z")
     count, width = rows.shape
     vmem, hbm = pl.BlockSpec(memory_space=pltpu.VMEM), pl.BlockSpec(memory_space=pl.ANY)
@@ -642,13 +656,14 @@
     out = [jax.ShapeDtypeStruct((2, 2, 2, count, width), BF), jax.ShapeDtypeStruct((count, width), F32)]
     scratch = [pltpu.VMEM((count, width), BF), dma((2, 8)), dma((2,))]
     if cot is None:
-        inputs, specs = [part, rows, gain, down], [vmem] * 3 + [hbm]
+        inputs, specs = [left, right, rows, gain, down], [vmem] * 4 + [hbm]
         out += [jax.ShapeDtypeStruct((n,) + down.shape, BF)]
         out_specs = [hbm, vmem, hbm]
-        scratch += [dma((2, 2, n))]
+        scratch += [dma((2, 2, n)), pltpu.VMEM((2, 2, 2, count, width), BF)]
     else:
-        inputs = [part, rows, gain, cot, active, down, incoming]
-        specs = [vmem] * 6 + [hbm]
+        inputs = [left, right, rows, gain, cot, active, down, incoming]
+        specs = [vmem] * 7 + [hbm]
+        scratch += [pltpu.VMEM((2, 2, 2, count, width), BF)]
         half = (2, incoming.shape[0] // 4, width)
         out += [jax.ShapeDtypeStruct((1, width), F32), jax.ShapeDtypeStruct(down.shape, BF)]
         out += [jax.ShapeDtypeStruct(half, BF)] * 2
@@ -662,7 +677,7 @@
         out_shape=out,
         scratch_shapes=scratch + sum_scratch(count, width),
         compiler_params=pltpu.CompilerParams(
-            collective_id=1 if cot is None else 2, has_side_effects=True, vmem_limit_bytes=VMEM
+            collective_id=1 if cot is None else 2, has_side_effects=True, vmem_limit_bytes=60 * 1024 * 1024
         ),
         name="middle" if cot is None else "middle_back",
     )(*inputs)
@@ -1641,8 +1656,7 @@
     normed = (normal * gain_mamba).astype(BF)
     mixed = jnp.concatenate([normed, attended], axis=1)
     block = (2, 2, 2, token_count, model_dim)
-    mixer_sum = mm(mixed, w_out).astype(BF).reshape(block)
-    second, middle, w_down = middle_calls(mixer_sum, token_rows, gain_ffn[None], down_half)
+    second, middle, w_down = middle_calls(mixed, w_out, token_rows, gain_ffn[None], down_half)
     w_down = w_down.reshape(ff, model_dim)
     second = second.reshape(rows, model_dim)
     gate_up = mm(second, w_gateup)
@@ -1656,9 +1670,8 @@
     grad_gateup = jnp.concatenate([grad_gate.astype(BF), grad_up.astype(BF)], axis=1)
     grad_wgateup = outer_product(second, grad_gateup)
     sum_gateup = lax.psum_scatter(grad_wgateup.astype(BF).reshape(-1, 4 * count, 2 * ff), "z")
-    grad_second = across(grad_gateup, w_gateup).astype(BF).reshape(block)
     grad_mixer, grad_middle, grad_gain_ffn, grad_down, *results = middle_calls(
-        grad_second, middle, gain_ffn[None], w_down, grad_rows, active, incoming
+        grad_gateup, w_gateup, middle, gain_ffn[None], w_down, grad_rows, active, incoming
     )
     sum_down = lax.psum_scatter(
         grad_down.reshape(-1, ff // lax.axis_size("z"), model_dim), "z"

time: 646 us -> 643 us (level)
  matrix products: 82.7 us -> 66 us
  Pallas kernels: 453 us -> 466 us
    pallas_call x2, Pallas kernels: 140 us -> 152 us  [middle_calls(): pl.pallas_call(middle_kernel if cot is None else middle_back_kernel, in_s...]
    dot_general x3 -> x2, matrix products: 23.8 us -> 12.5 us  [across(): lax.dot_general(left, right, (((1,), (1,)), ((), ())), preferred_element_...]
    concatenate x0 -> x3, other arithmetic: none -> 6.83 us  [the longest x1 3.96 us: shards(): jnp.concatenate([grad_gate.astype(BF), grad_up.astype(BF)], axis=1)]
    dot_general x3 -> x2, matrix products: 32.9 us -> 27.6 us  [mm(): return jnp.dot(left, right, preferred_element_type=F32)]
    unnamed x146 -> x124, local copies, waits for them, and re-layouts: 24.3 us -> 21 us
  transfers between devices with their start and end apart: 20 -> 20, of which waited for: 0 -> 0; matrix products, arithmetic and copies ran while one was open for 17% -> 15% of each run, Pallas kernels for 70% -> 72%
where the time goes in v6:
time: 643 us; the launch traced here: 639 us
  Pallas kernels  466 us (72%)
  matrix products  66 us (10%)
  local copies, waits for them, and re-layouts  43 us (7%)
  other arithmetic  35.4 us (6%)
  between operations  15 us (2%)
  starting transfers between devices  12.9 us (2%)
    pallas_call x2, Pallas kernels, middle_calls(): pl.pallas_call(middle_kernel if cot is None else middle_back_kernel, in_s...  152 us
    pallas_call x1, Pallas kernels, last_call(): pl.pallas_call(last_kernel, in_specs=[vmem] * 4 + [hbm] * 5, out_specs=[v...  119 us
    pallas_call x1, Pallas kernels, start_call(): pl.pallas_call(start_kernel, in_specs=[vmem, vmem, hbm, hbm, hbm, hbm], o...  117 us
    pallas_call x1, Pallas kernels, mixer_backward(): pl.pallas_call(mixer_back_kernel, grid=(seqs,), in_specs=mixer_specs(leng...  34.1 us
    dot_general x2, matrix products, mm(): return jnp.dot(left, right, preferred_element_type=F32)  27.6 us
    dot_general x3, matrix products, outer_product(): lax.dot_general(left, right, (((0,), (0,)), ((), ())), preferred_element_...  25.9 us
    unnamed x124, local copies, waits for them, and re-layouts  21 us
    pallas_call x2, Pallas kernels, plane_total(): pl.pallas_call(total_kernel, in_specs=[vmem], out_specs=vmem, out_shape=j...  20.3 us
  transfers between devices with their start and end apart: 20, of which 0 were waited for; matrix products, arithmetic and copies ran while one was open for 15% of the time, Pallas kernels for 72%

profile of v6, /device:TPU:0, one launch (start us, length us, event | category | flops | bytes accessed | tf_op | source)
XLA Modules:
  0.0 638.6 jit_solution(15492110948354347430)
XLA Ops:
  7.3 1.9 fusion.10
  17.3 2.1 prepare.1
  19.5 117.1 %start.1 = (bf16[2,2,2,192,2048]{4,3,2,1,0:T(8,128)(2,1)}, f32[4,2,2,16,128]{4,3,2,1,0:T(8,128)S(1)}, bf16[4,2,2,128,1792]{4,3,2,1,0:T(8,128)(2,1)}, bf16[2,2,12...) custom-call(bf16[192,2048]{1,0:T(8,128)(2,1)S(1)} %bitcast.147, f32[16,128]{1,0:T(8,128)S(1)} %bitcast.158, ...), custom_call_target="tpu_custom_call" | custom-call | tf_op jit(solution)/shard_map/start/pallas_call | solution.py:1262
  143.6 3.1 dynamic-slice_bitcast_fusion.1
  148.7 17.4 %fusion.25.x_ref.m0_ref.m1_ref.m2_ref.m3_ref.s_ref.z_ref.q_ref.k_ref.v_ref = f32[1536,1792]{1,0:T(8,128)} fusion(bf16[1536,2048]{1,0:T(8,128)(2,1)} %bitcast.166, bf16[2048,1792]{1,0:T(8,128)(2,1)} %bitcast.162), kind=kOutput, calls=%fused_computation.118 | convolution fusion | flops 11274289152 | bytes 24641536 | tf_op jit(solution)/shard_map/dot_general | solution.py:29
  166.2 14.7 %mixer.1 = (bf16[1536,384]{1,0:T(8,128)(2,1)S(1)}, f32[1536,384]{1,0:T(8,128)S(1)}, f32[1536,1]{1,0:T(8,128)S(1)}, bf16[1536,128]{1,0:T(8,128)(2,1)S(1)}) custom-call(f32[1536,1792]{1,0:T(8,128)} %fusion.25.x_ref.m0_ref.m1_ref.m2_ref.m3_ref.s_ref.z_ref.q_ref.k_ref.v_ref, f32[1536,1792]{1,0:T(8,128)} %fusion.25.x_ref.m0_ref.m1_ref.m2_ref.m3_ref.s_ref.z_ref.q_ref.k_ref.v_ref, ...), custom_call_target="tpu_custom_call" | custom-call | tf_op jit(solution)/shard_map/mixer/pallas_call | solution.py:293
  183.5 9.0 %total.2 = f32[12,128]{1,0:T(8,128)} custom-call(f32[12,128]{1,0:T(8,128)} %bitcast.194), custom_call_target="tpu_custom_call" | custom-call | tf_op jit(solution)/shard_map/total/pallas_call | solution.py:698
  200.9 71.5 %middle.1 = (bf16[2,2,2,192,2048]{4,3,2,1,0:T(8,128)(2,1)}, f32[192,2048]{1,0:T(8,128)}, bf16[4,128,2048]{2,1,0:T(8,128)(2,1)}) custom-call(bf16[1536,512]{1,0:T(8,128)(2,1)} %pad_maximum_fusion.3.left_ref, bf16[512,2048]{1,0:T(8,128)(2,1)} %pad_maximum_fusion.1.right_ref, bf16[192,2048]{1,0:T(8,128)(2,1)} %bitcast.145, f32[1,2048]{1,0:T(1,128)} %bitcast.191, ...), custom_call_target="tpu_custom_call" | custom-call | tf_op jit(solution)/shard_map/middle/pallas_call | solution.py:673
  272.4 10.1 %fusion.26 = f32[1536,1024]{1,0:T(8,128)S(1)} fusion(bf16[1536,2048]{1,0:T(8,128)(2,1)} %bitcast.207, bf16[2048,1024]{1,0:T(8,128)(2,1)} %all-gather.4.cloned.1.call-done.right_ref), kind=kOutput, calls=%fused_computation.119 | convolution fusion | flops 6442450944 | bytes 16777216 | tf_op jit(solution)/shard_map/dot_general | solution.py:29
  282.6 9.0 %multiply_convert_fusion.2 = (bf16[1536,512]{1,0:T(8,128)(2,1)S(1)}, bf16[1536,512]{1,0:T(8,128)(2,1)S(1)}, bf16[1536,512]{1,0:T(8,128)(2,1)}) fusion(f32[1536,1024]{1,0:T(8,128)S(1)} %fusion.26, bf16[1536,2048]{1,0:T(8,128)(2,1)} %bitcast.169, bf16[512,2048]{1,0:T(8,128)(2,1)S(1)} %bitcast.176), kind=kOutput, calls=%fused_computation.5 | convolution fusion | flops 3233808384 | bytes 19398656 | tf_op jit(solution)/shard_map/dot_general | solution.py:37
  291.6 8.8 %convolution_convert_fusion = bf16[2048,1024]{1,0:T(8,128)(2,1)} fusion(bf16[1536,2048]{1,0:T(8,128)(2,1)S(1)} %bitcast.210, bf16[1536,512]{1,0:T(8,128)(2,1)S(1)} %get-tuple-element.178, bf16[1536,512]{1,0:T(8,128)(2,1)S(1)} %get-tuple-element.177), kind=kOutput, calls=%fused_computation | convolution fusion | flops 6450839552 | bytes 13631488 | tf_op jit(solution)/shard_map/dot_general | solution.py:33
  300.7 4.0 pad_maximum_fusion.left_ref
  304.6 80.0 %middle_back.1 = (bf16[2,2,2,192,2048]{4,3,2,1,0:T(8,128)(2,1)}, f32[192,2048]{1,0:T(8,128)}, f32[1,2048]{1,0:T(1,128)}, bf16[512,2048]{1,0:T(8,128)(2,1)}, bf16...) custom-call(bf16[1536,1024]{1,0:T(8,128)(2,1)} %pad_maximum_fusion.left_ref, ...), custom_call_target="tpu_custom_call" | custom-call | tf_op jit(solution)/shard_map/middle_back/pallas_call | solution.py:673
  384.8 6.8 %convolution_convert_fusion.2 = bf16[512,2048]{1,0:T(8,128)(2,1)S(1)} fusion(bf16[1536,2048]{1,0:T(8,128)(2,1)} %bitcast.205, bf16[1536,128]{1,0:T(8,128)(2,1)S(1)} %copy-done.15, bf16[1536,384]{1,0:T(8,128)(2,1)} %copy-done.34), kind=kOutput, calls=%fused_computation.7 | convolution fusion | flops 3225419776 | bytes 9961472 | tf_op jit(solution)/shard_map/dot_general | solution.py:33
  396.9 3.5 fusion.18.gn_ref.ga_ref
  409.5 11.3 %total.3 = f32[12,128]{1,0:T(8,128)} custom-call(f32[12,128]{1,0:T(8,128)} %bitcast.193), custom_call_target="tpu_custom_call" | custom-call | tf_op jit(solution)/shard_map/total/pallas_call | solution.py:698
  425.3 2.0 constant_dynamic-slice_fusion
  433.2 34.1 %mixer_back.1 = (bf16[1536,1792]{1,0:T(8,128)(2,1)}, f32[4,384]{1,0:T(4,128)S(1)}, f32[1,384]{1,0:T(1,128)S(1)}, f32[4,512]{1,0:T(4,128)S(1)}, f32[1,512]{1,0:T(1,128)S(1)}, /*index=5*/f32[8,128]{1,0:T(8,128)S(1)}) custom-call(f32[1536,1792]{1,0:T(8,128)} %fusion.25.x_ref.m0_ref.m1_ref.m2_ref.m3_ref.s_ref.z_ref.q_ref.k_ref.v_ref, ...), custom_call_target="tpu_custom_call" | custom-call | tf_op jit(solution)/shard_map/mixer_back/pallas_call | solution.py:310
  472.6 2.3 fusion.7
  476.0 2.2 fusion.8
  479.2 10.4 %convolution_convert_fusion.1 = bf16[2048,896]{1,0:T(8,128)(2,1)} fusion(bf16[1536,2048]{1,0:T(8,128)(2,1)} %bitcast.167, bf16[1536,1792]{1,0:T(8,128)(2,1)S(1)} %copy-done.33), kind=kOutput, calls=%fused_computation.1 | convolution fusion | flops 5638979584 | bytes 12713984 | tf_op jit(solution)/shard_map/dot_general | solution.py:33
  489.6 119.1 %last.1 = (f32[192,2048]{1,0:T(8,128)}, f32[16,128]{1,0:T(8,128)}, bf16[2,2,2,128,896]{4,3,2,1,0:T(8,128)(2,1)}, bf16[2,2,2,128,256]{4,3,2,1,0:T(8,128)(2,1)}, bf16[256,1024]{1,0:T(8,128)(2,1)}) custom-call(bf16[192,2048]{1,0:T(8,128)(2,1)} %bitcast.146, f32[1,2048]{1,0:T(1,128)} %bitcast.195, f32[192,2048]{1,0:T(8,128)} %get-tuple-element.152.grad_ref, ...), custom_call_target="tpu_custom_call" | custom-call | tf_op jit(solution)/shard_map/last/pallas_call | solution.py:1041
  618.9 3.9 finish.1
  627.3 3.5 units.1
  (257 shorter events, 75.9 us)
Async XLA Ops:
  7.2 135.6 %copy-start = (bf16[256,2048]{1,0:T(8,128)(2,1)S(1)}, bf16[256,2048]{1,0:T(8,128)(2,1)}, u32[]{:S(2)}) copy-start(bf16[256,2048]{1,0:T(8,128)(2,1)} %param.41) | copy-start | bytes 3145732
  7.2 136.4 %all-gather.6.cloned.1.call-start = ((), (), s32[]{:S(2)}) async-start(), calls=%async_computation.7 | async-start | bytes 2621440 | tf_op jit(solution)/shard_map/all_gather | solution.py:1615
  9.2 263.2 %all-gather.4.cloned.1.call-start = ((), (), s32[]{:S(2)}) async-start(), calls=%async_computation.3 | async-start | bytes 5242880 | tf_op jit(solution)/shard_map/all_gather | solution.py:1617
  19.4 118.5 %copy-start.54 = (bf16[48]{0:T(256)(128)(2,1)S(1)}, bf16[48]{0:T(256)(128)(2,1)}, u32[]{:S(2)}) copy-start(bf16[48]{0:T(256)(128)(2,1)} %param.34) | copy-start | bytes 292
  19.5 118.5 %copy-start.55 = (bf16[48]{0:T(256)(128)(2,1)S(1)}, bf16[48]{0:T(256)(128)(2,1)}, u32[]{:S(2)}) copy-start(bf16[48]{0:T(256)(128)(2,1)} %param.35) | copy-start | bytes 292
  137.5 287.8 %reduce-scatter.4.cloned.1.call-start = ((), (), s32[]{:S(2)}) async-start(), calls=%async_computation.4 | async-start | bytes 5242880 | tf_op jit(solution)/shard_map/reduce_scatter | solution.py:1672
  146.7 49.4 %collective-permute-start.2 = (bf16[256,1024]{1,0:T(8,128)(2,1)}, bf16[256,1024]{1,0:T(8,128)(2,1)}, u32[]{:S(2)}, u32[]{:S(2)}) collective-permute-start(bf16[256,1024]{1,0:T(8,128)(2,1)} %get-tuple-element.200), channel_id=1, source_target_pairs={{0,17},{1,16},{16,1},{17,0},{2,19},{3,18},{18,3},{19,2},{4,21},{5,... | collective-permute-start | bytes 1572872 | tf_op jit(solution)/shard_map/ppermute | solution.py:1444
  148.2 48.0 %collective-permute-start.1 = (bf16[256,1024]{1,0:T(8,128)(2,1)}, bf16[256,1024]{1,0:T(8,128)(2,1)}, u32[]{:S(2)}, u32[]{:S(2)}) collective-permute-start(bf16[256,1024]{1,0:T(8,128)(2,1)} %get-tuple-element.201), channel_id=1, source_target_pairs={{0,16},{16,0},{1,17},{17,1},{2,18},{18,2},{3,19},{19,3},{4,20},{20... | collective-permute-start | bytes 1572872 | tf_op jit(solution)/shard_map/ppermute | solution.py:1444
  148.7 47.4 %collective-permute-start = (bf16[256,1024]{1,0:T(8,128)(2,1)}, bf16[256,1024]{1,0:T(8,128)(2,1)}, u32[]{:S(2)}, u32[]{:S(2)}) collective-permute-start(bf16[256,1024]{1,0:T(8,128)(2,1)} %get-tuple-element.202), channel_id=1, source_target_pairs={{0,1},{1,0},{2,3},{3,2},{4,5},{5,4},{6,7},{7,6},{8,9},{9,8},{10,11... | collective-permute-start | bytes 1572872 | tf_op jit(solution)/shard_map/ppermute | solution.py:1444
  300.5 131.1 %reduce-scatter.6.cloned.1.call-start = ((), (), s32[]{:S(2)}) async-start(), calls=%async_computation.5 | async-start | bytes 2621440 | tf_op jit(solution)/shard_map/reduce_scatter | solution.py:1676
  384.7 104.9 %reduce-scatter.8.cloned.1.call-start = ((), (), s32[]{:S(2)}) async-start(), calls=%async_computation.6 | async-start | bytes 2621440 | tf_op jit(solution)/shard_map/reduce_scatter | solution.py:1550
  393.4 27.4 %collective-permute-start.5 = (bf16[256,1024]{1,0:T(8,128)(2,1)}, bf16[256,1024]{1,0:T(8,128)(2,1)}, u32[]{:S(2)}, u32[]{:S(2)}) collective-permute-start(bf16[256,1024]{1,0:T(8,128)(2,1)} %pad_maximum_fusion.7), channel_id=1, source_target_pairs={{0,1},{1,0},{2,3},{3,2},{4,5},{5,4},{6,7},{7,6},{8,9},{9,8},{10,11... | collective-permute-start | bytes 1572872 | tf_op jit(solution)/shard_map/ppermute | solution.py:1444
  394.6 26.2 %collective-permute-start.6 = (bf16[256,1024]{1,0:T(8,128)(2,1)}, bf16[256,1024]{1,0:T(8,128)(2,1)}, u32[]{:S(2)}, u32[]{:S(2)}) collective-permute-start(bf16[256,1024]{1,0:T(8,128)(2,1)} %pad_maximum_fusion.8), channel_id=1, source_target_pairs={{0,16},{16,0},{1,17},{17,1},{2,18},{18,2},{3,19},{19,3},{4,20},{20... | collective-permute-start | bytes 1572872 | tf_op jit(solution)/shard_map/ppermute | solution.py:1444
  396.1 24.7 %collective-permute-start.7 = (bf16[256,1024]{1,0:T(8,128)(2,1)}, bf16[256,1024]{1,0:T(8,128)(2,1)}, u32[]{:S(2)}, u32[]{:S(2)}) collective-permute-start(bf16[256,1024]{1,0:T(8,128)(2,1)} %pad_maximum_fusion.9), channel_id=1, source_target_pairs={{0,17},{1,16},{16,1},{17,0},{2,19},{3,18},{18,3},{19,2},{4,21},{5,... | collective-permute-start | bytes 1572872 | tf_op jit(solution)/shard_map/ppermute | solution.py:1444
  427.4 41.7 %collective-permute-start.12 = (bf16[128,1024]{1,0:T(8,128)(2,1)}, bf16[128,1024]{1,0:T(8,128)(2,1)}, u32[]{:S(2)}, u32[]{:S(2)}) collective-permute-start(bf16[128,1024]{1,0:T(8,128)(2,1)} %get-tuple-element.208), channel_id=1, source_target_pairs={{0,3},{1,2},{2,1},{3,0},{4,7},{5,6},{6,5},{7,4},{8,11},{9,10},{10,... | collective-permute-start | bytes 786440 | tf_op jit(solution)/shard_map/ppermute | solution.py:1444
  427.4 42.5 %collective-permute-start.11 = (bf16[128,1024]{1,0:T(8,128)(2,1)}, bf16[128,1024]{1,0:T(8,128)(2,1)}, u32[]{:S(2)}, u32[]{:S(2)}) collective-permute-start(bf16[128,1024]{1,0:T(8,128)(2,1)} %get-tuple-element.209), channel_id=1, source_target_pairs={{0,1},{1,0},{2,3},{3,2},{4,5},{5,4},{6,7},{7,6},{8,9},{9,8},{10,11... | collective-permute-start | bytes 786440 | tf_op jit(solution)/shard_map/ppermute | solution.py:1444
  428.2 41.7 %collective-permute-start.10 = (bf16[128,1024]{1,0:T(8,128)(2,1)S(1)}, bf16[128,1024]{1,0:T(8,128)(2,1)}, u32[]{:S(2)}, u32[]{:S(2)}) collective-permute-start(bf16[128,1024]{1,0:T(8,128)(2,1)S(1)} %get-tuple-element.210), channel_id=1, source_target_pairs={{0,2},{2,0},{1,3},{3,1},{4,6},{6,4},{5,7},{7,5},{8,10},{10,8},{9,1... | collective-permute-start | bytes 786440 | tf_op jit(solution)/shard_map/ppermute | solution.py:1444
  429.5 43.1 %collective-permute-start.3 = (bf16[2,192,1024]{2,1,0:T(8,128)(2,1)}, bf16[2,192,1024]{2,1,0:T(8,128)(2,1)}, u32[]{:S(2)}, u32[]{:S(2)}) collective-permute-start(bf16[2,192,1024]{2,1,0:T(8,128)(2,1)} %fusion.3), channel_id=1, source_target_pairs={{0,2},{2,0},{1,3},{3,1},{4,6},{6,4},{5,7},{7,5},{8,10},{10,8},{9,1... | collective-permute-start | bytes 2359304 | tf_op jit(solution)/shard_map/ppermute | solution.py:1444
  430.2 42.4 %collective-permute-start.4 = (bf16[2,192,1024]{2,1,0:T(8,128)(2,1)}, bf16[2,192,1024]{2,1,0:T(8,128)(2,1)}, u32[]{:S(2)}, u32[]{:S(2)}) collective-permute-start(bf16[2,192,1024]{2,1,0:T(8,128)(2,1)} %fusion.4), channel_id=1, source_target_pairs={{0,16},{16,0},{1,17},{17,1},{2,18},{18,2},{3,19},{19,3},{4,20},{20... | collective-permute-start | bytes 2359304 | tf_op jit(solution)/shard_map/ppermute | solution.py:1444
  469.1 146.3 %collective-permute-start.13 = (bf16[128,2048]{1,0:T(8,128)(2,1)S(1)}, bf16[128,2048]{1,0:T(8,128)(2,1)S(1)}, u32[]{:S(2)}, u32[]{:S(2)}) collective-permute-start(bf16[128,2048]{1,0:T(8,128)(2,1)S(1)} %bitcast.155), channel_id=1, source_target_pairs={{0,16},{16,0},{1,17},{17,1},{2,18},{18,2},{3,19},{19,3},{4,20},{20... | collective-permute-start | bytes 1572872 | tf_op jit(solution)/shard_map/ppermute | solution.py:1444
  471.3 156.0 %collective-permute-start.14 = (bf16[2,2,128,1024]{3,2,1,0:T(8,128)(2,1)S(1)}, bf16[2,2,128,1024]{3,2,1,0:T(8,128)(2,1)}, u32[]{:S(2)}, u32[]{:S(2)}) collective-permute-start(bf16[2,2,128,1024]{3,2,1,0:T(8,128)(2,1)S(1)} %pad_maximum_fusion.4.own_ref), channel_id=1, source_target_pairs={{0,16},{16,0},{1,17},{17,1},{2,18},{18,2},{3,19},{19,3},{4,20},{20... | collective-permute-start | bytes 3145736 | tf_op jit(solution)/shard_map/ppermute | solution.py:1444
  475.0 147.9 %collective-permute-start.9 = (bf16[192,1024]{1,0:T(8,128)(2,1)}, bf16[192,1024]{1,0:T(8,128)(2,1)}, u32[]{:S(2)}, u32[]{:S(2)}) collective-permute-start(bf16[192,1024]{1,0:T(8,128)(2,1)} %fusion.7), channel_id=1, source_target_pairs={{0,2},{2,0},{1,3},{3,1},{4,6},{6,4},{5,7},{7,5},{8,10},{10,8},{9,1... | collective-permute-start | bytes 1179656 | tf_op jit(solution)/shard_map/ppermute | solution.py:1444
  478.2 144.6 %collective-permute-start.8 = (bf16[192,1024]{1,0:T(8,128)(2,1)}, bf16[192,1024]{1,0:T(8,128)(2,1)}, u32[]{:S(2)}, u32[]{:S(2)}) collective-permute-start(bf16[192,1024]{1,0:T(8,128)(2,1)} %fusion.8), channel_id=1, source_target_pairs={{0,16},{16,0},{1,17},{17,1},{2,18},{18,2},{3,19},{19,3},{4,20},{20... | collective-permute-start | bytes 1179656 | tf_op jit(solution)/shard_map/ppermute | solution.py:1444
  489.6 125.7 %copy-start.4 = (bf16[1,256,1024]{2,1,0:T(8,128)(2,1)S(1)}, bf16[1,256,1024]{2,1,0:T(8,128)(2,1)}, u32[]{:S(2)}) copy-start(bf16[1,256,1024]{2,1,0:T(8,128)(2,1)} %reduce-scatter.8.cloned.1.call-done) | copy-start | bytes 1572868
  (54 other events, 475.8 us)
Sparse Core Ops, SparseCore 0:
  10.2 63.3 all-gather.5
  137.7 86.8 all-gather.3
  300.6 75.8 reduce-scatter.3
  384.8 42.9 reduce-scatter.5
  430.5 43.1 reduce-scatter.7
